TPU v7x, 512 devices: a whole 4x4x16 slice. The times are simulated.
512 devices in a mesh: gx: 8 (over z_lo), gy: 16 (over z_hi, x, core), gz: 4 (over y).
Axes of the slice: x: 4, y: 4, z: 16 (z_hi: 2, z_lo: 8; z = z_hi * 8 + z_lo), core: 2. Of those that a mesh axis runs over, the one named last changes fastest.
Arguments:
- voltage_gradient_components: float32 [3, 128, 128, 1024], P(None, 'gx', 'gy', 'gz'), may hold values from -6 to 6
- flux_curl_components: float32 [3, 128, 128, 1024], P(None, 'gx', 'gy', 'gz'), may hold values from -6 to 6
- phase_label_grid: int32 [128, 128, 1024], P('gx', 'gy', 'gz'), may hold values from 0 to 3
- feeding_spot_positions: int32 [512, 16], P(('gx', 'gy', 'gz')), may hold values from 0 to 32767
- thermal_rise_kelvin: float32 [64, 64, 512], P('gx', ('gy', 'gz')), may hold values from 0 to 1
- packing_fraction: float32 [64, 64, 512], P('gx', ('gy', 'gz')), may hold values from 0.55 to 0.95
Outputs:
- temp_out: float32 [64, 64, 512], P('gx', ('gy', 'gz'))
- density_out: float32 [64, 64, 512], P('gx', ('gy', 'gz'))
Inputs may be any that keep to these rules, and one draw needn't show every extreme that they name: `feeding_spot_positions`: each entry is a cell index inside its own brick, x-major; several may name the same cell.
All inputs are finite; a program needn't handle non-finite values.
Results may differ from a plain program's by a relative error of at most 0.0001.
Values sent between devices are 32-bit elements; how exact they have to be, the bound alone decides.
No kernel may reach another device: no remote copies, remote signals or barrier semaphores. Data moves between devices by JAX's collectives and lax.ppermute only.
A program may use at most 64 MiB of HBM per device.

v0:
```python
import math

import jax
import jax.numpy as jnp
from jax import lax
from jax.sharding import PartitionSpec as P

ITERS = 4
HEAT_STEPS = 2


eps_table = (3.0, 9.0, 12.0, 1.0)
sig_table = (0.05, 0.01, 0.4, 0.0)
courant_dt = 0.99 / math.sqrt(3.0)


def passed_along(block, axis, distance):
    devices = range(lax.axis_size(axis))
    route = [(i - distance, i) for i in devices if i - distance in devices]
    return lax.ppermute(block, axis, route)


def extended(x, sides, width):
    for axis, dim in sides:
        peers, length = (lax.axis_size(axis), x.shape[dim])
        up = [(i, (i + 1) % peers) for i in range(peers - 1)]
        down = [(j, i) for i, j in up]
        last = lax.slice_in_dim(x, length - width, length, axis=dim)
        initial = lax.slice_in_dim(x, 0, width, axis=dim)
        before = lax.ppermute(last, axis, up)
        after = lax.ppermute(initial, axis, down)
        x = jnp.concatenate([before, x, after], axis=dim)
    return x


def lookup(phase_label_grid, table):
    result = jnp.zeros(phase_label_grid.shape, jnp.float32)
    for index in range(4):
        result = result + (phase_label_grid == index).astype(jnp.float32) * table[index]
    return result


def append_after(field, plane, axis):
    size = field.shape[axis]
    return jnp.concatenate([lax.slice_in_dim(field, 1, size, axis=axis), plane], axis=axis)


def prepend_before(field, plane, axis):
    size = field.shape[axis]
    return jnp.concatenate([plane, lax.slice_in_dim(field, 0, size - 1, axis=axis)], axis=axis)


def electric_ahead(efield_first, efield_second, efield_third):
    planes_x = passed_along(jnp.stack([efield_second[:1], efield_third[:1]]), "gx", -1)
    planes_y = passed_along(jnp.stack([efield_first[:, :1], efield_third[:, :1]]), "gy", -1)
    planes_z = passed_along(jnp.stack([efield_first[:, :, :1], efield_second[:, :, :1]]), "gz", -1)
    return (
        append_after(efield_second, planes_x[0], 0),
        append_after(efield_third, planes_x[1], 0),
        append_after(efield_first, planes_y[0], 1),
        append_after(efield_third, planes_y[1], 1),
        append_after(efield_first, planes_z[0], 2),
        append_after(efield_second, planes_z[1], 2),
    )


def magnetic_behind(hfield_first, hfield_second, hfield_third):
    planes_x = passed_along(jnp.stack([hfield_second[-1:], hfield_third[-1:]]), "gx", 1)
    planes_y = passed_along(jnp.stack([hfield_first[:, -1:], hfield_third[:, -1:]]), "gy", 1)
    planes_z = passed_along(jnp.stack([hfield_first[:, :, -1:], hfield_second[:, :, -1:]]), "gz", 1)
    return (
        prepend_before(hfield_second, planes_x[0], 0),
        prepend_before(hfield_third, planes_x[1], 0),
        prepend_before(hfield_first, planes_y[0], 1),
        prepend_before(hfield_third, planes_y[1], 1),
        prepend_before(hfield_first, planes_z[0], 2),
        prepend_before(hfield_second, planes_z[1], 2),
    )


def restrict(power):
    cells_x, cells_y, cells_z = power.shape
    return power.reshape(cells_x // 2, 2, cells_y // 2, 2, cells_z // 2, 2).mean(axis=(1, 3, 5))


def local(
    voltage_gradient_components,
    flux_curl_components,
    phase_label_grid,
    feeding_spot_positions,
    thermal_rise_kelvin,
    packing_fraction,
):
    cells_x, cells_y, cells_z = phase_label_grid.shape
    eps_map = lookup(phase_label_grid, eps_table)
    sig_map = lookup(phase_label_grid, sig_table)
    loss = sig_map * courant_dt / (2.0 * eps_map)
    coef_a = (1.0 - loss) / (1.0 + loss)
    coef_b = courant_dt / (eps_map * (1.0 + loss))
    count = (
        jnp.zeros((cells_x * cells_y * cells_z,), jnp.float32)
        .at[feeding_spot_positions.reshape(-1)]
        .add(1.0)
    )
    count = count.reshape(cells_x, cells_y, cells_z)
    efield_first, efield_second, efield_third = (
        voltage_gradient_components[0],
        voltage_gradient_components[1],
        voltage_gradient_components[2],
    )
    hfield_first, hfield_second, hfield_third = (
        flux_curl_components[0],
        flux_curl_components[1],
        flux_curl_components[2],
    )
    powers = []
    for step in range(ITERS):
        ey_xp, ez_xp, ex_yp, ez_yp, ex_zp, ey_zp = electric_ahead(
            efield_first, efield_second, efield_third
        )
        hfield_first = hfield_first - courant_dt * (ez_yp - efield_third - (ey_zp - efield_second))
        hfield_second = hfield_second - courant_dt * (ex_zp - efield_first - (ez_xp - efield_third))
        hfield_third = hfield_third - courant_dt * (ey_xp - efield_second - (ex_yp - efield_first))
        hy_xm, hz_xm, hx_ym, hz_ym, hx_zm, hy_zm = magnetic_behind(
            hfield_first, hfield_second, hfield_third
        )
        wave = 60.0 * math.sin(0.6 * (step + 0.5) * courant_dt)
        efield_first = coef_a * efield_first + coef_b * (
            hfield_third - hz_ym - (hfield_second - hy_zm)
        )
        efield_second = coef_a * efield_second + coef_b * (
            hfield_first - hx_zm - (hfield_third - hz_xm)
        )
        efield_third = (
            coef_a * efield_third
            + coef_b * (hfield_second - hy_xm - (hfield_first - hx_ym))
            - coef_b * count * wave
        )
        powers.append(
            sig_map
            * (
                efield_first * efield_first
                + efield_second * efield_second
                + efield_third * efield_third
            )
        )
    deposited_microwave_joules = jnp.zeros_like(thermal_rise_kelvin)
    for power in powers:
        deposited_microwave_joules = deposited_microwave_joules + lax.all_to_all(
            restrict(power), "gz", split_axis=1, concat_axis=2, tiled=True
        )
    deposited_microwave_joules = deposited_microwave_joules / ITERS
    for step in range(HEAT_STEPS):
        bordered_warmth = extended(thermal_rise_kelvin, (("gx", 0), (("gy", "gz"), 1)), 1)
        bordered_warmth = jnp.pad(bordered_warmth, ((0, 0), (0, 0), (1, 1)))
        spreading_stencil_matrix = (
            bordered_warmth[2:, 1:-1, 1:-1]
            + bordered_warmth[:-2, 1:-1, 1:-1]
            + bordered_warmth[1:-1, 2:, 1:-1]
            + bordered_warmth[1:-1, :-2, 1:-1]
            + bordered_warmth[1:-1, 1:-1, 2:]
            + bordered_warmth[1:-1, 1:-1, :-2]
            - 6.0 * thermal_rise_kelvin
        )
        advanced_thermal_rise = thermal_rise_kelvin + 0.1 * (
            (0.2 + packing_fraction) * spreading_stencil_matrix + 10.0 * deposited_microwave_joules
        )
        packing_fraction = packing_fraction + 0.3 * (1.0 - packing_fraction) * jnp.exp(
            -3.0 / (1.0 + thermal_rise_kelvin)
        )
        thermal_rise_kelvin = advanced_thermal_rise
    return (thermal_rise_kelvin, packing_fraction)


def solution(mesh):
    return jax.shard_map(
        local,
        mesh=mesh,
        in_specs=(
            P(None, "gx", "gy", "gz"),
            P(None, "gx", "gy", "gz"),
            P("gx", "gy", "gz"),
            P(("gx", "gy", "gz"), None),
            P("gx", ("gy", "gz"), None),
            P("gx", ("gy", "gz"), None),
        ),
        out_specs=(P("gx", ("gy", "gz"), None), P("gx", ("gy", "gz"), None)),
        check_vma=False,
    )
```

profile of v0, /device:TPU:384, one launch (start us, length us, event | category | flops | bytes accessed | tf_op | source)
XLA Modules:
  0.0 271.3 jit_solution(3531748957615125223)
XLA Ops:
  1.8 5.3 %collective-permute-start.5 = (f32[2,16,1,256]{3,2,1,0:T(1,128)S(1)}, f32[2,16,1,256]{3,2,1,0:T(1,128)S(1)}, u32[]{:S(2)}, u32[]{:S(2)}) collective-permute-start(f32[2,16,1,256]{3,2,1,0:T(1,128)S(1)} %pad_maximum_fusion.1), channel_id=1, source_target_pairs={{4,0},{8,4},{12,8},{16,12},{20,16},{24,20},{28,24},{32,28},{36,32}... | collective-permute-start | bytes 98312 | tf_op jit(solution)/shard_map/ppermute | solution.py:20
  14.1 3.8 %collective-permute-start.1 = (f32[1,1,512]{2,0,1:T(1,128)S(1)}, f32[1,1,512]{2,0,1:T(1,128)S(1)}, u32[]{:S(2)}, u32[]{:S(2)}) collective-permute-start(f32[1,1,512]{2,0,1:T(1,128)S(1)} %get-tuple-element.77), channel_id=1, source_target_pairs={{0,64},{64,128},{128,192},{192,256},{256,320},{320,384},{384,448},... | collective-permute-start | bytes 6152 | tf_op jit(solution)/shard_map/ppermute | solution.py:30
  21.6 5.6 %collective-permute-start.2 = (f32[10,1,512]{2,0,1:T(8,128)S(1)}, f32[10,1,512]{2,0,1:T(8,128)S(1)}, u32[]{:S(2)}, u32[]{:S(2)}) collective-permute-start(f32[10,1,512]{2,0,1:T(8,128)S(1)} %pad_maximum_fusion), channel_id=1, source_target_pairs={{1,0},{2,1},{3,2},{4,3},{5,4},{6,5},{7,6},{8,7},{9,8},{10,9},{11,1... | collective-permute-start | bytes 61448 | tf_op jit(solution)/shard_map/ppermute | solution.py:31
  37.0 3.8 %collective-permute-start.9 = (f32[2,1,8,256]{3,2,1,0:T(8,128)S(1)}, f32[2,1,8,256]{3,2,1,0:T(8,128)S(1)}, u32[]{:S(2)}, u32[]{:S(2)}) collective-permute-start(f32[2,1,8,256]{3,2,1,0:T(8,128)S(1)} %pad_maximum_fusion.14), channel_id=1, source_target_pairs={{0,64},{64,128},{128,192},{192,256},{256,320},{320,384},{384,448},... | collective-permute-start | bytes 49160 | tf_op jit(solution)/shard_map/ppermute | solution.py:20
  43.8 4.3 %collective-permute-done.7 = f32[2,16,1,256]{3,2,1,0:T(1,128)S(1)} collective-permute-done((f32[2,16,1,256]{3,2,1,0:T(1,128)S(1)}, f32[2,16,1,256]{3,2,1,0:T(1,128)S(1)}, u32[]{:S(2)}, u32[]{:S(2)}) %collective-permute-start.7) | collective-permute-done | bytes 32800 | tf_op jit(solution)/shard_map/ppermute | solution.py:20
  54.7 7.4 %collective-permute-start.11 = (f32[2,16,1,256]{3,2,1,0:T(1,128)S(1)}, f32[2,16,1,256]{3,2,1,0:T(1,128)S(1)}, u32[]{:S(2)}, u32[]{:S(2)}) collective-permute-start(f32[2,16,1,256]{3,2,1,0:T(1,128)S(1)} %pad_maximum_fusion.3), channel_id=1, source_target_pairs={{4,0},{8,4},{12,8},{16,12},{20,16},{24,20},{28,24},{32,28},{36,32}... | collective-permute-start | bytes 98312 | tf_op jit(solution)/shard_map/ppermute | solution.py:20
  62.2 9.8 %reshape.123 = f32[8,2,4,2,128,2]{5,4,3,2,1,0:T(8,128)} reshape(f32[16,8,256]{2,1,0:T(8,128)S(1)} %get-tuple-element.19) | data formatting | bytes 262144 | tf_op jit(solution)/shard_map/reshape | solution.py:83
  72.0 4.0 %reduce_sum.36 = f32[8,4,128]{2,1,0:T(4,128)S(1)} reduce(f32[8,2,4,2,128,2]{5,4,3,2,1,0:T(8,128)} %reshape.123, f32[]{:T(128)} %constant.27.clone.1), dimensions={1,3,5}, to_apply=%region_1.0 | reduce | flops 28672 | bytes 147460 | tf_op jit(solution)/shard_map/reduce_sum | solution.py:83
  76.6 6.3 %all-to-all-start = ((f32[8,4,128]{2,0,1:T(8,128)}), f32[8,4,128]{2,0,1:T(8,128)S(1)}, u32[]{:S(2)}, u32[]{:S(2)}) async-start(f32[8,4,128]{2,0,1:T(8,128)} %copy_multiply_fusion.3), calls=%async_computation | async-start | bytes 32768 | tf_op jit(solution)/shard_map/all_to_all | solution.py:149
  83.6 3.6 %collective-permute-start.15 = (f32[2,1,8,256]{3,2,1,0:T(8,128)S(1)}, f32[2,1,8,256]{3,2,1,0:T(8,128)S(1)}, u32[]{:S(2)}, u32[]{:S(2)}) collective-permute-start(f32[2,1,8,256]{3,2,1,0:T(8,128)S(1)} %pad_maximum_fusion.16), channel_id=1, source_target_pairs={{0,64},{64,128},{128,192},{192,256},{256,320},{320,384},{384,448},... | collective-permute-start | bytes 49160 | tf_op jit(solution)/shard_map/ppermute | solution.py:20
  87.6 3.9 %collective-permute-start.14 = (f32[2,16,8,1]{1,2,3,0:T(8,128)S(1)}, f32[2,16,8,1]{1,2,3,0:T(8,128)S(1)}, u32[]{:S(2)}, u32[]{:S(2)}) collective-permute-start(f32[2,16,8,1]{1,2,3,0:T(8,128)S(1)} %pad_maximum_fusion.24), channel_id=1, source_target_pairs={{0,1},{1,2},{2,3},{4,5},{5,6},{6,7},{8,9},{9,10},{10,11},{12,13},{... | collective-permute-start | bytes 3080 | tf_op jit(solution)/shard_map/ppermute | solution.py:20
  93.8 13.9 %collective-permute-done.13 = f32[2,16,1,256]{3,2,1,0:T(1,128)S(1)} collective-permute-done((f32[2,16,1,256]{3,2,1,0:T(1,128)S(1)}, f32[2,16,1,256]{3,2,1,0:T(1,128)S(1)}, u32[]{:S(2)}, u32[]{:S(2)}) %collective-permute-start.13) | collective-permute-done | bytes 32800 | tf_op jit(solution)/shard_map/ppermute | solution.py:20
  108.1 3.4 %collective-permute-start.16 = (f32[2,1,8,256]{3,2,1,0:T(8,128)S(1)}, f32[2,1,8,256]{3,2,1,0:T(8,128)S(1)}, u32[]{:S(2)}, u32[]{:S(2)}) collective-permute-start(f32[2,1,8,256]{3,2,1,0:T(8,128)S(1)} %pad_maximum_fusion.17), channel_id=1, source_target_pairs={{64,0},{128,64},{192,128},{256,192},{320,256},{384,320},{448,384},... | collective-permute-start | bytes 49160 | tf_op jit(solution)/shard_map/ppermute | solution.py:20
  115.0 9.8 %reshape.124 = f32[8,2,4,2,128,2]{5,4,3,2,1,0:T(8,128)} reshape(f32[16,8,256]{2,1,0:T(8,128)S(1)} %get-tuple-element.15) | data formatting | bytes 262144 | tf_op jit(solution)/shard_map/reshape | solution.py:83
  124.7 4.0 %reduce_sum.37 = f32[8,4,128]{2,1,0:T(4,128)S(1)} reduce(f32[8,2,4,2,128,2]{5,4,3,2,1,0:T(8,128)} %reshape.124, f32[]{:T(128)} %constant.27.clone.1), dimensions={1,3,5}, to_apply=%region_2.0 | reduce | flops 28672 | bytes 147460 | tf_op jit(solution)/shard_map/reduce_sum | solution.py:83
  133.1 4.5 %collective-permute-start.20 = (f32[2,16,8,1]{1,2,3,0:T(8,128)S(1)}, f32[2,16,8,1]{1,2,3,0:T(8,128)S(1)}, u32[]{:S(2)}, u32[]{:S(2)}) collective-permute-start(f32[2,16,8,1]{1,2,3,0:T(8,128)S(1)} %pad_maximum_fusion.26), channel_id=1, source_target_pairs={{0,1},{1,2},{2,3},{4,5},{5,6},{6,7},{8,9},{9,10},{10,11},{12,13},{... | collective-permute-start | bytes 3080 | tf_op jit(solution)/shard_map/ppermute | solution.py:20
  140.0 13.8 %collective-permute-done.19 = f32[2,16,1,256]{3,2,1,0:T(1,128)S(1)} collective-permute-done((f32[2,16,1,256]{3,2,1,0:T(1,128)S(1)}, f32[2,16,1,256]{3,2,1,0:T(1,128)S(1)}, u32[]{:S(2)}, u32[]{:S(2)}) %collective-permute-start.19) | collective-permute-done | bytes 32800 | tf_op jit(solution)/shard_map/ppermute | solution.py:20
  156.2 4.6 %collective-permute-start.22 = (f32[2,1,8,256]{3,2,1,0:T(8,128)S(1)}, f32[2,1,8,256]{3,2,1,0:T(8,128)S(1)}, u32[]{:S(2)}, u32[]{:S(2)}) collective-permute-start(f32[2,1,8,256]{3,2,1,0:T(8,128)S(1)} %pad_maximum_fusion.19), channel_id=1, source_target_pairs={{64,0},{128,64},{192,128},{256,192},{320,256},{384,320},{448,384},... | collective-permute-start | bytes 49160 | tf_op jit(solution)/shard_map/ppermute | solution.py:20
  162.5 9.8 %reshape.125 = f32[8,2,4,2,128,2]{5,4,3,2,1,0:T(8,128)} reshape(f32[16,8,256]{2,1,0:T(8,128)S(1)} %get-tuple-element.23) | data formatting | bytes 262144 | tf_op jit(solution)/shard_map/reshape | solution.py:83
  172.3 4.0 %reduce_sum.38 = f32[8,4,128]{2,1,0:T(4,128)S(1)} reduce(f32[8,2,4,2,128,2]{5,4,3,2,1,0:T(8,128)} %reshape.125, f32[]{:T(128)} %constant.27.clone.1), dimensions={1,3,5}, to_apply=%region_3.0 | reduce | flops 28672 | bytes 147460 | tf_op jit(solution)/shard_map/reduce_sum | solution.py:83
  180.2 4.5 %collective-permute-start.26 = (f32[2,16,8,1]{1,2,3,0:T(8,128)S(1)}, f32[2,16,8,1]{1,2,3,0:T(8,128)S(1)}, u32[]{:S(2)}, u32[]{:S(2)}) collective-permute-start(f32[2,16,8,1]{1,2,3,0:T(8,128)S(1)} %pad_maximum_fusion.28), channel_id=1, source_target_pairs={{0,1},{1,2},{2,3},{4,5},{5,6},{6,7},{8,9},{9,10},{10,11},{12,13},{... | collective-permute-start | bytes 3080 | tf_op jit(solution)/shard_map/ppermute | solution.py:20
  187.0 13.9 %collective-permute-done.25 = f32[2,16,1,256]{3,2,1,0:T(1,128)S(1)} collective-permute-done((f32[2,16,1,256]{3,2,1,0:T(1,128)S(1)}, f32[2,16,1,256]{3,2,1,0:T(1,128)S(1)}, u32[]{:S(2)}, u32[]{:S(2)}) %collective-permute-start.25) | collective-permute-done | bytes 32800 | tf_op jit(solution)/shard_map/ppermute | solution.py:20
  200.9 3.9 %all-to-all-start.1 = ((f32[8,4,128]{2,0,1:T(8,128)}), f32[8,4,128]{2,0,1:T(8,128)S(1)}, u32[]{:S(2)}, u32[]{:S(2)}) async-start(f32[8,4,128]{2,0,1:T(8,128)} %copy_multiply_fusion.2), calls=%async_computation.1 | async-start | bytes 32768 | tf_op jit(solution)/shard_map/all_to_all | solution.py:149
  205.2 9.8 %reshape.126 = f32[8,2,4,2,128,2]{5,4,3,2,1,0:T(8,128)} reshape(f32[16,8,256]{2,1,0:T(8,128)S(1)} %fusion.69) | data formatting | bytes 262144 | tf_op jit(solution)/shard_map/reshape | solution.py:83
  215.0 4.0 %reduce_sum.39 = f32[8,4,128]{2,1,0:T(4,128)S(1)} reduce(f32[8,2,4,2,128,2]{5,4,3,2,1,0:T(8,128)} %reshape.126, f32[]{:T(128)} %constant.27.clone.1), dimensions={1,3,5}, to_apply=%region_4.0 | reduce | flops 28672 | bytes 147460 | tf_op jit(solution)/shard_map/reduce_sum | solution.py:83
  219.0 4.8 %all-to-all-start.2 = ((f32[8,4,128]{2,0,1:T(8,128)}), f32[8,4,128]{2,0,1:T(8,128)S(1)}, u32[]{:S(2)}, u32[]{:S(2)}) async-start(f32[8,4,128]{2,0,1:T(8,128)} %copy_multiply_fusion.1), calls=%async_computation.2 | async-start | bytes 32768 | tf_op jit(solution)/shard_map/all_to_all | solution.py:149
  224.4 4.8 %all-to-all-done.2 = f32[8,4,128]{2,0,1:T(8,128)S(1)} async-done(((f32[8,4,128]{2,0,1:T(8,128)}), f32[8,4,128]{2,0,1:T(8,128)S(1)}, u32[]{:S(2)}, u32[]{:S(2)}) %all-to-all-start.2) | async-done | bytes 16416 | tf_op jit(solution)/shard_map/all_to_all | solution.py:149
  232.6 5.2 %all-to-all-done.3 = f32[8,4,128]{2,0,1:T(8,128)S(1)} async-done(((f32[8,4,128]{2,0,1:T(8,128)}), f32[8,4,128]{2,0,1:T(8,128)S(1)}, u32[]{:S(2)}, u32[]{:S(2)}) %all-to-all-start.3) | async-done | bytes 16416 | tf_op jit(solution)/shard_map/all_to_all | solution.py:149
  237.9 5.8 %collective-permute-start.28 = (f32[1,1,512]{2,0,1:T(1,128)S(1)}, f32[1,1,512]{2,0,1:T(1,128)S(1)}, u32[]{:S(2)}, u32[]{:S(2)}) collective-permute-start(f32[1,1,512]{2,0,1:T(1,128)S(1)} %get-tuple-element.60), channel_id=1, source_target_pairs={{64,0},{128,64},{192,128},{256,192},{320,256},{384,320},{448,384},... | collective-permute-start | bytes 6152 | tf_op jit(solution)/shard_map/ppermute | solution.py:31
  245.6 4.8 %collective-permute-done.29 = f32[1,1,512]{2,0,1:T(1,128)S(1)} collective-permute-done((f32[1,1,512]{2,0,1:T(1,128)S(1)}, f32[1,1,512]{2,0,1:T(1,128)S(1)}, u32[]{:S(2)}, u32[]{:S(2)}) %collective-permute-start.29) | collective-permute-done | bytes 2080 | tf_op jit(solution)/shard_map/ppermute | solution.py:30
  252.3 3.9 %collective-permute-start.31 = (f32[10,1,512]{2,0,1:T(8,128)S(1)}, f32[10,1,512]{2,0,1:T(8,128)S(1)}, u32[]{:S(2)}, u32[]{:S(2)}) collective-permute-start(f32[10,1,512]{2,0,1:T(8,128)S(1)} %pad_maximum_fusion.9), channel_id=1, source_target_pairs={{0,1},{1,2},{2,3},{3,4},{4,5},{5,6},{6,7},{7,8},{8,9},{9,10},{10,1... | collective-permute-start | bytes 61448 | tf_op jit(solution)/shard_map/ppermute | solution.py:30
  256.9 13.6 %collective-permute-done.31 = f32[10,1,512]{2,0,1:T(8,128)S(1)} collective-permute-done((f32[10,1,512]{2,0,1:T(8,128)S(1)}, f32[10,1,512]{2,0,1:T(8,128)S(1)}, u32[]{:S(2)}, u32[]{:S(2)}) %collective-permute-start.31) | collective-permute-done | bytes 20512 | tf_op jit(solution)/shard_map/ppermute | solution.py:30
  (239 shorter events, 64.6 us)
Async XLA Ops:
  1.8 28.8 %collective-permute-start.5 = (f32[2,16,1,256]{3,2,1,0:T(1,128)S(1)}, f32[2,16,1,256]{3,2,1,0:T(1,128)S(1)}, u32[]{:S(2)}, u32[]{:S(2)}) collective-permute-start(f32[2,16,1,256]{3,2,1,0:T(1,128)S(1)} %pad_maximum_fusion.1), channel_id=1, source_target_pairs={{4,0},{8,4},{12,8},{16,12},{20,16},{24,20},{28,24},{32,28},{36,32}... | collective-permute-start | bytes 98312 | tf_op jit(solution)/shard_map/ppermute | solution.py:20
  7.3 14.0 %collective-permute-start.6 = (f32[2,16,8,1]{1,2,3,0:T(8,128)S(1)}, f32[2,16,8,1]{1,2,3,0:T(8,128)S(1)}, u32[]{:S(2)}, u32[]{:S(2)}) collective-permute-start(f32[2,16,8,1]{1,2,3,0:T(8,128)S(1)} %pad_maximum_fusion.21), channel_id=1, source_target_pairs={{1,0},{2,1},{3,2},{5,4},{6,5},{7,6},{9,8},{10,9},{11,10},{13,12},{... | collective-permute-start | bytes 3080 | tf_op jit(solution)/shard_map/ppermute | solution.py:20
  9.3 19.8 %collective-permute-start.4 = (f32[2,1,8,256]{3,2,1,0:T(8,128)S(1)}, f32[2,1,8,256]{3,2,1,0:T(8,128)S(1)}, u32[]{:S(2)}, u32[]{:S(2)}) collective-permute-start(f32[2,1,8,256]{3,2,1,0:T(8,128)S(1)} %stack.212), channel_id=1, source_target_pairs={{64,0},{128,64},{192,128},{256,192},{320,256},{384,320},{448,384},... | collective-permute-start | bytes 49160 | tf_op jit(solution)/shard_map/ppermute | solution.py:20
  12.1 9.5 %collective-permute-start = (f32[1,1,512]{2,0,1:T(1,128)S(1)}, f32[1,1,512]{2,0,1:T(1,128)S(1)}, u32[]{:S(2)}, u32[]{:S(2)}) collective-permute-start(f32[1,1,512]{2,0,1:T(1,128)S(1)} %get-tuple-element.78), channel_id=1, source_target_pairs={{64,0},{128,64},{192,128},{256,192},{320,256},{384,320},{448,384},... | collective-permute-start | bytes 6152 | tf_op jit(solution)/shard_map/ppermute | solution.py:31
  14.1 7.5 %collective-permute-start.1 = (f32[1,1,512]{2,0,1:T(1,128)S(1)}, f32[1,1,512]{2,0,1:T(1,128)S(1)}, u32[]{:S(2)}, u32[]{:S(2)}) collective-permute-start(f32[1,1,512]{2,0,1:T(1,128)S(1)} %get-tuple-element.77), channel_id=1, source_target_pairs={{0,64},{64,128},{128,192},{192,256},{256,320},{320,384},{384,448},... | collective-permute-start | bytes 6152 | tf_op jit(solution)/shard_map/ppermute | solution.py:30
  21.6 210.8 %collective-permute-start.2 = (f32[10,1,512]{2,0,1:T(8,128)S(1)}, f32[10,1,512]{2,0,1:T(8,128)S(1)}, u32[]{:S(2)}, u32[]{:S(2)}) collective-permute-start(f32[10,1,512]{2,0,1:T(8,128)S(1)} %pad_maximum_fusion), channel_id=1, source_target_pairs={{1,0},{2,1},{3,2},{4,3},{5,4},{6,5},{7,6},{8,7},{9,8},{10,9},{11,1... | collective-permute-start | bytes 61448 | tf_op jit(solution)/shard_map/ppermute | solution.py:31
  27.2 205.2 %collective-permute-start.3 = (f32[10,1,512]{2,0,1:T(8,128)S(1)}, f32[10,1,512]{2,0,1:T(8,128)S(1)}, u32[]{:S(2)}, u32[]{:S(2)}) collective-permute-start(f32[10,1,512]{2,0,1:T(8,128)S(1)} %pad_maximum_fusion), channel_id=1, source_target_pairs={{0,1},{1,2},{2,3},{3,4},{4,5},{5,6},{6,7},{7,8},{8,9},{9,10},{10,1... | collective-permute-start | bytes 61448 | tf_op jit(solution)/shard_map/ppermute | solution.py:30
  32.0 16.1 %collective-permute-start.7 = (f32[2,16,1,256]{3,2,1,0:T(1,128)S(1)}, f32[2,16,1,256]{3,2,1,0:T(1,128)S(1)}, u32[]{:S(2)}, u32[]{:S(2)}) collective-permute-start(f32[2,16,1,256]{3,2,1,0:T(1,128)S(1)} %pad_maximum_fusion.2), channel_id=1, source_target_pairs={{0,4},{4,8},{8,12},{12,16},{16,20},{20,24},{24,28},{28,32},{32,36}... | collective-permute-start | bytes 98312 | tf_op jit(solution)/shard_map/ppermute | solution.py:20
  37.0 6.8 %collective-permute-start.9 = (f32[2,1,8,256]{3,2,1,0:T(8,128)S(1)}, f32[2,1,8,256]{3,2,1,0:T(8,128)S(1)}, u32[]{:S(2)}, u32[]{:S(2)}) collective-permute-start(f32[2,1,8,256]{3,2,1,0:T(8,128)S(1)} %pad_maximum_fusion.14), channel_id=1, source_target_pairs={{0,64},{64,128},{128,192},{192,256},{256,320},{320,384},{384,448},... | collective-permute-start | bytes 49160 | tf_op jit(solution)/shard_map/ppermute | solution.py:20
  49.9 33.3 %collective-permute-start.10 = (f32[2,1,8,256]{3,2,1,0:T(8,128)S(1)}, f32[2,1,8,256]{3,2,1,0:T(8,128)S(1)}, u32[]{:S(2)}, u32[]{:S(2)}) collective-permute-start(f32[2,1,8,256]{3,2,1,0:T(8,128)S(1)} %pad_maximum_fusion.15), channel_id=1, source_target_pairs={{64,0},{128,64},{192,128},{256,192},{320,256},{384,320},{448,384},... | collective-permute-start | bytes 49160 | tf_op jit(solution)/shard_map/ppermute | solution.py:20
  53.4 29.5 %collective-permute-start.12 = (f32[2,16,8,1]{1,2,3,0:T(8,128)S(1)}, f32[2,16,8,1]{1,2,3,0:T(8,128)S(1)}, u32[]{:S(2)}, u32[]{:S(2)}) collective-permute-start(f32[2,16,8,1]{1,2,3,0:T(8,128)S(1)} %pad_maximum_fusion.23), channel_id=1, source_target_pairs={{1,0},{2,1},{3,2},{5,4},{6,5},{7,6},{9,8},{10,9},{11,10},{13,12},{... | collective-permute-start | bytes 3080 | tf_op jit(solution)/shard_map/ppermute | solution.py:20
  54.7 28.5 %collective-permute-start.11 = (f32[2,16,1,256]{3,2,1,0:T(1,128)S(1)}, f32[2,16,1,256]{3,2,1,0:T(1,128)S(1)}, u32[]{:S(2)}, u32[]{:S(2)}) collective-permute-start(f32[2,16,1,256]{3,2,1,0:T(1,128)S(1)} %pad_maximum_fusion.3), channel_id=1, source_target_pairs={{4,0},{8,4},{12,8},{16,12},{20,16},{24,20},{28,24},{32,28},{36,32}... | collective-permute-start | bytes 98312 | tf_op jit(solution)/shard_map/ppermute | solution.py:20
  76.6 124.3 %all-to-all-start = ((f32[8,4,128]{2,0,1:T(8,128)}), f32[8,4,128]{2,0,1:T(8,128)S(1)}, u32[]{:S(2)}, u32[]{:S(2)}) async-start(f32[8,4,128]{2,0,1:T(8,128)} %copy_multiply_fusion.3), calls=%async_computation | async-start | bytes 32768 | tf_op jit(solution)/shard_map/all_to_all | solution.py:149
  83.6 10.1 %collective-permute-start.15 = (f32[2,1,8,256]{3,2,1,0:T(8,128)S(1)}, f32[2,1,8,256]{3,2,1,0:T(8,128)S(1)}, u32[]{:S(2)}, u32[]{:S(2)}) collective-permute-start(f32[2,1,8,256]{3,2,1,0:T(8,128)S(1)} %pad_maximum_fusion.16), channel_id=1, source_target_pairs={{0,64},{64,128},{128,192},{192,256},{256,320},{320,384},{384,448},... | collective-permute-start | bytes 49160 | tf_op jit(solution)/shard_map/ppermute | solution.py:20
  91.5 16.1 %collective-permute-start.13 = (f32[2,16,1,256]{3,2,1,0:T(1,128)S(1)}, f32[2,16,1,256]{3,2,1,0:T(1,128)S(1)}, u32[]{:S(2)}, u32[]{:S(2)}) collective-permute-start(f32[2,16,1,256]{3,2,1,0:T(1,128)S(1)} %pad_maximum_fusion.4), channel_id=1, source_target_pairs={{0,4},{4,8},{8,12},{12,16},{16,20},{20,24},{24,28},{28,32},{32,36}... | collective-permute-start | bytes 98312 | tf_op jit(solution)/shard_map/ppermute | solution.py:20
  108.1 21.9 %collective-permute-start.16 = (f32[2,1,8,256]{3,2,1,0:T(8,128)S(1)}, f32[2,1,8,256]{3,2,1,0:T(8,128)S(1)}, u32[]{:S(2)}, u32[]{:S(2)}) collective-permute-start(f32[2,1,8,256]{3,2,1,0:T(8,128)S(1)} %pad_maximum_fusion.17), channel_id=1, source_target_pairs={{64,0},{128,64},{192,128},{256,192},{320,256},{384,320},{448,384},... | collective-permute-start | bytes 49160 | tf_op jit(solution)/shard_map/ppermute | solution.py:20
  111.7 18.0 %collective-permute-start.18 = (f32[2,16,8,1]{1,2,3,0:T(8,128)S(1)}, f32[2,16,8,1]{1,2,3,0:T(8,128)S(1)}, u32[]{:S(2)}, u32[]{:S(2)}) collective-permute-start(f32[2,16,8,1]{1,2,3,0:T(8,128)S(1)} %pad_maximum_fusion.25), channel_id=1, source_target_pairs={{1,0},{2,1},{3,2},{5,4},{6,5},{7,6},{9,8},{10,9},{11,10},{13,12},{... | collective-permute-start | bytes 3080 | tf_op jit(solution)/shard_map/ppermute | solution.py:20
  113.0 16.9 %collective-permute-start.17 = (f32[2,16,1,256]{3,2,1,0:T(1,128)S(1)}, f32[2,16,1,256]{3,2,1,0:T(1,128)S(1)}, u32[]{:S(2)}, u32[]{:S(2)}) collective-permute-start(f32[2,16,1,256]{3,2,1,0:T(1,128)S(1)} %pad_maximum_fusion.5), channel_id=1, source_target_pairs={{4,0},{8,4},{12,8},{16,12},{20,16},{24,20},{28,24},{32,28},{36,32}... | collective-permute-start | bytes 98312 | tf_op jit(solution)/shard_map/ppermute | solution.py:20
  130.4 9.5 %collective-permute-start.21 = (f32[2,1,8,256]{3,2,1,0:T(8,128)S(1)}, f32[2,1,8,256]{3,2,1,0:T(8,128)S(1)}, u32[]{:S(2)}, u32[]{:S(2)}) collective-permute-start(f32[2,1,8,256]{3,2,1,0:T(8,128)S(1)} %pad_maximum_fusion.18), channel_id=1, source_target_pairs={{0,64},{64,128},{128,192},{192,256},{256,320},{320,384},{384,448},... | collective-permute-start | bytes 49160 | tf_op jit(solution)/shard_map/ppermute | solution.py:20
  133.1 6.5 %collective-permute-start.20 = (f32[2,16,8,1]{1,2,3,0:T(8,128)S(1)}, f32[2,16,8,1]{1,2,3,0:T(8,128)S(1)}, u32[]{:S(2)}, u32[]{:S(2)}) collective-permute-start(f32[2,16,8,1]{1,2,3,0:T(8,128)S(1)} %pad_maximum_fusion.26), channel_id=1, source_target_pairs={{0,1},{1,2},{2,3},{4,5},{5,6},{6,7},{8,9},{9,10},{10,11},{12,13},{... | collective-permute-start | bytes 3080 | tf_op jit(solution)/shard_map/ppermute | solution.py:20
  137.7 16.1 %collective-permute-start.19 = (f32[2,16,1,256]{3,2,1,0:T(1,128)S(1)}, f32[2,16,1,256]{3,2,1,0:T(1,128)S(1)}, u32[]{:S(2)}, u32[]{:S(2)}) collective-permute-start(f32[2,16,1,256]{3,2,1,0:T(1,128)S(1)} %pad_maximum_fusion.6), channel_id=1, source_target_pairs={{0,4},{4,8},{8,12},{12,16},{16,20},{20,24},{24,28},{28,32},{32,36}... | collective-permute-start | bytes 98312 | tf_op jit(solution)/shard_map/ppermute | solution.py:20
  154.3 23.3 %collective-permute-start.23 = (f32[2,16,1,256]{3,2,1,0:T(1,128)S(1)}, f32[2,16,1,256]{3,2,1,0:T(1,128)S(1)}, u32[]{:S(2)}, u32[]{:S(2)}) collective-permute-start(f32[2,16,1,256]{3,2,1,0:T(1,128)S(1)} %pad_maximum_fusion.7), channel_id=1, source_target_pairs={{4,0},{8,4},{12,8},{16,12},{20,16},{24,20},{28,24},{32,28},{36,32}... | collective-permute-start | bytes 98312 | tf_op jit(solution)/shard_map/ppermute | solution.py:20
  156.2 21.3 %collective-permute-start.22 = (f32[2,1,8,256]{3,2,1,0:T(8,128)S(1)}, f32[2,1,8,256]{3,2,1,0:T(8,128)S(1)}, u32[]{:S(2)}, u32[]{:S(2)}) collective-permute-start(f32[2,1,8,256]{3,2,1,0:T(8,128)S(1)} %pad_maximum_fusion.19), channel_id=1, source_target_pairs={{64,0},{128,64},{192,128},{256,192},{320,256},{384,320},{448,384},... | collective-permute-start | bytes 49160 | tf_op jit(solution)/shard_map/ppermute | solution.py:20
  161.1 16.2 %collective-permute-start.24 = (f32[2,16,8,1]{1,2,3,0:T(8,128)S(1)}, f32[2,16,8,1]{1,2,3,0:T(8,128)S(1)}, u32[]{:S(2)}, u32[]{:S(2)}) collective-permute-start(f32[2,16,8,1]{1,2,3,0:T(8,128)S(1)} %pad_maximum_fusion.27), channel_id=1, source_target_pairs={{1,0},{2,1},{3,2},{5,4},{6,5},{7,6},{9,8},{10,9},{11,10},{13,12},{... | collective-permute-start | bytes 3080 | tf_op jit(solution)/shard_map/ppermute | solution.py:20
  178.0 9.0 %collective-permute-start.27 = (f32[2,1,8,256]{3,2,1,0:T(8,128)S(1)}, f32[2,1,8,256]{3,2,1,0:T(8,128)S(1)}, u32[]{:S(2)}, u32[]{:S(2)}) collective-permute-start(f32[2,1,8,256]{3,2,1,0:T(8,128)S(1)} %pad_maximum_fusion.20), channel_id=1, source_target_pairs={{0,64},{64,128},{128,192},{192,256},{256,320},{320,384},{384,448},... | collective-permute-start | bytes 49160 | tf_op jit(solution)/shard_map/ppermute | solution.py:20
  184.8 16.1 %collective-permute-start.25 = (f32[2,16,1,256]{3,2,1,0:T(1,128)S(1)}, f32[2,16,1,256]{3,2,1,0:T(1,128)S(1)}, u32[]{:S(2)}, u32[]{:S(2)}) collective-permute-start(f32[2,16,1,256]{3,2,1,0:T(1,128)S(1)} %pad_maximum_fusion.8), channel_id=1, source_target_pairs={{0,4},{4,8},{8,12},{12,16},{16,20},{20,24},{24,28},{28,32},{32,36}... | collective-permute-start | bytes 98312 | tf_op jit(solution)/shard_map/ppermute | solution.py:20
  200.9 18.1 %all-to-all-start.1 = ((f32[8,4,128]{2,0,1:T(8,128)}), f32[8,4,128]{2,0,1:T(8,128)S(1)}, u32[]{:S(2)}, u32[]{:S(2)}) async-start(f32[8,4,128]{2,0,1:T(8,128)} %copy_multiply_fusion.2), calls=%async_computation.1 | async-start | bytes 32768 | tf_op jit(solution)/shard_map/all_to_all | solution.py:149
  219.0 10.2 %all-to-all-start.2 = ((f32[8,4,128]{2,0,1:T(8,128)}), f32[8,4,128]{2,0,1:T(8,128)S(1)}, u32[]{:S(2)}, u32[]{:S(2)}) async-start(f32[8,4,128]{2,0,1:T(8,128)} %copy_multiply_fusion.1), calls=%async_computation.2 | async-start | bytes 32768 | tf_op jit(solution)/shard_map/all_to_all | solution.py:149
  229.2 8.6 %all-to-all-start.3 = ((f32[8,4,128]{2,0,1:T(8,128)}), f32[8,4,128]{2,0,1:T(8,128)S(1)}, u32[]{:S(2)}, u32[]{:S(2)}) async-start(f32[8,4,128]{2,0,1:T(8,128)} %copy_multiply_fusion), calls=%async_computation.3 | async-start | bytes 32768 | tf_op jit(solution)/shard_map/all_to_all | solution.py:149
  237.9 7.7 %collective-permute-start.28 = (f32[1,1,512]{2,0,1:T(1,128)S(1)}, f32[1,1,512]{2,0,1:T(1,128)S(1)}, u32[]{:S(2)}, u32[]{:S(2)}) collective-permute-start(f32[1,1,512]{2,0,1:T(1,128)S(1)} %get-tuple-element.60), channel_id=1, source_target_pairs={{64,0},{128,64},{192,128},{256,192},{320,256},{384,320},{448,384},... | collective-permute-start | bytes 6152 | tf_op jit(solution)/shard_map/ppermute | solution.py:31
  243.7 6.7 %collective-permute-start.29 = (f32[1,1,512]{2,0,1:T(1,128)S(1)}, f32[1,1,512]{2,0,1:T(1,128)S(1)}, u32[]{:S(2)}, u32[]{:S(2)}) collective-permute-start(f32[1,1,512]{2,0,1:T(1,128)S(1)} %get-tuple-element.59), channel_id=1, source_target_pairs={{0,64},{64,128},{128,192},{192,256},{256,320},{320,384},{384,448},... | collective-permute-start | bytes 6152 | tf_op jit(solution)/shard_map/ppermute | solution.py:30
  252.3 18.2 %collective-permute-start.31 = (f32[10,1,512]{2,0,1:T(8,128)S(1)}, f32[10,1,512]{2,0,1:T(8,128)S(1)}, u32[]{:S(2)}, u32[]{:S(2)}) collective-permute-start(f32[10,1,512]{2,0,1:T(8,128)S(1)} %pad_maximum_fusion.9), channel_id=1, source_target_pairs={{0,1},{1,2},{2,3},{3,4},{4,5},{5,6},{6,7},{7,8},{8,9},{9,10},{10,1... | collective-permute-start | bytes 61448 | tf_op jit(solution)/shard_map/ppermute | solution.py:30
  (7 other events, 135.5 us)
where the time goes:
time: 273 us; the launch traced here: 271 us
  starting transfers between devices  116 us (42%)
  waiting for transfers between devices  77 us (28%)
  local copies, waits for them, and re-layouts  50.7 us (19%)
  other arithmetic  26 us (10%)
    ppermute x24, starting transfers between devices, passed_along(): return lax.ppermute(block, axis, route)  70.5 us
    ppermute x24, waiting for transfers between devices, passed_along(): return lax.ppermute(block, axis, route)  48.6 us
    reshape x4, local copies, waits for them, and re-layouts, restrict(): power.reshape(cells_x // 2, 2, cells_y // 2, 2, cells_z // 2, 2)  39.1 us
    ppermute x4, waiting for transfers between devices, extended(): before = lax.ppermute(last, axis, up)  18.4 us
    all_to_all x4, starting transfers between devices, local(): lax.all_to_all(restrict(power), 'gz', split_axis=1, concat_axis=2, tiled=...  18.3 us
    reduce_sum x4, other arithmetic, restrict(): power.reshape(cells_x // 2, 2, cells_y // 2, 2, cells_z // 2, 2)  16.1 us
    ppermute x4, starting transfers between devices, extended(): after = lax.ppermute(initial, axis, down)  15.3 us
    ppermute x4, starting transfers between devices, extended(): before = lax.ppermute(last, axis, up)  11.6 us
  transfers between devices with their start and end apart: 36, of which 9 were waited for; matrix products, arithmetic and copies ran while one was open for 28% of the time, Pallas kernels for 0%

commit v1 on v0

v1 whole, which is shorter than its diff:
```python
import functools
import math

import jax
import jax.numpy as jnp
from jax import lax
from jax.experimental import pallas as pl
from jax.experimental.pallas import tpu as pltpu
from jax.sharding import PartitionSpec as P

ITERS = 4
W = 4
CX, CY, CZ = 16, 8, 256
NX, NY = CX + 2 * W, CY + 2 * W
LANES = 128
FIELDS = 8
TILES = 2 * FIELDS

eps_table = (3.0, 9.0, 12.0, 1.0)
sig_table = (0.05, 0.01, 0.4, 0.0)
courant_dt = 0.99 / math.sqrt(3.0)
loss_table = tuple(s * courant_dt / (2.0 * e) for s, e in zip(sig_table, eps_table))
ca_table = tuple((1.0 - l) / (1.0 + l) for l in loss_table)
cb_table = tuple(courant_dt / (e * (1.0 + l)) for l, e in zip(loss_table, eps_table))

F32 = jnp.float32
VMEM = pl.BlockSpec(memory_space=pltpu.VMEM)
SMEM = pl.BlockSpec(memory_space=pltpu.SMEM)
PARAMS = pltpu.CompilerParams(vmem_limit_bytes=48 * 1024 * 1024)


def f32(*shape):
    return jax.ShapeDtypeStruct(shape, F32)


def call(body, outs, ins, scratch=(), flops=0, size=0):
    return pl.pallas_call(
        body,
        out_shape=outs,
        in_specs=ins,
        out_specs=jax.tree.map(lambda _: VMEM, outs),
        scratch_shapes=list(scratch),
        compiler_params=PARAMS,
        cost_estimate=pl.CostEstimate(flops=flops, bytes_accessed=size, transcendentals=0),
    )


def swaps(size, first):
    pairs = [(i, i + 1) for i in range(first, size - 1, 2)]
    return pairs + [(j, i) for i, j in pairs]


def shifts(size, step):
    return [(i, i + step) for i in range(size) if 0 <= i + step < size]


def lane_ids(shape):
    return lax.broadcasted_iota(jnp.int32, shape, len(shape) - 1)


def pack_kernel(place, spots, e_ref, h_ref, phase_ref, own, out_a, out_b, z_up, z_down):
    odd = place[0]
    for y in range(CY):
        for t in range(2):
            rows = pl.ds(t * CY + y, CX, stride=2 * CY)
            for c in range(3):
                own[2 * c + t, y] = e_ref[c, rows, :]
                own[2 * (c + 3) + t, y] = h_ref[c, rows, :]
            own[12 + t, y] = (phase_ref[rows, :] + 1).astype(F32)
            own[14 + t, y] = jnp.zeros((CX, LANES), F32)

    lane = lane_ids((1, LANES))

    def drop(i, carry):
        spot = spots[0, i]
        x, y = spot >> 11, (spot >> 8) & (CY - 1)
        t, place_z = 14 + ((spot >> 7) & 1), spot & (LANES - 1)
        row = own[t, y, pl.ds(x, 1), :]
        own[t, y, pl.ds(x, 1), :] = row + (lane == place_z).astype(F32)
        return carry

    lax.fori_loop(0, spots.shape[1], drop, 0)

    wide = lane_ids((CX, LANES))
    slot = wide // 8
    upper = wide % 8 >= W
    for y in range(CY):
        up = jnp.zeros((CX, LANES), F32)
        down = jnp.zeros((CX, LANES), F32)
        for f in range(FIELDS):
            here = slot == f
            up = jnp.where(here & ~upper, pltpu.roll(own[2 * f + 1, y], 8 * f + W, 1), up)
            down = jnp.where(here & upper, pltpu.roll(own[2 * f, y], 8 * f + W, 1), down)
        z_up[y] = up
        z_down[y] = down
    start_a = odd * (CY - W)
    start_b = (1 - odd) * (CY - W)
    for k in range(TILES):
        for i in range(W):
            out_a[k, i] = own[k, start_a + i]
            out_b[k, i] = own[k, start_b + i]


def edge_kernel(place, z_up, z_down, own_z, out_a, out_b):
    odd = place[0]
    own_z[...] = z_up[...] + z_down[...]
    start_a = odd * (CY - W)
    start_b = (1 - odd) * (CY - W)
    for i in range(W):
        out_a[i] = own_z[start_a + i]
        out_b[i] = own_z[start_b + i]


def side_kernel(place, own, own_z, in_a, in_b, z_a, z_b, out_up, out_down):
    odd = place[0]
    block_a, block_b = 3 * odd, 3 * (1 - odd)

    def move(read, k, block, first):
        for i in range(W):
            rows = read(first + i)
            out_up[k, block, pl.ds(W * i, W), :] = rows[CX - W :]
            out_down[k, block, pl.ds(W * i, W), :] = rows[:W]

    for k in range(TILES):
        for b in range(CY // W):
            move(lambda i: own[k, i], k, 1 + b, W * b)
        move(lambda i: in_a[k, i], k, block_a, 0)
        move(lambda i: in_b[k, i], k, block_b, 0)
    for b in range(CY // W):
        move(lambda i: own_z[i], TILES, 1 + b, W * b)
    move(lambda i: z_a[i], TILES, block_a, 0)
    move(lambda i: z_b[i], TILES, block_b, 0)


def field_kernel(place, own, own_z, in_a, in_b, z_a, z_b, from_low, from_high, out, s, zs, coef, power, pair):
    odd = place[0]
    first_a, first_b = odd * (CY + W), (1 - odd) * (CY + W)
    wide = lane_ids((NX, LANES))
    near = (wide < W) | (wide >= LANES - W)

    def settle(j, block, i, read, read_z):
        for k in range(TILES + 1):
            rows = jnp.concatenate(
                [
                    from_low[k, block, pl.ds(W * i, W), :],
                    read_z() if k == TILES else read(k),
                    from_high[k, block, pl.ds(W * i, W), :],
                ],
                axis=0,
            )
            if k == TILES:
                for f in range(FIELDS):
                    turned = pltpu.roll(rows, LANES - (8 * f + W), 1)
                    s[f, j, :, 2 * LANES :] = jnp.where(near, turned, 0.0)
            else:
                s[k // 2, j, :, pl.ds((k % 2) * LANES, LANES)] = rows

    for i in range(W):
        for b in range(CY // W):
            y = W * b + i
            settle(W + y, 1 + b, i, lambda k: own[k, y], lambda: own_z[y])
        settle(first_a + i, 3 * odd, i, lambda k: in_a[k, i], lambda: z_a[i])
        settle(first_b + i, 3 * (1 - odd), i, lambda k: in_b[k, i], lambda: z_b[i])

    def coefs(j, carry):
        phase = s[6, j]

        def chosen(table):
            value = jnp.zeros_like(phase)
            for index in range(4):
                value = jnp.where(phase == index + 1.0, table[index], value)
            return value

        coef[0, j] = chosen(ca_table)
        coef[1, j] = chosen(cb_table)
        coef[2, j] = chosen(sig_table)
        coef[3, j] = jnp.where(phase > 0.0, courant_dt, 0.0)
        power[j] = jnp.zeros_like(phase)
        return carry

    lax.fori_loop(0, NY, coefs, 0)

    span = 3 * LANES
    for step in range(ITERS):
        wave = 60.0 * math.sin(0.6 * (step + 0.5) * courant_dt)

        def plane(j, carry):
            back = jnp.maximum(j - 1, 0)
            ex, ey, ez = s[0, j], s[1, j], s[2, j]
            step_h = coef[3, j]
            hx = s[3, j] - step_h * ((s[2, j + 1] - ez) - (pltpu.roll(ey, span - 1, 1) - ey))
            hy = s[4, j] - step_h * ((pltpu.roll(ex, span - 1, 1) - ex) - (pltpu.roll(ez, NX - 1, 0) - ez))
            hz = s[5, j] - step_h * ((pltpu.roll(ey, NX - 1, 0) - ey) - (s[0, j + 1] - ex))
            s[3, j] = hx
            s[4, j] = hy
            s[5, j] = hz
            ca, cb, sig = coef[0, j], coef[1, j], coef[2, j]
            ex = ca * ex + cb * ((hz - s[5, back]) - (hy - pltpu.roll(hy, 1, 1)))
            ey = ca * ey + cb * ((hx - pltpu.roll(hx, 1, 1)) - (hz - pltpu.roll(hz, 1, 0)))
            ez = ca * ez + cb * ((hy - pltpu.roll(hy, 1, 0)) - (hx - s[3, back])) - cb * s[7, j] * wave
            s[0, j] = ex
            s[1, j] = ey
            s[2, j] = ez
            power[j] += sig * (ex * ex + ey * ey + ez * ez)
            return carry

        lax.fori_loop(step, NY - 1 - step, plane, 0)

    rows = []
    for t in range(CY // 2):
        halves = []
        for k in range(2):
            lanes = pl.ds(k * LANES, LANES)
            pair[...] = power[W + 2 * t, :, lanes] + power[W + 2 * t + 1, :, lanes]
            halves.append(pair[pl.ds(W, CX // 2, stride=2), :] + pair[pl.ds(W + 1, CX // 2, stride=2), :])
        rows.append(jnp.concatenate(halves, axis=1))
    stacked = jnp.concatenate(rows, axis=0)
    source = lax.broadcasted_iota(jnp.int32, (2 * LANES, LANES), 0)
    target = lax.broadcasted_iota(jnp.int32, (2 * LANES, LANES), 1)
    gather = (source // 2 == target).astype(F32)
    summed = jnp.dot(stacked, gather, precision=lax.Precision.HIGHEST, preferred_element_type=F32)
    out[...] = (summed * (1.0 / (8.0 * ITERS))).reshape(CY // 2, CX // 2, LANES)


def laplacian(t, side_a, side_b, before, after):
    rows, span = t.shape
    wide = lane_ids((rows, span))
    x = lax.broadcasted_iota(jnp.int32, (rows, span), 0)
    up_x = jnp.where(x == rows - 1, after, pltpu.roll(t, rows - 1, 0))
    down_x = jnp.where(x == 0, before, pltpu.roll(t, 1, 0))
    up_z = jnp.where(wide == span - 1, 0.0, pltpu.roll(t, span - 1, 1))
    down_z = jnp.where(wide == 0, 0.0, pltpu.roll(t, 1, 1))
    return up_x + down_x + side_a + side_b + up_z + down_z - 6.0 * t


def densified(packing, warmth):
    return packing + 0.3 * (1.0 - packing) * jnp.exp(-3.0 / (1.0 + warmth))


def warm_kernel(t_ref, p_ref, side_a, side_b, before, after, base, packed):
    t, p = t_ref[...], p_ref[...]
    lap = laplacian(t, side_a[...], side_b[...], before[...], after[...])
    base[...] = t + 0.1 * ((0.2 + p) * lap)
    packed[...] = densified(p, t)


def first_kernel(base, packed, heat, warmth, density):
    for k in range(heat.shape[0]):
        lanes = pl.ds(k * LANES, LANES)
        t = base[:, lanes] + heat[k]
        warmth[:, lanes] = t
        density[:, lanes] = densified(packed[:, lanes], t)


def second_kernel(t_ref, p_ref, heat, side_a, side_b, before, after, warmth):
    t = t_ref[...]
    lap = laplacian(t, side_a[...], side_b[...], before[...], after[...])
    grown = t + 0.1 * ((0.2 + p_ref[...]) * lap)
    for k in range(heat.shape[0]):
        lanes = slice(k * LANES, (k + 1) * LANES)
        warmth[:, lanes] = grown[:, lanes] + heat[k]


def around(t):
    pencils = lax.axis_size("gy") * lax.axis_size("gz")
    side_a = lax.ppermute(t, ("gy", "gz"), swaps(pencils, 1))
    side_b = lax.ppermute(t, ("gy", "gz"), swaps(pencils, 0))
    bricks = lax.axis_size("gx")
    before = lax.ppermute(t[-1:], "gx", shifts(bricks, 1))
    after = lax.ppermute(t[:1], "gx", shifts(bricks, -1))
    return side_a, side_b, before, after


def tile_rows(a):
    lead = a.shape[:-3]
    a = a.reshape(lead + (CX, CY, 2, LANES))
    return jnp.swapaxes(a, -3, -2).reshape(lead + (2 * CX * CY, LANES))


def local(e, h, phase, spots, warmth, packing):
    n_y, n_z, n_x = lax.axis_size("gy"), lax.axis_size("gz"), lax.axis_size("gx")
    place = (lax.axis_index("gy") % 2).astype(jnp.int32).reshape(1)
    across, within = swaps(n_y, 1), swaps(n_y, 0)
    warmth = warmth.reshape(CX // 2, -1)
    packing = packing.reshape(CX // 2, -1)
    pencil = f32(*warmth.shape)

    own, to_a, to_b, z_up, z_down = call(
        pack_kernel,
        (f32(TILES, CY, CX, LANES), f32(TILES, W, CX, LANES), f32(TILES, W, CX, LANES), f32(CY, CX, LANES), f32(CY, CX, LANES)),
        [SMEM, SMEM, VMEM, VMEM, VMEM],
    )(place, spots, tile_rows(e), tile_rows(h), tile_rows(phase))
    in_a = lax.ppermute(to_a, "gy", across)
    in_b = lax.ppermute(to_b, "gy", within)
    z_up = lax.ppermute(z_up, "gz", shifts(n_z, 1))
    z_down = lax.ppermute(z_down, "gz", shifts(n_z, -1))
    own_z, z_a, z_b = call(
        edge_kernel,
        (f32(CY, CX, LANES), f32(W, CX, LANES), f32(W, CX, LANES)),
        [SMEM, VMEM, VMEM],
    )(place, z_up, z_down)
    z_a = lax.ppermute(z_a, "gy", across)
    z_b = lax.ppermute(z_b, "gy", within)

    base, packed = call(warm_kernel, (pencil, pencil), [VMEM] * 6)(warmth, packing, *around(warmth))

    block = f32(TILES + 1, NY // W, W * W, LANES)
    to_up, to_down = call(side_kernel, (block, block), [SMEM] + [VMEM] * 6)(
        place, own, own_z, in_a, in_b, z_a, z_b
    )
    from_low = lax.ppermute(to_up, "gx", shifts(n_x, 1))
    from_high = lax.ppermute(to_down, "gx", shifts(n_x, -1))
    heat = call(
        field_kernel,
        f32(CY // 2, CX // 2, LANES),
        [SMEM] + [VMEM] * 8,
        scratch=[
            pltpu.VMEM((FIELDS, NY, NX, 3 * LANES), F32),
            pltpu.VMEM((NX, LANES), F32),
            pltpu.VMEM((4, NY, NX, 3 * LANES), F32),
            pltpu.VMEM((NY, NX, 3 * LANES), F32),
            pltpu.VMEM((NX, LANES), F32),
        ],
    )(place, own, own_z, in_a, in_b, z_a, z_b, from_low, from_high)
    heat = lax.all_to_all(heat, "gz", split_axis=0, concat_axis=0, tiled=True)
    warmth, density = call(first_kernel, (pencil, pencil), [VMEM] * 3)(base, packed, heat)
    result = call(second_kernel, pencil, [VMEM] * 7)(warmth, packed, heat, *around(warmth))
    shape = (CX // 2, 1, -1)
    return result.reshape(shape), density.reshape(shape)


def solution(mesh):
    return jax.shard_map(
        local,
        mesh=mesh,
        in_specs=(
            P(None, "gx", "gy", "gz"),
            P(None, "gx", "gy", "gz"),
            P("gx", "gy", "gz"),
            P(("gx", "gy", "gz"), None),
            P("gx", ("gy", "gz"), None),
            P("gx", ("gy", "gz"), None),
        ),
        out_specs=(P("gx", ("gy", "gz"), None), P("gx", ("gy", "gz"), None)),
        check_vma=False,
    )
```

time: 273 us -> 112 us (0.41)
  the two profiles are of different devices: /device:TPU:384 before, /device:TPU:31 now
where the time goes in v1:
time: 112 us; the launch traced here: 111 us
  starting transfers between devices  73.3 us (65%)
  waiting for transfers between devices  19.3 us (17%)
  Pallas kernels  12.9 us (12%)
  local copies, waits for them, and re-layouts  4.81 us (4%)
    ppermute x2, starting transfers between devices, around(): side_a = lax.ppermute(t, ('gy', 'gz'), swaps(pencils, 1))  21.2 us
    ppermute x1, starting transfers between devices, local(): in_a = lax.ppermute(to_a, 'gy', across)  15.9 us
    pallas_call x1, Pallas kernels, local(): call(field_kernel, f32(CY // 2, CX // 2, LANES), [SMEM] + [VMEM] * 8, scr...  11.2 us
    ppermute x1, waiting for transfers between devices, local(): z_a = lax.ppermute(z_a, 'gy', across)  9.53 us
    ppermute x2, starting transfers between devices, around(): before = lax.ppermute(t[-1:], 'gx', shifts(bricks, 1))  5.89 us
    ppermute x2, waiting for transfers between devices, around(): after = lax.ppermute(t[:1], 'gx', shifts(bricks, -1))  5.4 us
    all_to_all x1, starting transfers between devices, local(): heat = lax.all_to_all(heat, 'gz', split_axis=0, concat_axis=0, tiled=True)  5.25 us
    unnamed x16, local copies, waits for them, and re-layouts  4.81 us
  transfers between devices with their start and end apart: 17, of which 5 were waited for; matrix products, arithmetic and copies ran while one was open for 1% of the time, Pallas kernels for 10%

profile of v1, /device:TPU:31, one launch (start us, length us, event | category | flops | bytes accessed | tf_op | source)
XLA Modules:
  0.0 111.2 jit_solution(4513298143329027873)
XLA Ops:
  0.7 0.6 copy-done.3
  1.3 1.0 copy-done
  2.3 1.0 copy-done.1
  3.3 0.9 copy-done.2
  4.2 1.3 %shard_map.78 = (f32[16,8,16,128]{3,2,1,0:T(8,128)S(1)}, f32[16,4,16,128]{3,2,1,0:T(8,128)S(1)}, f32[16,4,16,128]{3,2,1,0:T(8,128)S(1)}, f32[8,16,128]{2,1,0:T(8,128)S(1)}, f32[8,16,128]{2,1,0:T(8,128)S(1)}) custom-call(s32[1]{0:T(128)} %bitcast.2.place, s32[1,16]{1,0:T(1,128)S(1)} %copy-done.3, f32[3,256,128]{2,1,0:T(8,128)S(1)} %bitcast.28, ...), custom_call_target="tpu_custom_call" | custom-call | tf_op jit(solution)/shard_map/pallas_call | solution.py:288
  5.5 15.9 %collective-permute-start.6 = (f32[16,4,16,128]{3,2,1,0:T(8,128)S(1)}, f32[16,4,16,128]{3,2,1,0:T(8,128)S(1)}, u32[]{:S(2)}, u32[]{:S(2)}) collective-permute-start(f32[16,4,16,128]{3,2,1,0:T(8,128)S(1)} %get-tuple-element.22), channel_id=1, source_target_pairs={{4,8},{12,16},{20,24},{28,32},{36,40},{44,48},{52,56},{8,4},{16,12... | collective-permute-start | bytes 1572872 | tf_op jit(solution)/shard_map/ppermute | solution.py:293
  21.4 1.9 %collective-permute-start.7 = (f32[16,4,16,128]{3,2,1,0:T(8,128)S(1)}, f32[16,4,16,128]{3,2,1,0:T(8,128)S(1)}, u32[]{:S(2)}, u32[]{:S(2)}) collective-permute-start(f32[16,4,16,128]{3,2,1,0:T(8,128)S(1)} %get-tuple-element.23), channel_id=1, source_target_pairs={{0,4},{8,12},{16,20},{24,28},{32,36},{40,44},{48,52},{56,60},{4,0}... | collective-permute-start | bytes 1572872 | tf_op jit(solution)/shard_map/ppermute | solution.py:294
  23.4 1.3 %collective-permute-start.4 = (f32[8,16,128]{2,1,0:T(8,128)S(1)}, f32[8,16,128]{2,1,0:T(8,128)S(1)}, u32[]{:S(2)}, u32[]{:S(2)}) collective-permute-start(f32[8,16,128]{2,1,0:T(8,128)S(1)} %get-tuple-element.19), channel_id=1, source_target_pairs={{0,1},{1,2},{2,3},{4,5},{5,6},{6,7},{8,9},{9,10},{10,11},{12,13},{... | collective-permute-start | bytes 196616 | tf_op jit(solution)/shard_map/ppermute | solution.py:295
  24.7 4.0 %collective-permute-start.5 = (f32[8,16,128]{2,1,0:T(8,128)S(1)}, f32[8,16,128]{2,1,0:T(8,128)S(1)}, u32[]{:S(2)}, u32[]{:S(2)}) collective-permute-start(f32[8,16,128]{2,1,0:T(8,128)S(1)} %get-tuple-element.20), channel_id=1, source_target_pairs={{1,0},{2,1},{3,2},{5,4},{6,5},{7,6},{9,8},{10,9},{11,10},{13,12},{... | collective-permute-start | bytes 196616 | tf_op jit(solution)/shard_map/ppermute | solution.py:296
  28.7 1.3 %collective-permute-done.5.z_down = f32[8,16,128]{2,1,0:T(8,128)S(1)} collective-permute-done((f32[8,16,128]{2,1,0:T(8,128)S(1)}, f32[8,16,128]{2,1,0:T(8,128)S(1)}, u32[]{:S(2)}, u32[]{:S(2)}) %collective-permute-start.5) | collective-permute-done | bytes 65568 | tf_op jit(solution)/shard_map/ppermute | solution.py:296
  30.0 4.6 %collective-permute-start.8 = (f32[4,16,128]{2,1,0:T(8,128)S(1)}, f32[4,16,128]{2,1,0:T(8,128)S(1)}, u32[]{:S(2)}, u32[]{:S(2)}) collective-permute-start(f32[4,16,128]{2,1,0:T(8,128)S(1)} %get-tuple-element.24), channel_id=1, source_target_pairs={{4,8},{12,16},{20,24},{28,32},{36,40},{44,48},{52,56},{8,4},{16,12... | collective-permute-start | bytes 98312 | tf_op jit(solution)/shard_map/ppermute | solution.py:302
  34.6 1.9 %collective-permute-start.9 = (f32[4,16,128]{2,1,0:T(8,128)S(1)}, f32[4,16,128]{2,1,0:T(8,128)S(1)}, u32[]{:S(2)}, u32[]{:S(2)}) collective-permute-start(f32[4,16,128]{2,1,0:T(8,128)S(1)} %get-tuple-element.25), channel_id=1, source_target_pairs={{0,4},{8,12},{16,20},{24,28},{32,36},{40,44},{48,52},{56,60},{4,0}... | collective-permute-start | bytes 98312 | tf_op jit(solution)/shard_map/ppermute | solution.py:303
  36.6 9.5 %collective-permute-done.8.z_a = f32[4,16,128]{2,1,0:T(8,128)S(1)} collective-permute-done((f32[4,16,128]{2,1,0:T(8,128)S(1)}, f32[4,16,128]{2,1,0:T(8,128)S(1)}, u32[]{:S(2)}, u32[]{:S(2)}) %collective-permute-start.8) | collective-permute-done | bytes 32800 | tf_op jit(solution)/shard_map/ppermute | solution.py:302
  46.1 0.1 shard_map.80
  46.3 3.5 %collective-permute-start.10 = (f32[17,4,16,128]{3,2,1,0:T(8,128)S(1)}, f32[17,4,16,128]{3,2,1,0:T(8,128)S(1)}, u32[]{:S(2)}, u32[]{:S(2)}) collective-permute-start(f32[17,4,16,128]{3,2,1,0:T(8,128)S(1)} %get-tuple-element.26), channel_id=1, source_target_pairs={{0,64},{64,128},{128,192},{192,256},{256,320},{320,384},{384,448},... | collective-permute-start | bytes 1671176 | tf_op jit(solution)/shard_map/ppermute | solution.py:311
  49.8 1.3 %collective-permute-start.11 = (f32[17,4,16,128]{3,2,1,0:T(8,128)S(1)}, f32[17,4,16,128]{3,2,1,0:T(8,128)S(1)}, u32[]{:S(2)}, u32[]{:S(2)}) collective-permute-start(f32[17,4,16,128]{3,2,1,0:T(8,128)S(1)} %get-tuple-element.27), channel_id=1, source_target_pairs={{64,0},{128,64},{192,128},{256,192},{320,256},{384,320},{448,384},... | collective-permute-start | bytes 1671176 | tf_op jit(solution)/shard_map/ppermute | solution.py:312
  51.1 14.2 %collective-permute-start = (f32[8,512]{1,0:T(8,128)S(1)}, f32[8,512]{1,0:T(8,128)S(1)}, u32[]{:S(2)}, u32[]{:S(2)}) collective-permute-start(f32[8,512]{1,0:T(8,128)S(1)} %bitcast.31), channel_id=1, source_target_pairs={{1,2},{3,4},{5,6},{7,8},{9,10},{11,12},{13,14},{15,16},{17,18},{19... | collective-permute-start | bytes 49160 | tf_op jit(solution)/shard_map/ppermute | solution.py:266
  65.3 1.9 %collective-permute-start.1 = (f32[8,512]{1,0:T(8,128)S(1)}, f32[8,512]{1,0:T(8,128)S(1)}, u32[]{:S(2)}, u32[]{:S(2)}) collective-permute-start(f32[8,512]{1,0:T(8,128)S(1)} %bitcast.32), channel_id=1, source_target_pairs={{0,1},{2,3},{4,5},{6,7},{8,9},{10,11},{12,13},{14,15},{16,17},{18,... | collective-permute-start | bytes 49160 | tf_op jit(solution)/shard_map/ppermute | solution.py:267
  67.3 11.2 %shard_map.81 = f32[4,8,128]{2,1,0:T(8,128)} custom-call(s32[1]{0:T(128)} %bitcast.2.place, f32[16,8,16,128]{3,2,1,0:T(8,128)S(1)} %get-tuple-element.18.own, f32[8,16,128]{2,1,0:T(8,128)S(1)} %get-tuple-element.21.own_z, f32[16,4,16,128]{3,2,1,0:T(8,128)S(1)} %collective-permute-done.6.in_a, f32[16,4,16,128]{3,2,1,0:T(8,128)S(1)} %collective-permute-done.7.in_b, ...), custom_call_target="tpu_custom_call" | custom-call | tf_op jit(solution)/shard_map/pallas_call | solution.py:313
  78.5 5.2 %all-to-all-start = ((f32[4,8,128]{2,1,0:T(8,128)}), f32[4,8,128]{2,1,0:T(8,128)S(1)}, u32[]{:S(2)}, u32[]{:S(2)}) async-start(f32[4,8,128]{2,1,0:T(8,128)} %shard_map.81), calls=%async_computation | async-start | bytes 32768 | tf_op jit(solution)/shard_map/all_to_all | solution.py:325
  83.8 4.3 %collective-permute-start.2 = (f32[1,512]{1,0:T(1,128)S(1)}, f32[1,512]{1,0:T(1,128)S(1)}, u32[]{:S(2)}, u32[]{:S(2)}) collective-permute-start(f32[1,512]{1,0:T(1,128)S(1)} %get-tuple-element.35), channel_id=1, source_target_pairs={{0,64},{64,128},{128,192},{192,256},{256,320},{320,384},{384,448},... | collective-permute-start | bytes 6152 | tf_op jit(solution)/shard_map/ppermute | solution.py:269
  88.0 1.3 %collective-permute-start.3 = (f32[1,512]{1,0:T(1,128)S(1)}, f32[1,512]{1,0:T(1,128)S(1)}, u32[]{:S(2)}, u32[]{:S(2)}) collective-permute-start(f32[1,512]{1,0:T(1,128)S(1)} %get-tuple-element.34), channel_id=1, source_target_pairs={{64,0},{128,64},{192,128},{256,192},{320,256},{384,320},{448,384},... | collective-permute-start | bytes 6152 | tf_op jit(solution)/shard_map/ppermute | solution.py:270
  89.3 3.0 %collective-permute-done.3.after = f32[1,512]{1,0:T(1,128)S(1)} collective-permute-done((f32[1,512]{1,0:T(1,128)S(1)}, f32[1,512]{1,0:T(1,128)S(1)}, u32[]{:S(2)}, u32[]{:S(2)}) %collective-permute-start.3) | collective-permute-done | bytes 2080 | tf_op jit(solution)/shard_map/ppermute | solution.py:270
  92.5 7.0 %collective-permute-start.12 = (f32[8,512]{1,0:T(8,128)S(1)}, f32[8,512]{1,0:T(8,128)S(1)}, u32[]{:S(2)}, u32[]{:S(2)}) collective-permute-start(f32[8,512]{1,0:T(8,128)S(1)} %get-tuple-element.28.t_ref), channel_id=1, source_target_pairs={{1,2},{3,4},{5,6},{7,8},{9,10},{11,12},{13,14},{15,16},{17,18},{19... | collective-permute-start | bytes 49160 | tf_op jit(solution)/shard_map/ppermute | solution.py:266
  99.5 1.9 %collective-permute-start.13 = (f32[8,512]{1,0:T(8,128)S(1)}, f32[8,512]{1,0:T(8,128)S(1)}, u32[]{:S(2)}, u32[]{:S(2)}) collective-permute-start(f32[8,512]{1,0:T(8,128)S(1)} %get-tuple-element.28.t_ref), channel_id=1, source_target_pairs={{0,1},{2,3},{4,5},{6,7},{8,9},{10,11},{12,13},{14,15},{16,17},{18,... | collective-permute-start | bytes 49160 | tf_op jit(solution)/shard_map/ppermute | solution.py:267
  101.5 1.6 %collective-permute-start.14 = (f32[1,512]{1,0:T(1,128)S(1)}, f32[1,512]{1,0:T(1,128)S(1)}, u32[]{:S(2)}, u32[]{:S(2)}) collective-permute-start(f32[1,512]{1,0:T(1,128)S(1)} %get-tuple-element.33), channel_id=1, source_target_pairs={{0,64},{64,128},{128,192},{192,256},{256,320},{320,384},{384,448},... | collective-permute-start | bytes 6152 | tf_op jit(solution)/shard_map/ppermute | solution.py:269
  103.1 1.3 %collective-permute-start.15 = (f32[1,512]{1,0:T(1,128)S(1)}, f32[1,512]{1,0:T(1,128)S(1)}, u32[]{:S(2)}, u32[]{:S(2)}) collective-permute-start(f32[1,512]{1,0:T(1,128)S(1)} %get-tuple-element.32), channel_id=1, source_target_pairs={{64,0},{128,64},{192,128},{256,192},{320,256},{384,320},{448,384},... | collective-permute-start | bytes 6152 | tf_op jit(solution)/shard_map/ppermute | solution.py:270
  104.4 0.6 copy.9
  105.0 2.4 %collective-permute-done.15.after = f32[1,512]{1,0:T(1,128)S(1)} collective-permute-done((f32[1,512]{1,0:T(1,128)S(1)}, f32[1,512]{1,0:T(1,128)S(1)}, u32[]{:S(2)}, u32[]{:S(2)}) %collective-permute-start.15) | collective-permute-done | bytes 2080 | tf_op jit(solution)/shard_map/ppermute | solution.py:270
  107.4 3.0 %collective-permute-done.12.side_a = f32[8,512]{1,0:T(8,128)S(1)} collective-permute-done((f32[8,512]{1,0:T(8,128)S(1)}, f32[8,512]{1,0:T(8,128)S(1)}, u32[]{:S(2)}, u32[]{:S(2)}) %collective-permute-start.12) | collective-permute-done | bytes 16416 | tf_op jit(solution)/shard_map/ppermute | solution.py:266
  110.5 0.1 shard_map.83
  110.6 0.6 copy.8
  (27 shorter events, 0.2 us)
Async XLA Ops:
  0.6 0.7 copy-start.3
  1.3 1.0 copy-start
  2.3 1.0 copy-start.1
  3.3 0.9 copy-start.2
  5.5 40.6 %collective-permute-start.6 = (f32[16,4,16,128]{3,2,1,0:T(8,128)S(1)}, f32[16,4,16,128]{3,2,1,0:T(8,128)S(1)}, u32[]{:S(2)}, u32[]{:S(2)}) collective-permute-start(f32[16,4,16,128]{3,2,1,0:T(8,128)S(1)} %get-tuple-element.22), channel_id=1, source_target_pairs={{4,8},{12,16},{20,24},{28,32},{36,40},{44,48},{52,56},{8,4},{16,12... | collective-permute-start | bytes 1572872 | tf_op jit(solution)/shard_map/ppermute | solution.py:293
  21.4 24.7 %collective-permute-start.7 = (f32[16,4,16,128]{3,2,1,0:T(8,128)S(1)}, f32[16,4,16,128]{3,2,1,0:T(8,128)S(1)}, u32[]{:S(2)}, u32[]{:S(2)}) collective-permute-start(f32[16,4,16,128]{3,2,1,0:T(8,128)S(1)} %get-tuple-element.23), channel_id=1, source_target_pairs={{0,4},{8,12},{16,20},{24,28},{32,36},{40,44},{48,52},{56,60},{4,0}... | collective-permute-start | bytes 1572872 | tf_op jit(solution)/shard_map/ppermute | solution.py:294
  23.4 5.3 %collective-permute-start.4 = (f32[8,16,128]{2,1,0:T(8,128)S(1)}, f32[8,16,128]{2,1,0:T(8,128)S(1)}, u32[]{:S(2)}, u32[]{:S(2)}) collective-permute-start(f32[8,16,128]{2,1,0:T(8,128)S(1)} %get-tuple-element.19), channel_id=1, source_target_pairs={{0,1},{1,2},{2,3},{4,5},{5,6},{6,7},{8,9},{9,10},{10,11},{12,13},{... | collective-permute-start | bytes 196616 | tf_op jit(solution)/shard_map/ppermute | solution.py:295
  24.7 5.3 %collective-permute-start.5 = (f32[8,16,128]{2,1,0:T(8,128)S(1)}, f32[8,16,128]{2,1,0:T(8,128)S(1)}, u32[]{:S(2)}, u32[]{:S(2)}) collective-permute-start(f32[8,16,128]{2,1,0:T(8,128)S(1)} %get-tuple-element.20), channel_id=1, source_target_pairs={{1,0},{2,1},{3,2},{5,4},{6,5},{7,6},{9,8},{10,9},{11,10},{13,12},{... | collective-permute-start | bytes 196616 | tf_op jit(solution)/shard_map/ppermute | solution.py:296
  30.0 16.1 %collective-permute-start.8 = (f32[4,16,128]{2,1,0:T(8,128)S(1)}, f32[4,16,128]{2,1,0:T(8,128)S(1)}, u32[]{:S(2)}, u32[]{:S(2)}) collective-permute-start(f32[4,16,128]{2,1,0:T(8,128)S(1)} %get-tuple-element.24), channel_id=1, source_target_pairs={{4,8},{12,16},{20,24},{28,32},{36,40},{44,48},{52,56},{8,4},{16,12... | collective-permute-start | bytes 98312 | tf_op jit(solution)/shard_map/ppermute | solution.py:302
  34.6 11.5 %collective-permute-start.9 = (f32[4,16,128]{2,1,0:T(8,128)S(1)}, f32[4,16,128]{2,1,0:T(8,128)S(1)}, u32[]{:S(2)}, u32[]{:S(2)}) collective-permute-start(f32[4,16,128]{2,1,0:T(8,128)S(1)} %get-tuple-element.25), channel_id=1, source_target_pairs={{0,4},{8,12},{16,20},{24,28},{32,36},{40,44},{48,52},{56,60},{4,0}... | collective-permute-start | bytes 98312 | tf_op jit(solution)/shard_map/ppermute | solution.py:303
  46.1 5.0 %copy-start.4 = (f32[8,1,512]{2,1,0:T(1,128)S(1)}, f32[8,1,512]{2,1,0:T(1,128)}, u32[]{:S(2)}) copy-start(f32[8,1,512]{2,1,0:T(1,128)} %param.10) | copy-start | bytes 49156
  46.3 21.0 %collective-permute-start.10 = (f32[17,4,16,128]{3,2,1,0:T(8,128)S(1)}, f32[17,4,16,128]{3,2,1,0:T(8,128)S(1)}, u32[]{:S(2)}, u32[]{:S(2)}) collective-permute-start(f32[17,4,16,128]{3,2,1,0:T(8,128)S(1)} %get-tuple-element.26), channel_id=1, source_target_pairs={{0,64},{64,128},{128,192},{192,256},{256,320},{320,384},{384,448},... | collective-permute-start | bytes 1671176 | tf_op jit(solution)/shard_map/ppermute | solution.py:311
  49.8 17.5 %collective-permute-start.11 = (f32[17,4,16,128]{3,2,1,0:T(8,128)S(1)}, f32[17,4,16,128]{3,2,1,0:T(8,128)S(1)}, u32[]{:S(2)}, u32[]{:S(2)}) collective-permute-start(f32[17,4,16,128]{3,2,1,0:T(8,128)S(1)} %get-tuple-element.27), channel_id=1, source_target_pairs={{64,0},{128,64},{192,128},{256,192},{320,256},{384,320},{448,384},... | collective-permute-start | bytes 1671176 | tf_op jit(solution)/shard_map/ppermute | solution.py:312
  51.1 41.2 %collective-permute-start = (f32[8,512]{1,0:T(8,128)S(1)}, f32[8,512]{1,0:T(8,128)S(1)}, u32[]{:S(2)}, u32[]{:S(2)}) collective-permute-start(f32[8,512]{1,0:T(8,128)S(1)} %bitcast.31), channel_id=1, source_target_pairs={{1,2},{3,4},{5,6},{7,8},{9,10},{11,12},{13,14},{15,16},{17,18},{19... | collective-permute-start | bytes 49160 | tf_op jit(solution)/shard_map/ppermute | solution.py:266
  65.3 27.0 %collective-permute-start.1 = (f32[8,512]{1,0:T(8,128)S(1)}, f32[8,512]{1,0:T(8,128)S(1)}, u32[]{:S(2)}, u32[]{:S(2)}) collective-permute-start(f32[8,512]{1,0:T(8,128)S(1)} %bitcast.32), channel_id=1, source_target_pairs={{0,1},{2,3},{4,5},{6,7},{8,9},{10,11},{12,13},{14,15},{16,17},{18,... | collective-permute-start | bytes 49160 | tf_op jit(solution)/shard_map/ppermute | solution.py:267
  78.5 10.8 %copy-start.5 = (f32[8,1,512]{2,1,0:T(1,128)S(1)}, f32[8,1,512]{2,1,0:T(1,128)}, u32[]{:S(2)}) copy-start(f32[8,1,512]{2,1,0:T(1,128)} %param.11) | copy-start | bytes 49156
  78.5 13.9 %all-to-all-start = ((f32[4,8,128]{2,1,0:T(8,128)}), f32[4,8,128]{2,1,0:T(8,128)S(1)}, u32[]{:S(2)}, u32[]{:S(2)}) async-start(f32[4,8,128]{2,1,0:T(8,128)} %shard_map.81), calls=%async_computation | async-start | bytes 32768 | tf_op jit(solution)/shard_map/all_to_all | solution.py:325
  83.8 5.6 %collective-permute-start.2 = (f32[1,512]{1,0:T(1,128)S(1)}, f32[1,512]{1,0:T(1,128)S(1)}, u32[]{:S(2)}, u32[]{:S(2)}) collective-permute-start(f32[1,512]{1,0:T(1,128)S(1)} %get-tuple-element.35), channel_id=1, source_target_pairs={{0,64},{64,128},{128,192},{192,256},{256,320},{320,384},{384,448},... | collective-permute-start | bytes 6152 | tf_op jit(solution)/shard_map/ppermute | solution.py:269
  88.0 4.3 %collective-permute-start.3 = (f32[1,512]{1,0:T(1,128)S(1)}, f32[1,512]{1,0:T(1,128)S(1)}, u32[]{:S(2)}, u32[]{:S(2)}) collective-permute-start(f32[1,512]{1,0:T(1,128)S(1)} %get-tuple-element.34), channel_id=1, source_target_pairs={{64,0},{128,64},{192,128},{256,192},{320,256},{384,320},{448,384},... | collective-permute-start | bytes 6152 | tf_op jit(solution)/shard_map/ppermute | solution.py:270
  92.5 18.0 %collective-permute-start.12 = (f32[8,512]{1,0:T(8,128)S(1)}, f32[8,512]{1,0:T(8,128)S(1)}, u32[]{:S(2)}, u32[]{:S(2)}) collective-permute-start(f32[8,512]{1,0:T(8,128)S(1)} %get-tuple-element.28.t_ref), channel_id=1, source_target_pairs={{1,2},{3,4},{5,6},{7,8},{9,10},{11,12},{13,14},{15,16},{17,18},{19... | collective-permute-start | bytes 49160 | tf_op jit(solution)/shard_map/ppermute | solution.py:266
  99.5 10.9 %collective-permute-start.13 = (f32[8,512]{1,0:T(8,128)S(1)}, f32[8,512]{1,0:T(8,128)S(1)}, u32[]{:S(2)}, u32[]{:S(2)}) collective-permute-start(f32[8,512]{1,0:T(8,128)S(1)} %get-tuple-element.28.t_ref), channel_id=1, source_target_pairs={{0,1},{2,3},{4,5},{6,7},{8,9},{10,11},{12,13},{14,15},{16,17},{18,... | collective-permute-start | bytes 49160 | tf_op jit(solution)/shard_map/ppermute | solution.py:267
  101.5 3.6 %collective-permute-start.14 = (f32[1,512]{1,0:T(1,128)S(1)}, f32[1,512]{1,0:T(1,128)S(1)}, u32[]{:S(2)}, u32[]{:S(2)}) collective-permute-start(f32[1,512]{1,0:T(1,128)S(1)} %get-tuple-element.33), channel_id=1, source_target_pairs={{0,64},{64,128},{128,192},{192,256},{256,320},{320,384},{384,448},... | collective-permute-start | bytes 6152 | tf_op jit(solution)/shard_map/ppermute | solution.py:269
  103.1 4.3 %collective-permute-start.15 = (f32[1,512]{1,0:T(1,128)S(1)}, f32[1,512]{1,0:T(1,128)S(1)}, u32[]{:S(2)}, u32[]{:S(2)}) collective-permute-start(f32[1,512]{1,0:T(1,128)S(1)} %get-tuple-element.32), channel_id=1, source_target_pairs={{64,0},{128,64},{192,128},{256,192},{320,256},{384,320},{448,384},... | collective-permute-start | bytes 6152 | tf_op jit(solution)/shard_map/ppermute | solution.py:270

commit v2 on v1

v2 whole, which is shorter than its diff:
```python
import math

import jax
import jax.numpy as jnp
from jax import lax
from jax.experimental import pallas as pl
from jax.experimental.pallas import tpu as pltpu
from jax.sharding import PartitionSpec as P

ITERS = 4
W = 4
CX, CY, CZ = 16, 8, 256
TX, TY = CX // 2, CY // 2
PAD = W
NX, NY = CX + 2 * PAD, CY + 2 * W
LANES = 128
FIELDS = 8
TILES = 2 * FIELDS

eps_table = (3.0, 9.0, 12.0, 1.0)
sig_table = (0.05, 0.01, 0.4, 0.0)
courant_dt = 0.99 / math.sqrt(3.0)
loss_table = tuple(s * courant_dt / (2.0 * e) for s, e in zip(sig_table, eps_table))
ca_table = tuple((1.0 - l) / (1.0 + l) for l in loss_table)
cb_table = tuple(courant_dt / (e * (1.0 + l)) for l, e in zip(loss_table, eps_table))

F32 = jnp.float32
VMEM = pl.BlockSpec(memory_space=pltpu.VMEM)
HBM = pl.BlockSpec(memory_space=pltpu.HBM)

Y_PLANES = (4, 4, 4, 4, 3, 4, 3, 3)
Y_START = []
for planes in Y_PLANES:
    Y_START += [sum(2 * p for p in Y_PLANES[: len(Y_START) // 2]), 0]
    Y_START[-1] = Y_START[-2] + planes
Y_TOTAL = 2 * sum(Y_PLANES)


def side_rows(low):
    table, place = {}, 0
    for k in range(TILES + 1):
        field = k // 2
        most = W - 1 if field in ((3, 6, 7) if low else (3, 4, 5, 6, 7)) else W
        for j in range(NY):
            corner = W - j if low else j - (W + CY - 1)
            count = min(most, W - corner) if corner > 0 else most
            table[k, j] = (place, count)
            place += count
    return table, place


LOW_TABLE, LOW_ROWS = side_rows(True)
HIGH_TABLE, HIGH_ROWS = side_rows(False)


def f32(*shape):
    return jax.ShapeDtypeStruct(shape, F32)


def call(body, outs, ins, scratch=(), limit=24):
    return pl.pallas_call(
        body,
        out_shape=outs,
        in_specs=ins,
        out_specs=jax.tree.map(lambda _: VMEM, outs),
        scratch_shapes=list(scratch),
        compiler_params=pltpu.CompilerParams(vmem_limit_bytes=limit * 1024 * 1024),
    )


def swaps(size, first):
    pairs = [(i, i + 1) for i in range(first, size - 1, 2)]
    return pairs + [(j, i) for i, j in pairs]


def shifts(size, step):
    return [(i, i + step) for i in range(size) if 0 <= i + step < size]


def lane_ids(shape):
    return lax.broadcasted_iota(jnp.int32, shape, len(shape) - 1)


def parity():
    return lax.rem(lax.axis_index("gy"), 2)


def pack_kernel(spots_hbm, e_hbm, h_hbm, phase_hbm, t_hbm, own, out_a, out_b, shared, spots, e_ref, h_ref, phase_ref, heat, sems):
    odd = parity()
    copies = [
        pltpu.make_async_copy(spots_hbm, spots, sems.at[0]),
        pltpu.make_async_copy(phase_hbm, phase_ref, sems.at[1]),
    ]
    for c in range(3):
        copies.append(pltpu.make_async_copy(e_hbm.at[c], e_ref.at[c], sems.at[2 + c]))
    for c in range(3):
        copies.append(pltpu.make_async_copy(h_hbm.at[c], h_ref.at[c], sems.at[5 + c]))
    copies.append(pltpu.make_async_copy(t_hbm, heat, sems.at[8]))
    for copy in copies:
        copy.start()
    for t in range(2):
        own[14 + t] = jnp.zeros((CY, CX, LANES), F32)

    lane = lane_ids((1, LANES))

    def drop(i, carry):
        spot = spots[0, i]
        x, y = spot >> 11, (spot >> 8) & (CY - 1)
        t, place_z = 14 + ((spot >> 7) & 1), spot & (LANES - 1)
        row = own[t, y, pl.ds(x, 1), :]
        own[t, y, pl.ds(x, 1), :] = row + (lane == place_z).astype(F32)
        return carry

    copies[0].wait()
    lax.fori_loop(0, spots.shape[1], drop, 0)

    def spread(k, source):
        for y in range(CY):
            for t in range(2):
                own[k + t, y] = source[pl.ds(t * CY + y, CX, stride=2 * CY), :].astype(F32)

    copies[1].wait()
    phase_ref[...] += 1
    spread(12, phase_ref)
    for c in range(3):
        copies[2 + c].wait()
        spread(2 * c, e_ref.at[c])
    for c in range(3):
        copies[5 + c].wait()
        spread(2 * (3 + c), h_ref.at[c])
    for k in range(TILES):
        planes = Y_PLANES[k // 2]
        for i in range(planes):
            out_a[Y_START[k] + i] = own[k, odd * (CY - planes) + i]
            out_b[Y_START[k] + i] = own[k, (1 - odd) * (CY - planes) + i]

    wide = lane_ids((CX, LANES))
    slot = wide // 8
    upper = wide % 8 >= W
    for y in range(CY):
        edge = jnp.zeros((CX, LANES), F32)
        for f in range(FIELDS):
            shift = 8 * f + W
            ends = jnp.where(upper, pltpu.roll(own[2 * f, y], shift, 1), pltpu.roll(own[2 * f + 1, y], shift, 1))
            edge = jnp.where(slot == f, ends, edge)
        shared[pl.ds(CX * y, CX), :] = edge
    copies[8].wait()
    for k in range(heat.shape[2] // LANES):
        shared[pl.ds(CX * CY + k * TX, TX), :] = heat[:, 0, pl.ds(k * LANES, LANES)]


def edge_kernel(from_below, from_above, own_z, out_a, out_b):
    odd, me = parity(), lax.axis_index("gz")
    upper = lane_ids((CX, LANES)) % 8 >= W
    has_below = (me > 0).astype(F32)
    has_above = (me < lax.axis_size("gz") - 1).astype(F32)
    for y in range(CY):
        rows = pl.ds(CX * y, CX)
        own_z[y] = jnp.where(upper, from_above[rows, :] * has_above, from_below[rows, :] * has_below)
    thermal = pl.ds(CX * CY, from_below.shape[0] - CX * CY)
    below, above = from_below[thermal, :], from_above[thermal, :]
    for out, up in ((out_a, odd), (out_b, 1 - odd)):
        for i in range(W):
            out[pl.ds(CX * i, CX), :] = own_z[up * (CY - W) + i]
        out[pl.ds(CX * W, thermal.size), :] = jnp.where(up == 1, below, above)


def side_kernel(own, own_z, in_a, in_b, z_a, z_b, warmth, out_up, out_down):
    odd = parity()

    def move(k, j, read):
        for out, table, up in ((out_up, LOW_TABLE, True), (out_down, HIGH_TABLE, False)):
            start, count = table[k, j]
            if count:
                rows = read()
                out[pl.ds(start, count), :] = rows[CX - count :] if up else rows[:count]

    for y in range(CY):
        for k in range(TILES):
            move(k, W + y, lambda: own[k, y])
        move(TILES, W + y, lambda: own_z[y])
    for k in range(warmth.shape[0] // TX):
        out_up[pl.ds(LOW_ROWS + k, 1), :] = warmth[pl.ds(k * TX + TX - 1, 1), :]
        out_down[pl.ds(HIGH_ROWS + k, 1), :] = warmth[pl.ds(k * TX, 1), :]

    def outside(low, high, z_low, z_high):
        for k in range(TILES):
            planes = Y_PLANES[k // 2]
            for i in range(planes):
                move(k, W - planes + i, lambda: low[Y_START[k] + i])
                move(k, W + CY + i, lambda: high[Y_START[k] + i])
        for i in range(W):
            move(TILES, i, lambda: z_low[pl.ds(CX * i, CX), :])
            move(TILES, W + CY + i, lambda: z_high[pl.ds(CX * i, CX), :])
    @pl.when(odd == 1)
    def _():
        outside(in_b, in_a, z_b, z_a)

    @pl.when(odd == 0)
    def _():
        outside(in_a, in_b, z_a, z_b)


def field_kernel(own, own_z, in_a, in_b, z_a, z_b, from_low, from_high, out, s, zs, coef, reach, power, pair):
    odd = parity()
    span = 3 * LANES
    middle = pl.ds(PAD, CX)
    outer = (pl.ds(0, PAD), pl.ds(PAD + CX, PAD))

    def lanes(k):
        return pl.ds((k % 2) * LANES, LANES)

    blank = jnp.zeros((PAD, LANES), F32)
    for j in range(NY):
        for rows in outer:
            for k in range(TILES):
                s[k // 2, j, rows, lanes(k)] = blank
            zs[j, rows, :] = blank
        for k in range(TILES + 1):
            start, count = LOW_TABLE[k, j]
            if count:
                part = from_low[pl.ds(start, count), :]
                if k < TILES:
                    s[k // 2, j, pl.ds(PAD - count, count), lanes(k)] = part
                else:
                    zs[j, pl.ds(PAD - count, count), :] = part
            start, count = HIGH_TABLE[k, j]
            if count:
                part = from_high[pl.ds(start, count), :]
                if k < TILES:
                    s[k // 2, j, pl.ds(PAD + CX, count), lanes(k)] = part
                else:
                    zs[j, pl.ds(PAD + CX, count), :] = part
    for y in range(CY):
        for k in range(TILES):
            s[k // 2, W + y, middle, lanes(k)] = own[k, y]
        zs[W + y, middle, :] = own_z[y]

    def outside(low, high, z_low, z_high):
        for k in range(TILES):
            planes = Y_PLANES[k // 2]
            if planes < W:
                s[k // 2, 0, middle, lanes(k)] = jnp.zeros((CX, LANES), F32)
                s[k // 2, NY - 1, middle, lanes(k)] = jnp.zeros((CX, LANES), F32)
            for i in range(planes):
                s[k // 2, W - planes + i, middle, lanes(k)] = low[Y_START[k] + i]
                s[k // 2, W + CY + i, middle, lanes(k)] = high[Y_START[k] + i]
        for i in range(W):
            zs[i, middle, :] = z_low[pl.ds(CX * i, CX), :]
            zs[W + CY + i, middle, :] = z_high[pl.ds(CX * i, CX), :]

    @pl.when(odd == 1)
    def _():
        outside(in_b, in_a, z_b, z_a)

    @pl.when(odd == 0)
    def _():
        outside(in_a, in_b, z_a, z_b)

    narrow = lane_ids((NX, LANES))
    near = (narrow < W) | (narrow >= LANES - W)
    for j in range(NY):
        edges = zs[j]
        for f in range(FIELDS):
            s[f, j, :, 2 * LANES :] = jnp.where(near, pltpu.roll(edges, LANES - (8 * f + W), 1), 0.0)

    wide = lane_ids((NX, span))
    x = lax.broadcasted_iota(jnp.int32, (NX, span), 0)
    inside = jnp.where((x < PAD) & (lax.axis_index("gx") == 0), 0.0, courant_dt)
    inside = jnp.where((wide >= span - W) & (lax.axis_index("gz") == 0), 0.0, inside)
    reach[0] = inside
    reach[1] = inside * (lax.axis_index("gy") > 0).astype(F32)

    def coefs(j, carry):
        phase = s[6, j]

        def chosen(table):
            value = jnp.zeros_like(phase)
            for index in range(4):
                value = jnp.where(phase == index + 1.0, table[index], value)
            return value

        coef[0, j] = chosen(ca_table)
        coef[1, j] = chosen(cb_table)
        coef[2, j] = chosen(sig_table)
        return carry

    lax.fori_loop(0, NY, coefs, 0)

    for step in range(ITERS):
        wave = 60.0 * math.sin(0.6 * (step + 0.5) * courant_dt)

        def magnetic(j):
            ex, ey, ez = s[0, j], s[1, j], s[2, j]
            step_h = reach[0 if j >= W else 1]
            s[3, j] -= step_h * ((s[2, j + 1] - ez) - (pltpu.roll(ey, span - 1, 1) - ey))
            s[4, j] -= step_h * ((pltpu.roll(ex, span - 1, 1) - ex) - (pltpu.roll(ez, NX - 1, 0) - ez))
            s[5, j] -= step_h * ((pltpu.roll(ey, NX - 1, 0) - ey) - (s[0, j + 1] - ex))

        def electric(j):
            hx, hy, hz = s[3, j], s[4, j], s[5, j]
            ca, cb, sig = coef[0, j], coef[1, j], coef[2, j]
            ex = ca * s[0, j] + cb * ((hz - s[5, j - 1]) - (hy - pltpu.roll(hy, 1, 1)))
            ey = ca * s[1, j] + cb * ((hx - pltpu.roll(hx, 1, 1)) - (hz - pltpu.roll(hz, 1, 0)))
            ez = ca * s[2, j] + cb * (((hy - pltpu.roll(hy, 1, 0)) - (hx - s[3, j - 1])) - s[7, j] * wave)
            s[0, j] = ex
            s[1, j] = ey
            s[2, j] = ez
            p = j - W
            if 0 <= p < CY:
                own_z_lanes = slice(0, 2 * LANES)
                ex, ey, ez = ex[:, own_z_lanes], ey[:, own_z_lanes], ez[:, own_z_lanes]
                now = sig[:, own_z_lanes] * (ex * ex + ey * ey + ez * ez)
                power[p] = now if step == 0 else power[p] + now

        magnetic(step)
        for j in range(step + 1, NY - 1 - step):
            magnetic(j)
            electric(j)

    rows = []
    for t in range(TY):
        halves = []
        for k in range(2):
            pair[...] = power[2 * t, :, lanes(k)] + power[2 * t + 1, :, lanes(k)]
            halves.append(pair[pl.ds(PAD, TX, stride=2), :] + pair[pl.ds(PAD + 1, TX, stride=2), :])
        rows.append(jnp.concatenate(halves, axis=1))
    stacked = jnp.concatenate(rows, axis=0)
    source = lax.broadcasted_iota(jnp.int32, (2 * LANES, LANES), 0)
    target = lax.broadcasted_iota(jnp.int32, (2 * LANES, LANES), 1)
    gather = (source // 2 == target).astype(F32)
    summed = jnp.dot(stacked, gather, precision=lax.Precision.HIGHEST, preferred_element_type=F32)
    out[...] = (summed * (1.0 / (8.0 * ITERS))).reshape(TY, TX, LANES)


def beside_z(t):
    wide = lane_ids(t.shape)
    span = t.shape[1]
    ahead = jnp.where(wide == span - 1, 0.0, pltpu.roll(t, span - 1, 1))
    behind = jnp.where(wide == 0, 0.0, pltpu.roll(t, 1, 1))
    return ahead + behind


def beside_x(t, before, after):
    rows = t.shape[0]
    x = lax.broadcasted_iota(jnp.int32, t.shape, 0)
    ahead = jnp.where(x == rows - 1, after, pltpu.roll(t, rows - 1, 0))
    behind = jnp.where(x == 0, before, pltpu.roll(t, 1, 0))
    return ahead + behind


def densified(packing, warmth):
    return packing + 0.3 * (1.0 - packing) * jnp.exp(-3.0 / (1.0 + warmth))


def warm_kernel(warmth, packing, from_below, from_above, z_a, z_b, from_low, from_high, base, packed):
    odd, me = parity(), lax.axis_index("gz")
    tiles = packing.shape[2] // LANES
    t, p, sides, before, after = [], [], [], [], []
    for k in range(tiles):
        near, far = pl.ds(CX * CY + k * TX, TX), pl.ds(CX * W + k * TX, TX)
        low = jnp.where(odd == 1, z_b[far, :], z_a[far, :])
        high = jnp.where(odd == 1, z_a[far, :], z_b[far, :])
        low = jnp.where(me == 0, low, from_below[near, :])
        high = jnp.where(me == lax.axis_size("gz") - 1, high, from_above[near, :])
        sides.append(low + high)
        before.append(from_low[pl.ds(LOW_ROWS + k, 1), :])
        after.append(from_high[pl.ds(HIGH_ROWS + k, 1), :])
        t.append(warmth[pl.ds(k * TX, TX), :])
        p.append(packing[:, 0, pl.ds(k * LANES, LANES)])
    t, p, sides, before, after = (jnp.concatenate(parts, axis=1) for parts in (t, p, sides, before, after))
    lap = beside_x(t, before, after) + sides + beside_z(t) - 6.0 * t
    base[...] = t + 0.1 * ((0.2 + p) * lap)
    packed[...] = densified(p, t)


def first_kernel(base, packed, heat, warmth, density, first, last):
    power = jnp.concatenate([heat[k] for k in range(heat.shape[0])], axis=1)
    t = base[...] + power
    warmth[...] = t
    first[...] = t[:1]
    last[...] = t[TX - 1 :]
    dense = densified(packed[...], t)
    for k in range(heat.shape[0]):
        here = slice(k * LANES, (k + 1) * LANES)
        density[:, 0, here] = dense[:, here]


def second_kernel(warmth, packed, heat, side_a, side_b, before, after, out):
    t = warmth[...]
    lap = beside_x(t, before[...], after[...]) + side_a[...] + side_b[...] + beside_z(t) - 6.0 * t
    grown = t + 0.1 * ((0.2 + packed[...]) * lap)
    for k in range(heat.shape[0]):
        here = slice(k * LANES, (k + 1) * LANES)
        out[:, 0, here] = grown[:, here] + heat[k]


def tile_rows(a):
    lead = a.shape[:-3]
    a = a.reshape(lead + (CX, CY, 2, LANES))
    return jnp.swapaxes(a, -3, -2).reshape(lead + (2 * CX * CY, LANES))


def local(e, h, phase, spots, warmth, packing):
    n_y, n_z, n_x = lax.axis_size("gy"), lax.axis_size("gz"), lax.axis_size("gx")
    across, within = swaps(n_y, 1), swaps(n_y, 0)
    span = warmth.shape[2]
    pencil_rows = TX * span // LANES

    own, to_a, to_b, shared = call(
        pack_kernel,
        (f32(TILES, CY, CX, LANES), f32(Y_TOTAL, CX, LANES), f32(Y_TOTAL, CX, LANES), f32(CX * CY + pencil_rows, LANES)),
        [HBM] * 5,
        scratch=[
            pltpu.SMEM(spots.shape, jnp.int32),
            pltpu.VMEM((3, 2 * CX * CY, LANES), F32),
            pltpu.VMEM((3, 2 * CX * CY, LANES), F32),
            pltpu.VMEM((2 * CX * CY, LANES), jnp.int32),
            pltpu.VMEM(warmth.shape, F32),
            pltpu.SemaphoreType.DMA((9,)),
        ],
        limit=60,
    )(spots, tile_rows(e), tile_rows(h), tile_rows(phase), warmth)
    in_a = lax.ppermute(to_a, "gy", across)
    in_b = lax.ppermute(to_b, "gy", within)
    from_below = lax.ppermute(shared, "gz", [(i, (i + 1) % n_z) for i in range(n_z)])
    from_above = lax.ppermute(shared, "gz", [(i, (i - 1) % n_z) for i in range(n_z)])
    edge = f32(CX * W + pencil_rows, LANES)
    own_z, z_a, z_b = call(edge_kernel, (f32(CY, CX, LANES), edge, edge), [VMEM] * 2)(from_below, from_above)
    z_a = lax.ppermute(z_a, "gy", across)
    z_b = lax.ppermute(z_b, "gy", within)

    def block(rows):
        rows += span // LANES
        return f32(rows + (-rows) % 8, LANES)

    pencil_tiles = shared[CX * CY :]
    to_up, to_down = call(side_kernel, (block(LOW_ROWS), block(HIGH_ROWS)), [VMEM] * 7)(
        own, own_z, in_a, in_b, z_a, z_b, pencil_tiles
    )
    from_low = lax.ppermute(to_up, "gx", shifts(n_x, 1))
    from_high = lax.ppermute(to_down, "gx", shifts(n_x, -1))
    heat = call(
        field_kernel,
        f32(TY, TX, LANES),
        [VMEM] * 8,
        scratch=[
            pltpu.VMEM((FIELDS, NY, NX, 3 * LANES), F32),
            pltpu.VMEM((NY, NX, LANES), F32),
            pltpu.VMEM((3, NY, NX, 3 * LANES), F32),
            pltpu.VMEM((2, NX, 3 * LANES), F32),
            pltpu.VMEM((CY, NX, 2 * LANES), F32),
            pltpu.VMEM((NX, LANES), F32),
        ],
    )(own, own_z, in_a, in_b, z_a, z_b, from_low, from_high)
    heat = lax.all_to_all(heat, "gz", split_axis=0, concat_axis=0, tiled=True)
    pencil, tall, line = f32(TX, span), f32(TX, 1, span), f32(1, span)
    base, packed = call(warm_kernel, (pencil, pencil), [VMEM] * 8)(
        pencil_tiles, packing, from_below, from_above, z_a, z_b, from_low, from_high
    )
    t, density, first, last = call(first_kernel, (pencil, tall, line, line), [VMEM] * 3)(base, packed, heat)
    pencils = n_y * n_z
    side_a = lax.ppermute(t, ("gy", "gz"), swaps(pencils, 1))
    side_b = lax.ppermute(t, ("gy", "gz"), swaps(pencils, 0))
    before = lax.ppermute(last, "gx", shifts(n_x, 1))
    after = lax.ppermute(first, "gx", shifts(n_x, -1))
    result = call(second_kernel, tall, [VMEM] * 7)(t, packed, heat, side_a, side_b, before, after)
    return result, density


def solution(mesh):
    return jax.shard_map(
        local,
        mesh=mesh,
        in_specs=(
            P(None, "gx", "gy", "gz"),
            P(None, "gx", "gy", "gz"),
            P("gx", "gy", "gz"),
            P(("gx", "gy", "gz"), None),
            P("gx", ("gy", "gz"), None),
            P("gx", ("gy", "gz"), None),
        ),
        out_specs=(P("gx", ("gy", "gz"), None), P("gx", ("gy", "gz"), None)),
        check_vma=False,
    )
```

time: 112 us -> 99.2 us (0.89)
  starting transfers between devices: 73.3 us -> 60.8 us
  waiting for transfers between devices: 19.3 us -> 23.5 us
  local copies, waits for them, and re-layouts: 4.81 us -> 1.94 us
  Pallas kernels: 12.9 us -> 11.5 us
    ppermute x10 -> x6, starting transfers between devices: 38.8 us -> 26 us  [the longest x1 14.2 us: local(): side_a = lax.ppermute(t, ('gy', 'gz'), swaps(pencils, 1))]
    ppermute x1, waiting for transfers between devices: 0.01 us -> 7.44 us  [local(): from_high = lax.ppermute(to_down, 'gx', shifts(n_x, -1))]
    ppermute x10 -> x6, waiting for transfers between devices: 9.74 us -> 4.81 us  [the longest x1 3.02 us: local(): after = lax.ppermute(first, 'gx', shifts(n_x, -1))]
    unnamed x16 -> x4, local copies, waits for them, and re-layouts: 4.81 us -> 1.22 us
    all_to_all x1, waiting for transfers between devices: 0.01 us -> 2.34 us  [local(): heat = lax.all_to_all(heat, 'gz', split_axis=0, concat_axis=0, tiled=True)]
    pallas_call x7, Pallas kernels: 12.9 us -> 11.5 us  [the longest x1 6.95 us: local(): call(field_kernel, f32(TY, TX, LANES), [VMEM] * 8, scratch=[pltpu.VMEM((F...]
  transfers between devices with their start and end apart: 17 -> 13, of which waited for: 5 -> 6; matrix products, arithmetic and copies ran while one was open for 1% -> 1% of each run, Pallas kernels for 10% -> 0%
where the time goes in v2:
time: 99.2 us; the launch traced here: 98.6 us
  starting transfers between devices  60.8 us (61%)
  waiting for transfers between devices  23.5 us (24%)
  Pallas kernels  11.5 us (12%)
  local copies, waits for them, and re-layouts  1.94 us (2%)
    ppermute x1, starting transfers between devices, local(): in_a = lax.ppermute(to_a, 'gy', across)  15.9 us
    ppermute x1, starting transfers between devices, local(): side_a = lax.ppermute(t, ('gy', 'gz'), swaps(pencils, 1))  14.2 us
    ppermute x1, waiting for transfers between devices, local(): z_a = lax.ppermute(z_a, 'gy', across)  8.94 us
    ppermute x1, waiting for transfers between devices, local(): from_high = lax.ppermute(to_down, 'gx', shifts(n_x, -1))  7.44 us
    pallas_call x1, Pallas kernels, local(): call(field_kernel, f32(TY, TX, LANES), [VMEM] * 8, scratch=[pltpu.VMEM((F...  6.95 us
    all_to_all x1, starting transfers between devices, local(): heat = lax.all_to_all(heat, 'gz', split_axis=0, concat_axis=0, tiled=True)  6.27 us
    ppermute x1, starting transfers between devices, local(): z_a = lax.ppermute(z_a, 'gy', across)  4.64 us
    ppermute x1, starting transfers between devices, local(): lax.ppermute(shared, 'gz', [(i, (i + 1) % n_z) for i in range(n_z)])  4.12 us
  transfers between devices with their start and end apart: 13, of which 6 were waited for; matrix products, arithmetic and copies ran while one was open for 1% of the time, Pallas kernels for 0%

profile of v2, /device:TPU:31, one launch (start us, length us, event | category | flops | bytes accessed | tf_op | source)
XLA Modules:
  0.0 98.6 jit_solution(16669795763383909112)
XLA Ops:
  0.6 3.0 %shard_map.77 = (f32[16,8,16,128]{3,2,1,0:T(8,128)}, f32[58,16,128]{2,1,0:T(8,128)}, f32[58,16,128]{2,1,0:T(8,128)}, f32[160,128]{1,0:T(8,128)}) custom-call(s32[1,16]{1,0:T(1,128)} %spots_hbm.1, f32[3,256,128]{2,1,0:T(8,128)} %bitcast.15, f32[3,256,128]{2,1,0:T(8,128)} %bitcast.16, s32[256,128]{1,0:T(8,128)} %bitcast.17, f32[8,1,512]{2,1,0:T(1,128)} %t_hbm.1), custom_call_target="tpu_custom_call" | custom-call | tf_op jit(solution)/shard_map/pallas_call | solution.py:410
  3.7 15.9 %collective-permute-start.4 = (f32[58,16,128]{2,1,0:T(8,128)}, f32[58,16,128]{2,1,0:T(8,128)S(1)}, u32[]{:S(2)}, u32[]{:S(2)}) collective-permute-start(f32[58,16,128]{2,1,0:T(8,128)} %get-tuple-element.22), channel_id=1, source_target_pairs={{4,8},{12,16},{20,24},{28,32},{36,40},{44,48},{52,56},{8,4},{16,12... | collective-permute-start | bytes 1425416 | tf_op jit(solution)/shard_map/ppermute | solution.py:424
  19.6 1.9 %collective-permute-start.5 = (f32[58,16,128]{2,1,0:T(8,128)}, f32[58,16,128]{2,1,0:T(8,128)S(1)}, u32[]{:S(2)}, u32[]{:S(2)}) collective-permute-start(f32[58,16,128]{2,1,0:T(8,128)} %get-tuple-element.23), channel_id=1, source_target_pairs={{0,4},{8,12},{16,20},{24,28},{32,36},{40,44},{48,52},{56,60},{4,0}... | collective-permute-start | bytes 1425416 | tf_op jit(solution)/shard_map/ppermute | solution.py:425
  21.5 2.4 %collective-permute-start.1 = (f32[160,128]{1,0:T(8,128)}, f32[160,128]{1,0:T(8,128)S(1)}, u32[]{:S(2)}, u32[]{:S(2)}) collective-permute-start(f32[160,128]{1,0:T(8,128)} %get-tuple-element.17), channel_id=1, source_target_pairs={{0,3},{1,0},{2,1},{3,2},{4,7},{5,4},{6,5},{7,6},{8,11},{9,8},{10,9... | collective-permute-start | bytes 245768 | tf_op jit(solution)/shard_map/ppermute | solution.py:427
  23.9 4.1 %collective-permute-start = (f32[160,128]{1,0:T(8,128)}, f32[160,128]{1,0:T(8,128)S(1)}, u32[]{:S(2)}, u32[]{:S(2)}) collective-permute-start(f32[160,128]{1,0:T(8,128)} %get-tuple-element.17), channel_id=1, source_target_pairs={{0,1},{1,2},{2,3},{3,0},{4,5},{5,6},{6,7},{7,4},{8,9},{9,10},{10,1... | collective-permute-start | bytes 245768 | tf_op jit(solution)/shard_map/ppermute | solution.py:426
  28.0 0.1 collective-permute-done.1.from_above
  28.1 1.7 %collective-permute-done.from_below = f32[160,128]{1,0:T(8,128)S(1)} collective-permute-done((f32[160,128]{1,0:T(8,128)}, f32[160,128]{1,0:T(8,128)S(1)}, u32[]{:S(2)}, u32[]{:S(2)}) %collective-permute-start) | collective-permute-done | bytes 81952 | tf_op jit(solution)/shard_map/ppermute | solution.py:426
  29.8 4.6 %collective-permute-start.2 = (f32[96,128]{1,0:T(8,128)S(1)}, f32[96,128]{1,0:T(8,128)S(1)}, u32[]{:S(2)}, u32[]{:S(2)}) collective-permute-start(f32[96,128]{1,0:T(8,128)S(1)} %get-tuple-element.18), channel_id=1, source_target_pairs={{4,8},{12,16},{20,24},{28,32},{36,40},{44,48},{52,56},{8,4},{16,12... | collective-permute-start | bytes 147464 | tf_op jit(solution)/shard_map/ppermute | solution.py:430
  34.5 1.9 %collective-permute-start.3 = (f32[96,128]{1,0:T(8,128)S(1)}, f32[96,128]{1,0:T(8,128)S(1)}, u32[]{:S(2)}, u32[]{:S(2)}) collective-permute-start(f32[96,128]{1,0:T(8,128)S(1)} %get-tuple-element.19), channel_id=1, source_target_pairs={{0,4},{8,12},{16,20},{24,28},{32,36},{40,44},{48,52},{56,60},{4,0}... | collective-permute-start | bytes 147464 | tf_op jit(solution)/shard_map/ppermute | solution.py:431
  36.4 0.7 slice.3.warmth
  37.1 8.9 %collective-permute-done.2.z_a = f32[96,128]{1,0:T(8,128)S(1)} collective-permute-done((f32[96,128]{1,0:T(8,128)S(1)}, f32[96,128]{1,0:T(8,128)S(1)}, u32[]{:S(2)}, u32[]{:S(2)}) %collective-permute-start.2) | collective-permute-done | bytes 49184 | tf_op jit(solution)/shard_map/ppermute | solution.py:430
  46.1 0.0 collective-permute-done.4.in_a
  46.1 0.0 collective-permute-done.5.in_b
  46.1 1.2 %copy-done = f32[16,8,16,128]{3,2,1,0:T(8,128)S(1)} copy-done((f32[16,8,16,128]{3,2,1,0:T(8,128)S(1)}, f32[16,8,16,128]{3,2,1,0:T(8,128)}, u32[]{:S(2)}) %copy-start) | copy-done | bytes 1048600
  47.3 0.1 shard_map.79
  47.4 2.8 %collective-permute-start.6 = (f32[856,128]{1,0:T(8,128)S(1)}, f32[856,128]{1,0:T(8,128)S(1)}, u32[]{:S(2)}, u32[]{:S(2)}) collective-permute-start(f32[856,128]{1,0:T(8,128)S(1)} %get-tuple-element.24), channel_id=1, source_target_pairs={{0,64},{64,128},{128,192},{192,256},{256,320},{320,384},{384,448},... | collective-permute-start | bytes 1314824 | tf_op jit(solution)/shard_map/ppermute | solution.py:441
  50.3 1.3 %collective-permute-start.7 = (f32[808,128]{1,0:T(8,128)S(1)}, f32[808,128]{1,0:T(8,128)S(1)}, u32[]{:S(2)}, u32[]{:S(2)}) collective-permute-start(f32[808,128]{1,0:T(8,128)S(1)} %get-tuple-element.25), channel_id=1, source_target_pairs={{64,0},{128,64},{192,128},{256,192},{320,256},{384,320},{448,384},... | collective-permute-start | bytes 1241096 | tf_op jit(solution)/shard_map/ppermute | solution.py:442
  51.6 7.4 %collective-permute-done.7.from_high = f32[808,128]{1,0:T(8,128)S(1)} collective-permute-done((f32[808,128]{1,0:T(8,128)S(1)}, f32[808,128]{1,0:T(8,128)S(1)}, u32[]{:S(2)}, u32[]{:S(2)}) %collective-permute-start.7) | collective-permute-done | bytes 413728 | tf_op jit(solution)/shard_map/ppermute | solution.py:442
  59.0 0.0 collective-permute-done.6.from_low
  59.0 6.9 %shard_map.81 = f32[4,8,128]{2,1,0:T(8,128)} custom-call(f32[16,8,16,128]{3,2,1,0:T(8,128)S(1)} %copy-done, f32[8,16,128]{2,1,0:T(8,128)S(1)} %get-tuple-element.21.own_z, f32[58,16,128]{2,1,0:T(8,128)S(1)} %collective-permute-done.4.in_a, f32[58,16,128]{2,1,0:T(8,128)S(1)} %collective-permute-done.5.in_b, f32[96,128]{1,0:T(8,128)S(1)} %collective-permute-done.2.z_a, ...), custom_call_target="tpu_custom_call" | custom-call | tf_op jit(solution)/shard_map/pallas_call | solution.py:443
  66.0 6.3 %all-to-all-start = ((f32[4,8,128]{2,1,0:T(8,128)}), f32[4,8,128]{2,1,0:T(8,128)S(1)}, u32[]{:S(2)}, u32[]{:S(2)}) async-start(f32[4,8,128]{2,1,0:T(8,128)} %shard_map.81), calls=%async_computation | async-start | bytes 32768 | tf_op jit(solution)/shard_map/all_to_all | solution.py:456
  72.3 0.1 shard_map.80
  72.3 2.3 %all-to-all-done.heat = f32[4,8,128]{2,1,0:T(8,128)S(1)} async-done(((f32[4,8,128]{2,1,0:T(8,128)}), f32[4,8,128]{2,1,0:T(8,128)S(1)}, u32[]{:S(2)}, u32[]{:S(2)}) %all-to-all-start) | async-done | bytes 16416 | tf_op jit(solution)/shard_map/all_to_all | solution.py:456
  74.7 0.6 shard_map.82
  75.3 2.4 %collective-permute-start.9 = (f32[8,512]{1,0:T(8,128)S(1)}, f32[8,512]{1,0:T(8,128)S(1)}, u32[]{:S(2)}, u32[]{:S(2)}) collective-permute-start(f32[8,512]{1,0:T(8,128)S(1)} %get-tuple-element.28.warmth), channel_id=1, source_target_pairs={{0,1},{2,3},{4,5},{6,7},{8,9},{10,11},{12,13},{14,15},{16,17},{18,... | collective-permute-start | bytes 49160 | tf_op jit(solution)/shard_map/ppermute | solution.py:464
  77.7 14.2 %collective-permute-start.8 = (f32[8,512]{1,0:T(8,128)S(1)}, f32[8,512]{1,0:T(8,128)S(1)}, u32[]{:S(2)}, u32[]{:S(2)}) collective-permute-start(f32[8,512]{1,0:T(8,128)S(1)} %get-tuple-element.28.warmth), channel_id=1, source_target_pairs={{1,2},{3,4},{5,6},{7,8},{9,10},{11,12},{13,14},{15,16},{17,18},{19... | collective-permute-start | bytes 49160 | tf_op jit(solution)/shard_map/ppermute | solution.py:463
  92.0 1.6 %collective-permute-start.10 = (f32[1,512]{1,0:T(1,128)S(1)}, f32[1,512]{1,0:T(1,128)S(1)}, u32[]{:S(2)}, u32[]{:S(2)}) collective-permute-start(f32[1,512]{1,0:T(1,128)S(1)} %get-tuple-element.29), channel_id=1, source_target_pairs={{0,64},{64,128},{128,192},{192,256},{256,320},{320,384},{384,448},... | collective-permute-start | bytes 6152 | tf_op jit(solution)/shard_map/ppermute | solution.py:465
  93.6 1.3 %collective-permute-start.11 = (f32[1,512]{1,0:T(1,128)S(1)}, f32[1,512]{1,0:T(1,128)S(1)}, u32[]{:S(2)}, u32[]{:S(2)}) collective-permute-start(f32[1,512]{1,0:T(1,128)S(1)} %get-tuple-element.30), channel_id=1, source_target_pairs={{64,0},{128,64},{192,128},{256,192},{320,256},{384,320},{448,384},... | collective-permute-start | bytes 6152 | tf_op jit(solution)/shard_map/ppermute | solution.py:466
  94.9 0.0 collective-permute-done.10.before
  94.9 3.0 %collective-permute-done.11.after = f32[1,512]{1,0:T(1,128)S(1)} collective-permute-done((f32[1,512]{1,0:T(1,128)S(1)}, f32[1,512]{1,0:T(1,128)S(1)}, u32[]{:S(2)}, u32[]{:S(2)}) %collective-permute-start.11) | collective-permute-done | bytes 2080 | tf_op jit(solution)/shard_map/ppermute | solution.py:466
  97.9 0.0 collective-permute-done.9.side_b
  97.9 0.7 shard_map.83
  (6 shorter events, 0.0 us)
Async XLA Ops:
  3.7 42.4 %collective-permute-start.4 = (f32[58,16,128]{2,1,0:T(8,128)}, f32[58,16,128]{2,1,0:T(8,128)S(1)}, u32[]{:S(2)}, u32[]{:S(2)}) collective-permute-start(f32[58,16,128]{2,1,0:T(8,128)} %get-tuple-element.22), channel_id=1, source_target_pairs={{4,8},{12,16},{20,24},{28,32},{36,40},{44,48},{52,56},{8,4},{16,12... | collective-permute-start | bytes 1425416 | tf_op jit(solution)/shard_map/ppermute | solution.py:424
  19.6 26.5 %collective-permute-start.5 = (f32[58,16,128]{2,1,0:T(8,128)}, f32[58,16,128]{2,1,0:T(8,128)S(1)}, u32[]{:S(2)}, u32[]{:S(2)}) collective-permute-start(f32[58,16,128]{2,1,0:T(8,128)} %get-tuple-element.23), channel_id=1, source_target_pairs={{0,4},{8,12},{16,20},{24,28},{32,36},{40,44},{48,52},{56,60},{4,0}... | collective-permute-start | bytes 1425416 | tf_op jit(solution)/shard_map/ppermute | solution.py:425
  21.5 6.6 %collective-permute-start.1 = (f32[160,128]{1,0:T(8,128)}, f32[160,128]{1,0:T(8,128)S(1)}, u32[]{:S(2)}, u32[]{:S(2)}) collective-permute-start(f32[160,128]{1,0:T(8,128)} %get-tuple-element.17), channel_id=1, source_target_pairs={{0,3},{1,0},{2,1},{3,2},{4,7},{5,4},{6,5},{7,6},{8,11},{9,8},{10,9... | collective-permute-start | bytes 245768 | tf_op jit(solution)/shard_map/ppermute | solution.py:427
  23.9 5.9 %collective-permute-start = (f32[160,128]{1,0:T(8,128)}, f32[160,128]{1,0:T(8,128)S(1)}, u32[]{:S(2)}, u32[]{:S(2)}) collective-permute-start(f32[160,128]{1,0:T(8,128)} %get-tuple-element.17), channel_id=1, source_target_pairs={{0,1},{1,2},{2,3},{3,0},{4,5},{5,6},{6,7},{7,4},{8,9},{9,10},{10,1... | collective-permute-start | bytes 245768 | tf_op jit(solution)/shard_map/ppermute | solution.py:426
  29.8 16.2 %collective-permute-start.2 = (f32[96,128]{1,0:T(8,128)S(1)}, f32[96,128]{1,0:T(8,128)S(1)}, u32[]{:S(2)}, u32[]{:S(2)}) collective-permute-start(f32[96,128]{1,0:T(8,128)S(1)} %get-tuple-element.18), channel_id=1, source_target_pairs={{4,8},{12,16},{20,24},{28,32},{36,40},{44,48},{52,56},{8,4},{16,12... | collective-permute-start | bytes 147464 | tf_op jit(solution)/shard_map/ppermute | solution.py:430
  34.5 11.6 %collective-permute-start.3 = (f32[96,128]{1,0:T(8,128)S(1)}, f32[96,128]{1,0:T(8,128)S(1)}, u32[]{:S(2)}, u32[]{:S(2)}) collective-permute-start(f32[96,128]{1,0:T(8,128)S(1)} %get-tuple-element.19), channel_id=1, source_target_pairs={{0,4},{8,12},{16,20},{24,28},{32,36},{40,44},{48,52},{56,60},{4,0}... | collective-permute-start | bytes 147464 | tf_op jit(solution)/shard_map/ppermute | solution.py:431
  46.1 1.2 %copy-start = (f32[16,8,16,128]{3,2,1,0:T(8,128)S(1)}, f32[16,8,16,128]{3,2,1,0:T(8,128)}, u32[]{:S(2)}) copy-start(f32[16,8,16,128]{3,2,1,0:T(8,128)} %get-tuple-element.20.own) | copy-start | bytes 3145732
  47.4 11.6 %collective-permute-start.6 = (f32[856,128]{1,0:T(8,128)S(1)}, f32[856,128]{1,0:T(8,128)S(1)}, u32[]{:S(2)}, u32[]{:S(2)}) collective-permute-start(f32[856,128]{1,0:T(8,128)S(1)} %get-tuple-element.24), channel_id=1, source_target_pairs={{0,64},{64,128},{128,192},{192,256},{256,320},{320,384},{384,448},... | collective-permute-start | bytes 1314824 | tf_op jit(solution)/shard_map/ppermute | solution.py:441
  50.3 8.7 %collective-permute-start.7 = (f32[808,128]{1,0:T(8,128)S(1)}, f32[808,128]{1,0:T(8,128)S(1)}, u32[]{:S(2)}, u32[]{:S(2)}) collective-permute-start(f32[808,128]{1,0:T(8,128)S(1)} %get-tuple-element.25), channel_id=1, source_target_pairs={{64,0},{128,64},{192,128},{256,192},{320,256},{384,320},{448,384},... | collective-permute-start | bytes 1241096 | tf_op jit(solution)/shard_map/ppermute | solution.py:442
  66.0 6.3 %copy-start.1 = (f32[8,1,512]{2,1,0:T(1,128)S(1)}, f32[8,1,512]{2,1,0:T(1,128)}, u32[]{:S(2)}) copy-start(f32[8,1,512]{2,1,0:T(1,128)} %packing.1) | copy-start | bytes 49156
  66.0 8.7 %all-to-all-start = ((f32[4,8,128]{2,1,0:T(8,128)}), f32[4,8,128]{2,1,0:T(8,128)S(1)}, u32[]{:S(2)}, u32[]{:S(2)}) async-start(f32[4,8,128]{2,1,0:T(8,128)} %shard_map.81), calls=%async_computation | async-start | bytes 32768 | tf_op jit(solution)/shard_map/all_to_all | solution.py:456
  75.3 22.6 %collective-permute-start.9 = (f32[8,512]{1,0:T(8,128)S(1)}, f32[8,512]{1,0:T(8,128)S(1)}, u32[]{:S(2)}, u32[]{:S(2)}) collective-permute-start(f32[8,512]{1,0:T(8,128)S(1)} %get-tuple-element.28.warmth), channel_id=1, source_target_pairs={{0,1},{2,3},{4,5},{6,7},{8,9},{10,11},{12,13},{14,15},{16,17},{18,... | collective-permute-start | bytes 49160 | tf_op jit(solution)/shard_map/ppermute | solution.py:464
  77.7 20.2 %collective-permute-start.8 = (f32[8,512]{1,0:T(8,128)S(1)}, f32[8,512]{1,0:T(8,128)S(1)}, u32[]{:S(2)}, u32[]{:S(2)}) collective-permute-start(f32[8,512]{1,0:T(8,128)S(1)} %get-tuple-element.28.warmth), channel_id=1, source_target_pairs={{1,2},{3,4},{5,6},{7,8},{9,10},{11,12},{13,14},{15,16},{17,18},{19... | collective-permute-start | bytes 49160 | tf_op jit(solution)/shard_map/ppermute | solution.py:463
  92.0 2.9 %collective-permute-start.10 = (f32[1,512]{1,0:T(1,128)S(1)}, f32[1,512]{1,0:T(1,128)S(1)}, u32[]{:S(2)}, u32[]{:S(2)}) collective-permute-start(f32[1,512]{1,0:T(1,128)S(1)} %get-tuple-element.29), channel_id=1, source_target_pairs={{0,64},{64,128},{128,192},{192,256},{256,320},{320,384},{384,448},... | collective-permute-start | bytes 6152 | tf_op jit(solution)/shard_map/ppermute | solution.py:465
  93.6 4.3 %collective-permute-start.11 = (f32[1,512]{1,0:T(1,128)S(1)}, f32[1,512]{1,0:T(1,128)S(1)}, u32[]{:S(2)}, u32[]{:S(2)}) collective-permute-start(f32[1,512]{1,0:T(1,128)S(1)} %get-tuple-element.30), channel_id=1, source_target_pairs={{64,0},{128,64},{192,128},{256,192},{320,256},{384,320},{448,384},... | collective-permute-start | bytes 6152 | tf_op jit(solution)/shard_map/ppermute | solution.py:466

commit v3 on v2

--- a/solution.py
+++ b/solution.py
@@ -165,33 +165,38 @@
         out[pl.ds(CX * W, thermal.size), :] = jnp.where(up == 1, below, above)
 
 
-def side_kernel(own, own_z, in_a, in_b, z_a, z_b, warmth, out_up, out_down):
-    odd = parity()
-
-    def move(k, j, read):
-        for out, table, up in ((out_up, LOW_TABLE, True), (out_down, HIGH_TABLE, False)):
-            start, count = table[k, j]
-            if count:
-                rows = read()
-                out[pl.ds(start, count), :] = rows[CX - count :] if up else rows[:count]
-
-    for y in range(CY):
-        for k in range(TILES):
-            move(k, W + y, lambda: own[k, y])
-        move(TILES, W + y, lambda: own_z[y])
+def moved(out, table, up, k, j, rows):
+    start, count = table[k, j]
+    if count:
+        out[pl.ds(start, count), :] = rows[CX - count :] if up else rows[:count]
+
+
+def middle_kernel(own, own_z, warmth, out_up, out_down):
+    for out, table, up in ((out_up, LOW_TABLE, True), (out_down, HIGH_TABLE, False)):
+        for k in range(TILES + 1):
+            for y in range(CY):
+                moved(out, table, up, k, W + y, own_z[y] if k == TILES else own[k, y])
     for k in range(warmth.shape[0] // TX):
         out_up[pl.ds(LOW_ROWS + k, 1), :] = warmth[pl.ds(k * TX + TX - 1, 1), :]
         out_down[pl.ds(HIGH_ROWS + k, 1), :] = warmth[pl.ds(k * TX, 1), :]
 
+
+def side_kernel(mid_up, mid_down, in_a, in_b, z_a, z_b, out_up, out_down):
+    odd = parity()
+    out_up[...] = mid_up[...]
+    out_down[...] = mid_down[...]
+
     def outside(low, high, z_low, z_high):
-        for k in range(TILES):
-            planes = Y_PLANES[k // 2]
-            for i in range(planes):
-                move(k, W - planes + i, lambda: low[Y_START[k] + i])
-                move(k, W + CY + i, lambda: high[Y_START[k] + i])
-        for i in range(W):
-            move(TILES, i, lambda: z_low[pl.ds(CX * i, CX), :])
-            move(TILES, W + CY + i, lambda: z_high[pl.ds(CX * i, CX), :])
+        for out, table, up in ((out_up, LOW_TABLE, True), (out_down, HIGH_TABLE, False)):
+            for k in range(TILES):
+                planes = Y_PLANES[k // 2]
+                for i in range(planes):
+                    moved(out, table, up, k, W - planes + i, low[Y_START[k] + i])
+                    moved(out, table, up, k, W + CY + i, high[Y_START[k] + i])
+            for i in range(W):
+                moved(out, table, up, TILES, i, z_low[pl.ds(CX * i, CX), :])
+                moved(out, table, up, TILES, W + CY + i, z_high[pl.ds(CX * i, CX), :])
+
     @pl.when(odd == 1)
     def _():
         outside(in_b, in_a, z_b, z_a)
@@ -201,7 +206,7 @@
         outside(in_a, in_b, z_a, z_b)
 
 
-def field_kernel(own, own_z, in_a, in_b, z_a, z_b, from_low, from_high, out, s, zs, coef, reach, power, pair):
+def field_kernel(own, own_z, in_a, in_b, z_a, z_b, from_low, from_high, base, out, s, zs, coef, reach, power, pair):
     odd = parity()
     span = 3 * LANES
     middle = pl.ds(PAD, CX)
@@ -330,7 +335,12 @@
     target = lax.broadcasted_iota(jnp.int32, (2 * LANES, LANES), 1)
     gather = (source // 2 == target).astype(F32)
     summed = jnp.dot(stacked, gather, precision=lax.Precision.HIGHEST, preferred_element_type=F32)
-    out[...] = (summed * (1.0 / (8.0 * ITERS))).reshape(TY, TX, LANES)
+    summed = summed * (1.0 / (8.0 * ITERS))
+    for d in range(TY):
+        for i, t in enumerate((d - 1, d, d + 1)):
+            out[d, i] = summed[TX * t : TX * (t + 1)] if 0 <= t < TY else jnp.zeros((TX, LANES), F32)
+        for k in range(base.shape[1] // LANES):
+            out[d, 3 + k] = base[:, pl.ds(k * LANES, LANES)]
 
 
 def beside_z(t):
@@ -374,25 +384,37 @@
     packed[...] = densified(p, t)
 
 
-def first_kernel(base, packed, heat, warmth, density, first, last):
-    power = jnp.concatenate([heat[k] for k in range(heat.shape[0])], axis=1)
-    t = base[...] + power
-    warmth[...] = t
-    first[...] = t[:1]
-    last[...] = t[TX - 1 :]
-    dense = densified(packed[...], t)
-    for k in range(heat.shape[0]):
+def first_kernel(base, heat, warmth, beside, first, last):
+    me = lax.axis_index("gz")
+    tiles = heat.shape[0]
+    has_low = (me > 0).astype(F32)
+    has_high = (me < tiles - 1).astype(F32)
+    low, high = jnp.maximum(me - 1, 0), jnp.minimum(me + 1, tiles - 1)
+    for k in range(tiles):
+        lanes = pl.ds(k * LANES, LANES)
+        t = base[:, lanes] + heat[k, 1]
+        warmth[:, lanes] = t
+        first[:, lanes] = t[:1]
+        last[:, lanes] = t[TX - 1 :]
+        below = (heat[low, 3 + k] + heat[k, 0]) * has_low
+        above = (heat[high, 3 + k] + heat[k, 2]) * has_high
+        beside[:, lanes] = below + above
+
+
+def dense_kernel(packed, warmth, density):
+    dense = densified(packed[...], warmth[...])
+    for k in range(dense.shape[1] // LANES):
         here = slice(k * LANES, (k + 1) * LANES)
         density[:, 0, here] = dense[:, here]
 
 
-def second_kernel(warmth, packed, heat, side_a, side_b, before, after, out):
+def second_kernel(warmth, packed, heat, beside, across, before, after, out):
     t = warmth[...]
-    lap = beside_x(t, before[...], after[...]) + side_a[...] + side_b[...] + beside_z(t) - 6.0 * t
+    lap = beside_x(t, before[...], after[...]) + beside[...] + across[...] + beside_z(t) - 6.0 * t
     grown = t + 0.1 * ((0.2 + packed[...]) * lap)
     for k in range(heat.shape[0]):
         here = slice(k * LANES, (k + 1) * LANES)
-        out[:, 0, here] = grown[:, here] + heat[k]
+        out[:, 0, here] = grown[:, here] + heat[k, 1]
 
 
 def tile_rows(a):
@@ -435,15 +457,19 @@
         return f32(rows + (-rows) % 8, LANES)
 
     pencil_tiles = shared[CX * CY :]
-    to_up, to_down = call(side_kernel, (block(LOW_ROWS), block(HIGH_ROWS)), [VMEM] * 7)(
-        own, own_z, in_a, in_b, z_a, z_b, pencil_tiles
-    )
+    blocks = (block(LOW_ROWS), block(HIGH_ROWS))
+    middle = call(middle_kernel, blocks, [VMEM] * 3)(own, own_z, pencil_tiles)
+    to_up, to_down = call(side_kernel, blocks, [VMEM] * 6)(*middle, in_a, in_b, z_a, z_b)
     from_low = lax.ppermute(to_up, "gx", shifts(n_x, 1))
     from_high = lax.ppermute(to_down, "gx", shifts(n_x, -1))
+    pencil, tall, line = f32(TX, span), f32(TX, 1, span), f32(1, span)
+    base, packed = call(warm_kernel, (pencil, pencil), [VMEM] * 8)(
+        pencil_tiles, packing, from_below, from_above, z_a, z_b, from_low, from_high
+    )
     heat = call(
         field_kernel,
-        f32(TY, TX, LANES),
-        [VMEM] * 8,
+        f32(TY, 3 + span // LANES, TX, LANES),
+        [VMEM] * 9,
         scratch=[
             pltpu.VMEM((FIELDS, NY, NX, 3 * LANES), F32),
             pltpu.VMEM((NY, NX, LANES), F32),
@@ -452,19 +478,15 @@
             pltpu.VMEM((CY, NX, 2 * LANES), F32),
             pltpu.VMEM((NX, LANES), F32),
         ],
-    )(own, own_z, in_a, in_b, z_a, z_b, from_low, from_high)
+    )(own, own_z, in_a, in_b, z_a, z_b, from_low, from_high, base)
     heat = lax.all_to_all(heat, "gz", split_axis=0, concat_axis=0, tiled=True)
-    pencil, tall, line = f32(TX, span), f32(TX, 1, span), f32(1, span)
-    base, packed = call(warm_kernel, (pencil, pencil), [VMEM] * 8)(
-        pencil_tiles, packing, from_below, from_above, z_a, z_b, from_low, from_high
-    )
-    t, density, first, last = call(first_kernel, (pencil, tall, line, line), [VMEM] * 3)(base, packed, heat)
-    pencils = n_y * n_z
-    side_a = lax.ppermute(t, ("gy", "gz"), swaps(pencils, 1))
-    side_b = lax.ppermute(t, ("gy", "gz"), swaps(pencils, 0))
+    t, beside, first, last = call(first_kernel, (pencil, pencil, line, line), [VMEM] * 2)(base, heat)
+    ends = [(i, i + 1) for i in range(n_z - 1, n_y * n_z - 1, n_z)]
+    outer = lax.ppermute(t, ("gy", "gz"), ends + [(j, i) for i, j in ends])
     before = lax.ppermute(last, "gx", shifts(n_x, 1))
     after = lax.ppermute(first, "gx", shifts(n_x, -1))
-    result = call(second_kernel, tall, [VMEM] * 7)(t, packed, heat, side_a, side_b, before, after)
+    density = call(dense_kernel, tall, [VMEM] * 2)(packed, t)
+    result = call(second_kernel, tall, [VMEM] * 7)(t, packed, heat, beside, outer, before, after)
     return result, density
 
 

time: 99.2 us -> 94.6 us (0.954)
  blocking collectives: 0 us -> 8.24 us
  starting transfers between devices: 60.8 us -> 52.9 us
  waiting for transfers between devices: 23.5 us -> 19.3 us
    all_to_all x0 -> x1, blocking collectives: none -> 8.24 us  [local(): heat = lax.all_to_all(heat, 'gz', split_axis=0, concat_axis=0, tiled=True)]
    all_to_all x1 -> x0, starting transfers between devices: 6.27 us -> none  [local(): heat = lax.all_to_all(heat, 'gz', split_axis=0, concat_axis=0, tiled=True)]
    all_to_all x1 -> x0, waiting for transfers between devices: 2.34 us -> none  [local(): heat = lax.all_to_all(heat, 'gz', split_axis=0, concat_axis=0, tiled=True)]
    ppermute x2 -> x1, starting transfers between devices: 16.6 us -> 14.8 us  [local(): outer = lax.ppermute(t, ('gy', 'gz'), ends + [(j, i) for i, j in ends])]
    ppermute x1, waiting for transfers between devices: 8.94 us -> 7.63 us  [local(): z_a = lax.ppermute(z_a, 'gy', across)]
    pallas_call x3 -> x5, Pallas kernels: 7.72 us -> 7.16 us  [the longest x1 6.3 us: local(): call(field_kernel, f32(TY, 3 + span // LANES, TX, LANES), [VMEM] * 9, scr...]
  transfers between devices with their start and end apart: 13 -> 11, of which waited for: 6 -> 5; matrix products, arithmetic and copies ran while one was open for 1% -> 1% of each run, Pallas kernels for 0% -> 1%
where the time goes in v3:
time: 94.6 us; the launch traced here: 94.1 us
  starting transfers between devices  52.9 us (56%)
  waiting for transfers between devices  19.3 us (20%)
  Pallas kernels  11 us (12%)
  blocking collectives  8.24 us (9%)
  local copies, waits for them, and re-layouts  1.96 us (2%)
    ppermute x1, starting transfers between devices, local(): in_a = lax.ppermute(to_a, 'gy', across)  15.9 us
    ppermute x1, starting transfers between devices, local(): outer = lax.ppermute(t, ('gy', 'gz'), ends + [(j, i) for i, j in ends])  14.8 us
    all_to_all x1, blocking collectives, local(): heat = lax.all_to_all(heat, 'gz', split_axis=0, concat_axis=0, tiled=True)  8.24 us
    ppermute x1, waiting for transfers between devices, local(): z_a = lax.ppermute(z_a, 'gy', across)  7.63 us
    ppermute x1, waiting for transfers between devices, local(): from_high = lax.ppermute(to_down, 'gx', shifts(n_x, -1))  7.44 us
    pallas_call x1, Pallas kernels, local(): call(field_kernel, f32(TY, 3 + span // LANES, TX, LANES), [VMEM] * 9, scr...  6.3 us
    ppermute x1, starting transfers between devices, local(): z_a = lax.ppermute(z_a, 'gy', across)  4.64 us
    ppermute x1, starting transfers between devices, local(): lax.ppermute(shared, 'gz', [(i, (i + 1) % n_z) for i in range(n_z)])  4.12 us
  transfers between devices with their start and end apart: 11, of which 5 were waited for; matrix products, arithmetic and copies ran while one was open for 1% of the time, Pallas kernels for 1%

profile of v3, /device:TPU:31, one launch (start us, length us, event | category | flops | bytes accessed | tf_op | source)
XLA Modules:
  0.0 94.1 jit_solution(16529373394161576795)
XLA Ops:
  0.6 3.0 %shard_map.77 = (f32[16,8,16,128]{3,2,1,0:T(8,128)}, f32[58,16,128]{2,1,0:T(8,128)}, f32[58,16,128]{2,1,0:T(8,128)}, f32[160,128]{1,0:T(8,128)}) custom-call(s32[1,16]{1,0:T(1,128)} %spots_hbm.1, f32[3,256,128]{2,1,0:T(8,128)} %bitcast.15, f32[3,256,128]{2,1,0:T(8,128)} %bitcast.16, s32[256,128]{1,0:T(8,128)} %bitcast.17, f32[8,1,512]{2,1,0:T(1,128)} %t_hbm.1), custom_call_target="tpu_custom_call" | custom-call | tf_op jit(solution)/shard_map/pallas_call | solution.py:432
  3.6 15.9 %collective-permute-start.4 = (f32[58,16,128]{2,1,0:T(8,128)}, f32[58,16,128]{2,1,0:T(8,128)S(1)}, u32[]{:S(2)}, u32[]{:S(2)}) collective-permute-start(f32[58,16,128]{2,1,0:T(8,128)} %get-tuple-element.26), channel_id=1, source_target_pairs={{4,8},{12,16},{20,24},{28,32},{36,40},{44,48},{52,56},{8,4},{16,12... | collective-permute-start | bytes 1425416 | tf_op jit(solution)/shard_map/ppermute | solution.py:446
  19.6 1.9 %collective-permute-start.5 = (f32[58,16,128]{2,1,0:T(8,128)}, f32[58,16,128]{2,1,0:T(8,128)S(1)}, u32[]{:S(2)}, u32[]{:S(2)}) collective-permute-start(f32[58,16,128]{2,1,0:T(8,128)} %get-tuple-element.27), channel_id=1, source_target_pairs={{0,4},{8,12},{16,20},{24,28},{32,36},{40,44},{48,52},{56,60},{4,0}... | collective-permute-start | bytes 1425416 | tf_op jit(solution)/shard_map/ppermute | solution.py:447
  21.5 2.4 %collective-permute-start.1 = (f32[160,128]{1,0:T(8,128)}, f32[160,128]{1,0:T(8,128)S(1)}, u32[]{:S(2)}, u32[]{:S(2)}) collective-permute-start(f32[160,128]{1,0:T(8,128)} %get-tuple-element.19), channel_id=1, source_target_pairs={{0,3},{1,0},{2,1},{3,2},{4,7},{5,4},{6,5},{7,6},{8,11},{9,8},{10,9... | collective-permute-start | bytes 245768 | tf_op jit(solution)/shard_map/ppermute | solution.py:449
  23.9 4.1 %collective-permute-start = (f32[160,128]{1,0:T(8,128)}, f32[160,128]{1,0:T(8,128)S(1)}, u32[]{:S(2)}, u32[]{:S(2)}) collective-permute-start(f32[160,128]{1,0:T(8,128)} %get-tuple-element.19), channel_id=1, source_target_pairs={{0,1},{1,2},{2,3},{3,0},{4,5},{5,6},{6,7},{7,4},{8,9},{9,10},{10,1... | collective-permute-start | bytes 245768 | tf_op jit(solution)/shard_map/ppermute | solution.py:448
  28.0 0.1 collective-permute-done.1.from_above
  28.1 1.7 %collective-permute-done.from_below = f32[160,128]{1,0:T(8,128)S(1)} collective-permute-done((f32[160,128]{1,0:T(8,128)}, f32[160,128]{1,0:T(8,128)S(1)}, u32[]{:S(2)}, u32[]{:S(2)}) %collective-permute-start) | collective-permute-done | bytes 81952 | tf_op jit(solution)/shard_map/ppermute | solution.py:448
  29.8 4.6 %collective-permute-start.2 = (f32[96,128]{1,0:T(8,128)S(1)}, f32[96,128]{1,0:T(8,128)S(1)}, u32[]{:S(2)}, u32[]{:S(2)}) collective-permute-start(f32[96,128]{1,0:T(8,128)S(1)} %get-tuple-element.20), channel_id=1, source_target_pairs={{4,8},{12,16},{20,24},{28,32},{36,40},{44,48},{52,56},{8,4},{16,12... | collective-permute-start | bytes 147464 | tf_op jit(solution)/shard_map/ppermute | solution.py:452
  34.4 1.9 %collective-permute-start.3 = (f32[96,128]{1,0:T(8,128)S(1)}, f32[96,128]{1,0:T(8,128)S(1)}, u32[]{:S(2)}, u32[]{:S(2)}) collective-permute-start(f32[96,128]{1,0:T(8,128)S(1)} %get-tuple-element.21), channel_id=1, source_target_pairs={{0,4},{8,12},{16,20},{24,28},{32,36},{40,44},{48,52},{56,60},{4,0}... | collective-permute-start | bytes 147464 | tf_op jit(solution)/shard_map/ppermute | solution.py:453
  36.4 0.7 slice.3.warmth
  37.1 1.2 %copy-done = f32[16,8,16,128]{3,2,1,0:T(8,128)S(1)} copy-done((f32[16,8,16,128]{3,2,1,0:T(8,128)S(1)}, f32[16,8,16,128]{3,2,1,0:T(8,128)}, u32[]{:S(2)}) %copy-start) | copy-done | bytes 1048600
  38.3 0.1 shard_map.79
  38.4 7.6 %collective-permute-done.2.z_a = f32[96,128]{1,0:T(8,128)S(1)} collective-permute-done((f32[96,128]{1,0:T(8,128)S(1)}, f32[96,128]{1,0:T(8,128)S(1)}, u32[]{:S(2)}, u32[]{:S(2)}) %collective-permute-start.2) | collective-permute-done | bytes 49184 | tf_op jit(solution)/shard_map/ppermute | solution.py:452
  46.0 0.0 collective-permute-done.3.z_b
  46.0 0.0 collective-permute-done.4.in_a
  46.0 0.0 collective-permute-done.5.in_b
  46.0 0.0 copy-start.2
  46.1 0.1 shard_map.80
  46.2 3.0 %collective-permute-start.6 = (f32[856,128]{1,0:T(8,128)S(1)}, f32[856,128]{1,0:T(8,128)S(1)}, u32[]{:S(2)}, u32[]{:S(2)}) collective-permute-start(f32[856,128]{1,0:T(8,128)S(1)} %get-tuple-element.28), channel_id=1, source_target_pairs={{0,64},{64,128},{128,192},{192,256},{256,320},{320,384},{384,448},... | collective-permute-start | bytes 1314824 | tf_op jit(solution)/shard_map/ppermute | solution.py:463
  49.2 1.3 %collective-permute-start.7 = (f32[808,128]{1,0:T(8,128)S(1)}, f32[808,128]{1,0:T(8,128)S(1)}, u32[]{:S(2)}, u32[]{:S(2)}) collective-permute-start(f32[808,128]{1,0:T(8,128)S(1)} %get-tuple-element.29), channel_id=1, source_target_pairs={{64,0},{128,64},{192,128},{256,192},{320,256},{384,320},{448,384},... | collective-permute-start | bytes 1241096 | tf_op jit(solution)/shard_map/ppermute | solution.py:464
  50.5 7.4 %collective-permute-done.7.from_high = f32[808,128]{1,0:T(8,128)S(1)} collective-permute-done((f32[808,128]{1,0:T(8,128)S(1)}, f32[808,128]{1,0:T(8,128)S(1)}, u32[]{:S(2)}, u32[]{:S(2)}) %collective-permute-start.7) | collective-permute-done | bytes 413728 | tf_op jit(solution)/shard_map/ppermute | solution.py:464
  57.9 0.1 shard_map.81
  58.0 6.3 %shard_map.82 = f32[4,7,8,128]{3,2,1,0:T(8,128)S(1)} custom-call(f32[16,8,16,128]{3,2,1,0:T(8,128)S(1)} %copy-done.1, f32[8,16,128]{2,1,0:T(8,128)S(1)} %get-tuple-element.23.own_z, f32[58,16,128]{2,1,0:T(8,128)S(1)} %collective-permute-done.4.in_a, f32[58,16,128]{2,1,0:T(8,128)S(1)} %collective-permute-done.5.in_b, ...), custom_call_target="tpu_custom_call" | custom-call | tf_op jit(solution)/shard_map/pallas_call | solution.py:469
  64.3 8.2 %all_to_all.5.heat = f32[4,7,8,128]{3,2,1,0:T(8,128)S(1)} all-to-all(f32[4,7,8,128]{3,2,1,0:T(8,128)S(1)} %shard_map.82), channel_id=1, replica_groups=mesh['gx'=8,'gy'=16,'gz'=4] {'gz'}, dimensions={0} | all-to-all | bytes 229376 | tf_op jit(solution)/shard_map/all_to_all | solution.py:482
  72.6 14.8 %collective-permute-start.8 = (f32[8,512]{1,0:T(8,128)S(1)}, f32[8,512]{1,0:T(8,128)S(1)}, u32[]{:S(2)}, u32[]{:S(2)}) collective-permute-start(f32[8,512]{1,0:T(8,128)S(1)} %get-tuple-element.31.warmth), channel_id=1, source_target_pairs={{3,4},{7,8},{11,12},{15,16},{19,20},{23,24},{27,28},{31,32},{35,36... | collective-permute-start | bytes 49160 | tf_op jit(solution)/shard_map/ppermute | solution.py:485
  87.4 1.6 %collective-permute-start.9 = (f32[1,512]{1,0:T(1,128)S(1)}, f32[1,512]{1,0:T(1,128)S(1)}, u32[]{:S(2)}, u32[]{:S(2)}) collective-permute-start(f32[1,512]{1,0:T(1,128)S(1)} %get-tuple-element.34), channel_id=1, source_target_pairs={{0,64},{64,128},{128,192},{192,256},{256,320},{320,384},{384,448},... | collective-permute-start | bytes 6152 | tf_op jit(solution)/shard_map/ppermute | solution.py:486
  89.0 1.3 %collective-permute-start.10 = (f32[1,512]{1,0:T(1,128)S(1)}, f32[1,512]{1,0:T(1,128)S(1)}, u32[]{:S(2)}, u32[]{:S(2)}) collective-permute-start(f32[1,512]{1,0:T(1,128)S(1)} %get-tuple-element.35), channel_id=1, source_target_pairs={{64,0},{128,64},{192,128},{256,192},{320,256},{384,320},{448,384},... | collective-permute-start | bytes 6152 | tf_op jit(solution)/shard_map/ppermute | solution.py:487
  90.3 0.6 shard_map.85
  91.0 0.0 collective-permute-done.9.before
  91.0 2.4 %collective-permute-done.10.after = f32[1,512]{1,0:T(1,128)S(1)} collective-permute-done((f32[1,512]{1,0:T(1,128)S(1)}, f32[1,512]{1,0:T(1,128)S(1)}, u32[]{:S(2)}, u32[]{:S(2)}) %collective-permute-start.10) | collective-permute-done | bytes 2080 | tf_op jit(solution)/shard_map/ppermute | solution.py:487
  93.4 0.0 collective-permute-done.8.across
  93.4 0.7 shard_map.84
  (7 shorter events, 0.1 us)
Async XLA Ops:
  3.6 42.4 %collective-permute-start.4 = (f32[58,16,128]{2,1,0:T(8,128)}, f32[58,16,128]{2,1,0:T(8,128)S(1)}, u32[]{:S(2)}, u32[]{:S(2)}) collective-permute-start(f32[58,16,128]{2,1,0:T(8,128)} %get-tuple-element.26), channel_id=1, source_target_pairs={{4,8},{12,16},{20,24},{28,32},{36,40},{44,48},{52,56},{8,4},{16,12... | collective-permute-start | bytes 1425416 | tf_op jit(solution)/shard_map/ppermute | solution.py:446
  19.6 26.5 %collective-permute-start.5 = (f32[58,16,128]{2,1,0:T(8,128)}, f32[58,16,128]{2,1,0:T(8,128)S(1)}, u32[]{:S(2)}, u32[]{:S(2)}) collective-permute-start(f32[58,16,128]{2,1,0:T(8,128)} %get-tuple-element.27), channel_id=1, source_target_pairs={{0,4},{8,12},{16,20},{24,28},{32,36},{40,44},{48,52},{56,60},{4,0}... | collective-permute-start | bytes 1425416 | tf_op jit(solution)/shard_map/ppermute | solution.py:447
  21.5 6.6 %collective-permute-start.1 = (f32[160,128]{1,0:T(8,128)}, f32[160,128]{1,0:T(8,128)S(1)}, u32[]{:S(2)}, u32[]{:S(2)}) collective-permute-start(f32[160,128]{1,0:T(8,128)} %get-tuple-element.19), channel_id=1, source_target_pairs={{0,3},{1,0},{2,1},{3,2},{4,7},{5,4},{6,5},{7,6},{8,11},{9,8},{10,9... | collective-permute-start | bytes 245768 | tf_op jit(solution)/shard_map/ppermute | solution.py:449
  23.9 5.9 %collective-permute-start = (f32[160,128]{1,0:T(8,128)}, f32[160,128]{1,0:T(8,128)S(1)}, u32[]{:S(2)}, u32[]{:S(2)}) collective-permute-start(f32[160,128]{1,0:T(8,128)} %get-tuple-element.19), channel_id=1, source_target_pairs={{0,1},{1,2},{2,3},{3,0},{4,5},{5,6},{6,7},{7,4},{8,9},{9,10},{10,1... | collective-permute-start | bytes 245768 | tf_op jit(solution)/shard_map/ppermute | solution.py:448
  29.8 16.2 %collective-permute-start.2 = (f32[96,128]{1,0:T(8,128)S(1)}, f32[96,128]{1,0:T(8,128)S(1)}, u32[]{:S(2)}, u32[]{:S(2)}) collective-permute-start(f32[96,128]{1,0:T(8,128)S(1)} %get-tuple-element.20), channel_id=1, source_target_pairs={{4,8},{12,16},{20,24},{28,32},{36,40},{44,48},{52,56},{8,4},{16,12... | collective-permute-start | bytes 147464 | tf_op jit(solution)/shard_map/ppermute | solution.py:452
  34.4 11.6 %collective-permute-start.3 = (f32[96,128]{1,0:T(8,128)S(1)}, f32[96,128]{1,0:T(8,128)S(1)}, u32[]{:S(2)}, u32[]{:S(2)}) collective-permute-start(f32[96,128]{1,0:T(8,128)S(1)} %get-tuple-element.21), channel_id=1, source_target_pairs={{0,4},{8,12},{16,20},{24,28},{32,36},{40,44},{48,52},{56,60},{4,0}... | collective-permute-start | bytes 147464 | tf_op jit(solution)/shard_map/ppermute | solution.py:453
  37.1 1.2 %copy-start = (f32[16,8,16,128]{3,2,1,0:T(8,128)S(1)}, f32[16,8,16,128]{3,2,1,0:T(8,128)}, u32[]{:S(2)}) copy-start(f32[16,8,16,128]{3,2,1,0:T(8,128)} %get-tuple-element.22.own) | copy-start | bytes 3145732
  46.0 11.9 %copy-start.2 = (f32[8,1,512]{2,1,0:T(1,128)S(1)}, f32[8,1,512]{2,1,0:T(1,128)}, u32[]{:S(2)}) copy-start(f32[8,1,512]{2,1,0:T(1,128)} %packing.1) | copy-start | bytes 49156
  46.2 11.8 %copy-start.1 = (f32[16,8,16,128]{3,2,1,0:T(8,128)S(1)}, f32[16,8,16,128]{3,2,1,0:T(8,128)}, u32[]{:S(2)}) copy-start(f32[16,8,16,128]{3,2,1,0:T(8,128)} %get-tuple-element.22.own) | copy-start | bytes 3145732
  46.2 11.7 %collective-permute-start.6 = (f32[856,128]{1,0:T(8,128)S(1)}, f32[856,128]{1,0:T(8,128)S(1)}, u32[]{:S(2)}, u32[]{:S(2)}) collective-permute-start(f32[856,128]{1,0:T(8,128)S(1)} %get-tuple-element.28), channel_id=1, source_target_pairs={{0,64},{64,128},{128,192},{192,256},{256,320},{320,384},{384,448},... | collective-permute-start | bytes 1314824 | tf_op jit(solution)/shard_map/ppermute | solution.py:463
  49.2 8.7 %collective-permute-start.7 = (f32[808,128]{1,0:T(8,128)S(1)}, f32[808,128]{1,0:T(8,128)S(1)}, u32[]{:S(2)}, u32[]{:S(2)}) collective-permute-start(f32[808,128]{1,0:T(8,128)S(1)} %get-tuple-element.29), channel_id=1, source_target_pairs={{64,0},{128,64},{192,128},{256,192},{320,256},{384,320},{448,384},... | collective-permute-start | bytes 1241096 | tf_op jit(solution)/shard_map/ppermute | solution.py:464
  72.6 20.8 %collective-permute-start.8 = (f32[8,512]{1,0:T(8,128)S(1)}, f32[8,512]{1,0:T(8,128)S(1)}, u32[]{:S(2)}, u32[]{:S(2)}) collective-permute-start(f32[8,512]{1,0:T(8,128)S(1)} %get-tuple-element.31.warmth), channel_id=1, source_target_pairs={{3,4},{7,8},{11,12},{15,16},{19,20},{23,24},{27,28},{31,32},{35,36... | collective-permute-start | bytes 49160 | tf_op jit(solution)/shard_map/ppermute | solution.py:485
  87.4 3.6 %collective-permute-start.9 = (f32[1,512]{1,0:T(1,128)S(1)}, f32[1,512]{1,0:T(1,128)S(1)}, u32[]{:S(2)}, u32[]{:S(2)}) collective-permute-start(f32[1,512]{1,0:T(1,128)S(1)} %get-tuple-element.34), channel_id=1, source_target_pairs={{0,64},{64,128},{128,192},{192,256},{256,320},{320,384},{384,448},... | collective-permute-start | bytes 6152 | tf_op jit(solution)/shard_map/ppermute | solution.py:486
  89.0 4.3 %collective-permute-start.10 = (f32[1,512]{1,0:T(1,128)S(1)}, f32[1,512]{1,0:T(1,128)S(1)}, u32[]{:S(2)}, u32[]{:S(2)}) collective-permute-start(f32[1,512]{1,0:T(1,128)S(1)} %get-tuple-element.35), channel_id=1, source_target_pairs={{64,0},{128,64},{192,128},{256,192},{320,256},{384,320},{448,384},... | collective-permute-start | bytes 6152 | tf_op jit(solution)/shard_map/ppermute | solution.py:487

commit v4 on v3

--- a/solution.py
+++ b/solution.py
@@ -11,8 +11,7 @@
 W = 4
 CX, CY, CZ = 16, 8, 256
 TX, TY = CX // 2, CY // 2
-PAD = W
-NX, NY = CX + 2 * PAD, CY + 2 * W
+NY = CY + 2 * W
 LANES = 128
 FIELDS = 8
 TILES = 2 * FIELDS
@@ -206,72 +205,55 @@
         outside(in_a, in_b, z_a, z_b)
 
 
-def field_kernel(own, own_z, in_a, in_b, z_a, z_b, from_low, from_high, base, out, s, zs, coef, reach, power, pair):
-    odd = parity()
-    span = 3 * LANES
-    middle = pl.ds(PAD, CX)
-    outer = (pl.ds(0, PAD), pl.ds(PAD + CX, PAD))
-
-    def lanes(k):
-        return pl.ds((k % 2) * LANES, LANES)
-
-    blank = jnp.zeros((PAD, LANES), F32)
-    for j in range(NY):
-        for rows in outer:
-            for k in range(TILES):
-                s[k // 2, j, rows, lanes(k)] = blank
-            zs[j, rows, :] = blank
-        for k in range(TILES + 1):
-            start, count = LOW_TABLE[k, j]
-            if count:
-                part = from_low[pl.ds(start, count), :]
-                if k < TILES:
-                    s[k // 2, j, pl.ds(PAD - count, count), lanes(k)] = part
-                else:
-                    zs[j, pl.ds(PAD - count, count), :] = part
-            start, count = HIGH_TABLE[k, j]
-            if count:
-                part = from_high[pl.ds(start, count), :]
-                if k < TILES:
-                    s[k // 2, j, pl.ds(PAD + CX, count), lanes(k)] = part
-                else:
-                    zs[j, pl.ds(PAD + CX, count), :] = part
+HALF = CX // 2
+
+
+def planes_of(own, own_z, in_a, in_b, z_a, z_b, put):
     for y in range(CY):
         for k in range(TILES):
-            s[k // 2, W + y, middle, lanes(k)] = own[k, y]
-        zs[W + y, middle, :] = own_z[y]
+            put(k, W + y, own[k, y])
+        put(TILES, W + y, own_z[y])
 
     def outside(low, high, z_low, z_high):
         for k in range(TILES):
             planes = Y_PLANES[k // 2]
             if planes < W:
-                s[k // 2, 0, middle, lanes(k)] = jnp.zeros((CX, LANES), F32)
-                s[k // 2, NY - 1, middle, lanes(k)] = jnp.zeros((CX, LANES), F32)
+                put(k, 0, jnp.zeros((CX, LANES), F32))
+                put(k, NY - 1, jnp.zeros((CX, LANES), F32))
             for i in range(planes):
-                s[k // 2, W - planes + i, middle, lanes(k)] = low[Y_START[k] + i]
-                s[k // 2, W + CY + i, middle, lanes(k)] = high[Y_START[k] + i]
+                put(k, W - planes + i, low[Y_START[k] + i])
+                put(k, W + CY + i, high[Y_START[k] + i])
         for i in range(W):
-            zs[i, middle, :] = z_low[pl.ds(CX * i, CX), :]
-            zs[W + CY + i, middle, :] = z_high[pl.ds(CX * i, CX), :]
-
-    @pl.when(odd == 1)
+            put(TILES, i, z_low[pl.ds(CX * i, CX), :])
+            put(TILES, W + CY + i, z_high[pl.ds(CX * i, CX), :])
+
+    @pl.when(parity() == 1)
     def _():
         outside(in_b, in_a, z_b, z_a)
 
-    @pl.when(odd == 0)
+    @pl.when(parity() == 0)
     def _():
         outside(in_a, in_b, z_a, z_b)
 
-    narrow = lane_ids((NX, LANES))
+
+def half_lanes(k):
+    return pl.ds((k % 2) * LANES, LANES)
+
+
+def leapfrog(s, zs, coef, reach, power, keep, middle):
+    span = 3 * LANES
+    narrow = lane_ids((CX, LANES))
     near = (narrow < W) | (narrow >= LANES - W)
     for j in range(NY):
         edges = zs[j]
         for f in range(FIELDS):
             s[f, j, :, 2 * LANES :] = jnp.where(near, pltpu.roll(edges, LANES - (8 * f + W), 1), 0.0)
 
-    wide = lane_ids((NX, span))
-    x = lax.broadcasted_iota(jnp.int32, (NX, span), 0)
-    inside = jnp.where((x < PAD) & (lax.axis_index("gx") == 0), 0.0, courant_dt)
+    wide = lane_ids((CX, span))
+    x = lax.broadcasted_iota(jnp.int32, (CX, span), 0)
+    inside = jnp.full((CX, span), courant_dt, F32)
+    if not middle:
+        inside = jnp.where((x < W) & (lax.axis_index("gx") == 0), 0.0, inside)
     inside = jnp.where((wide >= span - W) & (lax.axis_index("gz") == 0), 0.0, inside)
     reach[0] = inside
     reach[1] = inside * (lax.axis_index("gy") > 0).astype(F32)
@@ -295,27 +277,41 @@
     for step in range(ITERS):
         wave = 60.0 * math.sin(0.6 * (step + 0.5) * courant_dt)
 
+        def ahead_x(value, q, j):
+            turned = pltpu.roll(value, CX - 1, 0)
+            if middle:
+                keep[step, q, pl.ds(j, 1), :] = value[W : W + 1]
+                return turned
+            return jnp.where(x == HALF - 1, keep[step, q, pl.ds(j, 1), :], turned)
+
+        def behind_x(value, q, j):
+            turned = pltpu.roll(value, 1, 0)
+            if middle:
+                keep[step, q, pl.ds(j, 1), :] = value[CX - W - 1 : CX - W]
+                return turned
+            return jnp.where(x == HALF, keep[step, q, pl.ds(j, 1), :], turned)
+
         def magnetic(j):
             ex, ey, ez = s[0, j], s[1, j], s[2, j]
             step_h = reach[0 if j >= W else 1]
             s[3, j] -= step_h * ((s[2, j + 1] - ez) - (pltpu.roll(ey, span - 1, 1) - ey))
-            s[4, j] -= step_h * ((pltpu.roll(ex, span - 1, 1) - ex) - (pltpu.roll(ez, NX - 1, 0) - ez))
-            s[5, j] -= step_h * ((pltpu.roll(ey, NX - 1, 0) - ey) - (s[0, j + 1] - ex))
+            s[4, j] -= step_h * ((pltpu.roll(ex, span - 1, 1) - ex) - (ahead_x(ez, 1, j) - ez))
+            s[5, j] -= step_h * ((ahead_x(ey, 0, j) - ey) - (s[0, j + 1] - ex))
 
         def electric(j):
             hx, hy, hz = s[3, j], s[4, j], s[5, j]
             ca, cb, sig = coef[0, j], coef[1, j], coef[2, j]
             ex = ca * s[0, j] + cb * ((hz - s[5, j - 1]) - (hy - pltpu.roll(hy, 1, 1)))
-            ey = ca * s[1, j] + cb * ((hx - pltpu.roll(hx, 1, 1)) - (hz - pltpu.roll(hz, 1, 0)))
-            ez = ca * s[2, j] + cb * (((hy - pltpu.roll(hy, 1, 0)) - (hx - s[3, j - 1])) - s[7, j] * wave)
+            ey = ca * s[1, j] + cb * ((hx - pltpu.roll(hx, 1, 1)) - (hz - behind_x(hz, 3, j)))
+            ez = ca * s[2, j] + cb * (((hy - behind_x(hy, 2, j)) - (hx - s[3, j - 1])) - s[7, j] * wave)
             s[0, j] = ex
             s[1, j] = ey
             s[2, j] = ez
             p = j - W
             if 0 <= p < CY:
-                own_z_lanes = slice(0, 2 * LANES)
-                ex, ey, ez = ex[:, own_z_lanes], ey[:, own_z_lanes], ez[:, own_z_lanes]
-                now = sig[:, own_z_lanes] * (ex * ex + ey * ey + ez * ez)
+                own = slice(0, 2 * LANES)
+                ex, ey, ez = ex[:, own], ey[:, own], ez[:, own]
+                now = sig[:, own] * (ex * ex + ey * ey + ez * ez)
                 power[p] = now if step == 0 else power[p] + now
 
         magnetic(step)
@@ -323,12 +319,53 @@
             magnetic(j)
             electric(j)
 
+
+def middle_field_kernel(own, own_z, in_a, in_b, z_a, z_b, power, keep, s, zs, coef, reach):
+    def put(k, j, rows):
+        if k == TILES:
+            zs[j] = rows
+        else:
+            s[k // 2, j, :, half_lanes(k)] = rows
+
+    planes_of(own, own_z, in_a, in_b, z_a, z_b, put)
+    leapfrog(s, zs, coef, reach, power, keep, True)
+
+
+def field_kernel(own, own_z, in_a, in_b, z_a, z_b, from_low, from_high, base, inner, keep, out, s, zs, coef, reach, power, pair):
+    def store(k, j, start, rows):
+        here = pl.ds(start, rows.shape[0])
+        if k == TILES:
+            zs[j, here, :] = rows
+        else:
+            s[k // 2, j, here, half_lanes(k)] = rows
+
+    for j in range(NY):
+        for k in range(TILES + 1):
+            for message, table, edge in ((from_low, LOW_TABLE, 0), (from_high, HIGH_TABLE, CX - W)):
+                start, count = table[k, j]
+                if count < W:
+                    store(k, j, edge, jnp.zeros((W, LANES), F32))
+                if count:
+                    store(k, j, W - count if edge == 0 else edge, message[pl.ds(start, count), :])
+
+    def put(k, j, rows):
+        store(k, j, W, rows[:W])
+        store(k, j, HALF, rows[CX - W :])
+
+    planes_of(own, own_z, in_a, in_b, z_a, z_b, put)
+    leapfrog(s, zs, coef, reach, power, keep, False)
+
     rows = []
     for t in range(TY):
         halves = []
         for k in range(2):
-            pair[...] = power[2 * t, :, lanes(k)] + power[2 * t + 1, :, lanes(k)]
-            halves.append(pair[pl.ds(PAD, TX, stride=2), :] + pair[pl.ds(PAD + 1, TX, stride=2), :])
+            lanes = half_lanes(k)
+            ends = power[2 * t, :, lanes] + power[2 * t + 1, :, lanes]
+            centre = inner[2 * t, :, lanes] + inner[2 * t + 1, :, lanes]
+            pair[pl.ds(0, W), :] = ends[W : 2 * W]
+            pair[pl.ds(W, HALF), :] = centre[W : W + HALF]
+            pair[pl.ds(W + HALF, W), :] = ends[HALF : HALF + W]
+            halves.append(pair[pl.ds(0, TX, stride=2), :] + pair[pl.ds(1, TX, stride=2), :])
         rows.append(jnp.concatenate(halves, axis=1))
     stacked = jnp.concatenate(rows, axis=0)
     source = lax.broadcasted_iota(jnp.int32, (2 * LANES, LANES), 0)
@@ -466,19 +503,21 @@
     base, packed = call(warm_kernel, (pencil, pencil), [VMEM] * 8)(
         pencil_tiles, packing, from_below, from_above, z_a, z_b, from_low, from_high
     )
+    work = [
+        pltpu.VMEM((FIELDS, NY, CX, 3 * LANES), F32),
+        pltpu.VMEM((NY, CX, LANES), F32),
+        pltpu.VMEM((3, NY, CX, 3 * LANES), F32),
+        pltpu.VMEM((2, CX, 3 * LANES), F32),
+    ]
+    power = (CY, CX, 2 * LANES)
+    local_parts = (own, own_z, in_a, in_b, z_a, z_b)
+    inner = call(middle_field_kernel, (f32(*power), f32(ITERS, 4, NY, 3 * LANES)), [VMEM] * 6, scratch=work)(*local_parts)
     heat = call(
         field_kernel,
         f32(TY, 3 + span // LANES, TX, LANES),
-        [VMEM] * 9,
-        scratch=[
-            pltpu.VMEM((FIELDS, NY, NX, 3 * LANES), F32),
-            pltpu.VMEM((NY, NX, LANES), F32),
-            pltpu.VMEM((3, NY, NX, 3 * LANES), F32),
-            pltpu.VMEM((2, NX, 3 * LANES), F32),
-            pltpu.VMEM((CY, NX, 2 * LANES), F32),
-            pltpu.VMEM((NX, LANES), F32),
-        ],
-    )(own, own_z, in_a, in_b, z_a, z_b, from_low, from_high, base)
+        [VMEM] * 11,
+        scratch=work + [pltpu.VMEM(power, F32), pltpu.VMEM((CX, LANES), F32)],
+    )(*local_parts, from_low, from_high, base, *inner)
     heat = lax.all_to_all(heat, "gz", split_axis=0, concat_axis=0, tiled=True)
     t, beside, first, last = call(first_kernel, (pencil, pencil, line, line), [VMEM] * 2)(base, heat)
     ends = [(i, i + 1) for i in range(n_z - 1, n_y * n_z - 1, n_z)]

time: 94.6 us -> 92.9 us (0.982)
  waiting for transfers between devices: 19.3 us -> 15.6 us
  Pallas kernels: 11 us -> 14.4 us
  blocking collectives: 8.24 us -> 6.7 us
    ppermute x1, waiting for transfers between devices: 7.44 us -> 2.6 us  [local(): from_high = lax.ppermute(to_down, 'gx', shifts(n_x, -1))]
    pallas_call x1 -> x2, Pallas kernels: 6.3 us -> 9.7 us  [the longest x1 4.87 us: local(): call(field_kernel, f32(TY, 3 + span // LANES, TX, LANES), [VMEM] * 11, sc...]
    ppermute x1, waiting for transfers between devices: 0.1 us -> 3.14 us  [local(): lax.ppermute(shared, 'gz', [(i, (i - 1) % n_z) for i in range(n_z)])]
    ppermute x1, starting transfers between devices: 4.12 us -> 1.92 us  [local(): lax.ppermute(shared, 'gz', [(i, (i + 1) % n_z) for i in range(n_z)])]
    ppermute x1, waiting for transfers between devices: 1.68 us -> 0.1 us  [local(): lax.ppermute(shared, 'gz', [(i, (i + 1) % n_z) for i in range(n_z)])]
    all_to_all x1, blocking collectives: 8.24 us -> 6.7 us  [local(): heat = lax.all_to_all(heat, 'gz', split_axis=0, concat_axis=0, tiled=True)]
    ppermute x1, starting transfers between devices: 14.8 us -> 15.9 us  [local(): outer = lax.ppermute(t, ('gy', 'gz'), ends + [(j, i) for i, j in ends])]
    ppermute x1, starting transfers between devices: 2.37 us -> 3.36 us  [local(): lax.ppermute(shared, 'gz', [(i, (i - 1) % n_z) for i in range(n_z)])]
  transfers between devices with their start and end apart: 11 -> 11, of which waited for: 5 -> 5; matrix products, arithmetic and copies ran while one was open for 1% -> 1% of each run, Pallas kernels for 1% -> 6%
where the time goes in v4:
time: 92.9 us; the launch traced here: 92.3 us
  starting transfers between devices  52.9 us (57%)
  waiting for transfers between devices  15.6 us (17%)
  Pallas kernels  14.4 us (16%)
  blocking collectives  6.7 us (7%)
  local copies, waits for them, and re-layouts  1.96 us (2%)
    ppermute x1, starting transfers between devices, local(): in_a = lax.ppermute(to_a, 'gy', across)  15.9 us
    ppermute x1, starting transfers between devices, local(): outer = lax.ppermute(t, ('gy', 'gz'), ends + [(j, i) for i, j in ends])  15.9 us
    ppermute x1, waiting for transfers between devices, local(): z_a = lax.ppermute(z_a, 'gy', across)  7.4 us
    all_to_all x1, blocking collectives, local(): heat = lax.all_to_all(heat, 'gz', split_axis=0, concat_axis=0, tiled=True)  6.7 us
    pallas_call x1, Pallas kernels, local(): call(field_kernel, f32(TY, 3 + span // LANES, TX, LANES), [VMEM] * 11, sc...  4.87 us
    ppermute x1, starting transfers between devices, local(): z_a = lax.ppermute(z_a, 'gy', across)  4.86 us
    pallas_call x1, Pallas kernels, local(): call(middle_field_kernel, (f32(*power), f32(ITERS, 4, NY, 3 * LANES)), [V...  4.83 us
    ppermute x1, starting transfers between devices, local(): lax.ppermute(shared, 'gz', [(i, (i - 1) % n_z) for i in range(n_z)])  3.36 us
  transfers between devices with their start and end apart: 11, of which 5 were waited for; matrix products, arithmetic and copies ran while one was open for 1% of the time, Pallas kernels for 6%

profile of v4, /device:TPU:31, one launch (start us, length us, event | category | flops | bytes accessed | tf_op | source)
XLA Modules:
  0.0 92.3 jit_solution(16348040822122932541)
XLA Ops:
  0.6 3.0 %shard_map.77 = (f32[16,8,16,128]{3,2,1,0:T(8,128)}, f32[58,16,128]{2,1,0:T(8,128)}, f32[58,16,128]{2,1,0:T(8,128)}, f32[160,128]{1,0:T(8,128)}) custom-call(s32[1,16]{1,0:T(1,128)} %spots_hbm.1, f32[3,256,128]{2,1,0:T(8,128)} %bitcast.15, f32[3,256,128]{2,1,0:T(8,128)} %bitcast.16, s32[256,128]{1,0:T(8,128)} %bitcast.17, f32[8,1,512]{2,1,0:T(1,128)} %t_hbm.1), custom_call_target="tpu_custom_call" | custom-call | tf_op jit(solution)/shard_map/pallas_call | solution.py:469
  3.7 15.9 %collective-permute-start.4 = (f32[58,16,128]{2,1,0:T(8,128)}, f32[58,16,128]{2,1,0:T(8,128)S(1)}, u32[]{:S(2)}, u32[]{:S(2)}) collective-permute-start(f32[58,16,128]{2,1,0:T(8,128)} %get-tuple-element.28), channel_id=1, source_target_pairs={{4,8},{12,16},{20,24},{28,32},{36,40},{44,48},{52,56},{8,4},{16,12... | collective-permute-start | bytes 1425416 | tf_op jit(solution)/shard_map/ppermute | solution.py:483
  19.6 1.9 %collective-permute-start.5 = (f32[58,16,128]{2,1,0:T(8,128)}, f32[58,16,128]{2,1,0:T(8,128)S(1)}, u32[]{:S(2)}, u32[]{:S(2)}) collective-permute-start(f32[58,16,128]{2,1,0:T(8,128)} %get-tuple-element.29), channel_id=1, source_target_pairs={{0,4},{8,12},{16,20},{24,28},{32,36},{40,44},{48,52},{56,60},{4,0}... | collective-permute-start | bytes 1425416 | tf_op jit(solution)/shard_map/ppermute | solution.py:484
  21.5 1.9 %collective-permute-start = (f32[160,128]{1,0:T(8,128)}, f32[160,128]{1,0:T(8,128)S(1)}, u32[]{:S(2)}, u32[]{:S(2)}) collective-permute-start(f32[160,128]{1,0:T(8,128)} %get-tuple-element.21), channel_id=1, source_target_pairs={{0,1},{1,2},{2,3},{3,0},{4,5},{5,6},{6,7},{7,4},{8,9},{9,10},{10,1... | collective-permute-start | bytes 245768 | tf_op jit(solution)/shard_map/ppermute | solution.py:485
  23.4 3.4 %collective-permute-start.1 = (f32[160,128]{1,0:T(8,128)}, f32[160,128]{1,0:T(8,128)S(1)}, u32[]{:S(2)}, u32[]{:S(2)}) collective-permute-start(f32[160,128]{1,0:T(8,128)} %get-tuple-element.21), channel_id=1, source_target_pairs={{0,3},{1,0},{2,1},{3,2},{4,7},{5,4},{6,5},{7,6},{8,11},{9,8},{10,9... | collective-permute-start | bytes 245768 | tf_op jit(solution)/shard_map/ppermute | solution.py:486
  26.8 0.1 collective-permute-done.from_below
  26.9 3.1 %collective-permute-done.1.from_above = f32[160,128]{1,0:T(8,128)S(1)} collective-permute-done((f32[160,128]{1,0:T(8,128)}, f32[160,128]{1,0:T(8,128)S(1)}, u32[]{:S(2)}, u32[]{:S(2)}) %collective-permute-start.1) | collective-permute-done | bytes 81952 | tf_op jit(solution)/shard_map/ppermute | solution.py:486
  30.1 4.9 %collective-permute-start.2 = (f32[96,128]{1,0:T(8,128)S(1)}, f32[96,128]{1,0:T(8,128)S(1)}, u32[]{:S(2)}, u32[]{:S(2)}) collective-permute-start(f32[96,128]{1,0:T(8,128)S(1)} %get-tuple-element.22), channel_id=1, source_target_pairs={{4,8},{12,16},{20,24},{28,32},{36,40},{44,48},{52,56},{8,4},{16,12... | collective-permute-start | bytes 147464 | tf_op jit(solution)/shard_map/ppermute | solution.py:489
  34.9 1.9 %collective-permute-start.3 = (f32[96,128]{1,0:T(8,128)S(1)}, f32[96,128]{1,0:T(8,128)S(1)}, u32[]{:S(2)}, u32[]{:S(2)}) collective-permute-start(f32[96,128]{1,0:T(8,128)S(1)} %get-tuple-element.23), channel_id=1, source_target_pairs={{0,4},{8,12},{16,20},{24,28},{32,36},{40,44},{48,52},{56,60},{4,0}... | collective-permute-start | bytes 147464 | tf_op jit(solution)/shard_map/ppermute | solution.py:490
  36.9 0.7 slice.3.warmth
  37.6 1.2 %copy-done = f32[16,8,16,128]{3,2,1,0:T(8,128)S(1)} copy-done((f32[16,8,16,128]{3,2,1,0:T(8,128)S(1)}, f32[16,8,16,128]{3,2,1,0:T(8,128)}, u32[]{:S(2)}) %copy-start) | copy-done | bytes 1048600
  38.8 0.1 shard_map.79
  38.9 7.4 %collective-permute-done.2.z_a = f32[96,128]{1,0:T(8,128)S(1)} collective-permute-done((f32[96,128]{1,0:T(8,128)S(1)}, f32[96,128]{1,0:T(8,128)S(1)}, u32[]{:S(2)}, u32[]{:S(2)}) %collective-permute-start.2) | collective-permute-done | bytes 49184 | tf_op jit(solution)/shard_map/ppermute | solution.py:489
  46.3 0.0 collective-permute-done.3.z_b
  46.3 0.0 collective-permute-done.4.in_a
  46.3 0.0 collective-permute-done.5.in_b
  46.3 0.1 shard_map.80
  46.5 2.8 %collective-permute-start.6 = (f32[856,128]{1,0:T(8,128)S(1)}, f32[856,128]{1,0:T(8,128)S(1)}, u32[]{:S(2)}, u32[]{:S(2)}) collective-permute-start(f32[856,128]{1,0:T(8,128)S(1)} %get-tuple-element.30), channel_id=1, source_target_pairs={{0,64},{64,128},{128,192},{192,256},{256,320},{320,384},{384,448},... | collective-permute-start | bytes 1314824 | tf_op jit(solution)/shard_map/ppermute | solution.py:500
  49.3 0.0 copy-start.2
  49.3 1.3 %collective-permute-start.7 = (f32[808,128]{1,0:T(8,128)S(1)}, f32[808,128]{1,0:T(8,128)S(1)}, u32[]{:S(2)}, u32[]{:S(2)}) collective-permute-start(f32[808,128]{1,0:T(8,128)S(1)} %get-tuple-element.31), channel_id=1, source_target_pairs={{64,0},{128,64},{192,128},{256,192},{320,256},{384,320},{448,384},... | collective-permute-start | bytes 1241096 | tf_op jit(solution)/shard_map/ppermute | solution.py:501
  50.6 4.8 %shard_map.82 = (f32[8,16,256]{2,1,0:T(8,128)S(1)}, f32[4,4,16,384]{3,2,1,0:T(8,128)S(1)}) custom-call(f32[16,8,16,128]{3,2,1,0:T(8,128)S(1)} %copy-done.1, f32[8,16,128]{2,1,0:T(8,128)S(1)} %get-tuple-element.25.own_z, f32[58,16,128]{2,1,0:T(8,128)S(1)} %collective-permute-done.4.in_a, f32[58,16,128]{2,1,0:T(8,128)S(1)} %collective-permute-done.5.in_b, ...), custom_call_target="tpu_custom_call" | custom-call | tf_op jit(solution)/shard_map/pallas_call | solution.py:514
  55.5 2.6 %collective-permute-done.7.from_high = f32[808,128]{1,0:T(8,128)S(1)} collective-permute-done((f32[808,128]{1,0:T(8,128)S(1)}, f32[808,128]{1,0:T(8,128)S(1)}, u32[]{:S(2)}, u32[]{:S(2)}) %collective-permute-start.7) | collective-permute-done | bytes 413728 | tf_op jit(solution)/shard_map/ppermute | solution.py:501
  58.1 0.0 collective-permute-done.6.from_low
  58.1 0.1 shard_map.81
  58.1 4.9 %shard_map.83 = f32[4,7,8,128]{3,2,1,0:T(8,128)S(1)} custom-call(f32[16,8,16,128]{3,2,1,0:T(8,128)S(1)} %copy-done.1, f32[8,16,128]{2,1,0:T(8,128)S(1)} %get-tuple-element.25.own_z, f32[58,16,128]{2,1,0:T(8,128)S(1)} %collective-permute-done.4.in_a, f32[58,16,128]{2,1,0:T(8,128)S(1)} %collective-permute-done.5.in_b, ...), custom_call_target="tpu_custom_call" | custom-call | tf_op jit(solution)/shard_map/pallas_call | solution.py:515
  63.0 6.7 %all_to_all.5.heat = f32[4,7,8,128]{3,2,1,0:T(8,128)S(1)} all-to-all(f32[4,7,8,128]{3,2,1,0:T(8,128)S(1)} %shard_map.83), channel_id=1, replica_groups=mesh['gx'=8,'gy'=16,'gz'=4] {'gz'}, dimensions={0} | all-to-all | bytes 229376 | tf_op jit(solution)/shard_map/all_to_all | solution.py:521
  69.7 15.9 %collective-permute-start.8 = (f32[8,512]{1,0:T(8,128)S(1)}, f32[8,512]{1,0:T(8,128)S(1)}, u32[]{:S(2)}, u32[]{:S(2)}) collective-permute-start(f32[8,512]{1,0:T(8,128)S(1)} %get-tuple-element.35.warmth), channel_id=1, source_target_pairs={{3,4},{7,8},{11,12},{15,16},{19,20},{23,24},{27,28},{31,32},{35,36... | collective-permute-start | bytes 49160 | tf_op jit(solution)/shard_map/ppermute | solution.py:524
  85.7 1.6 %collective-permute-start.9 = (f32[1,512]{1,0:T(1,128)S(1)}, f32[1,512]{1,0:T(1,128)S(1)}, u32[]{:S(2)}, u32[]{:S(2)}) collective-permute-start(f32[1,512]{1,0:T(1,128)S(1)} %get-tuple-element.38), channel_id=1, source_target_pairs={{0,64},{64,128},{128,192},{192,256},{256,320},{320,384},{384,448},... | collective-permute-start | bytes 6152 | tf_op jit(solution)/shard_map/ppermute | solution.py:525
  87.3 1.3 %collective-permute-start.10 = (f32[1,512]{1,0:T(1,128)S(1)}, f32[1,512]{1,0:T(1,128)S(1)}, u32[]{:S(2)}, u32[]{:S(2)}) collective-permute-start(f32[1,512]{1,0:T(1,128)S(1)} %get-tuple-element.39), channel_id=1, source_target_pairs={{64,0},{128,64},{192,128},{256,192},{320,256},{384,320},{448,384},... | collective-permute-start | bytes 6152 | tf_op jit(solution)/shard_map/ppermute | solution.py:526
  88.6 0.6 shard_map.86
  89.2 2.4 %collective-permute-done.10.after = f32[1,512]{1,0:T(1,128)S(1)} collective-permute-done((f32[1,512]{1,0:T(1,128)S(1)}, f32[1,512]{1,0:T(1,128)S(1)}, u32[]{:S(2)}, u32[]{:S(2)}) %collective-permute-start.10) | collective-permute-done | bytes 2080 | tf_op jit(solution)/shard_map/ppermute | solution.py:526
  91.6 0.7 shard_map.85
  (8 shorter events, 0.1 us)
Async XLA Ops:
  3.7 42.7 %collective-permute-start.4 = (f32[58,16,128]{2,1,0:T(8,128)}, f32[58,16,128]{2,1,0:T(8,128)S(1)}, u32[]{:S(2)}, u32[]{:S(2)}) collective-permute-start(f32[58,16,128]{2,1,0:T(8,128)} %get-tuple-element.28), channel_id=1, source_target_pairs={{4,8},{12,16},{20,24},{28,32},{36,40},{44,48},{52,56},{8,4},{16,12... | collective-permute-start | bytes 1425416 | tf_op jit(solution)/shard_map/ppermute | solution.py:483
  19.6 26.7 %collective-permute-start.5 = (f32[58,16,128]{2,1,0:T(8,128)}, f32[58,16,128]{2,1,0:T(8,128)S(1)}, u32[]{:S(2)}, u32[]{:S(2)}) collective-permute-start(f32[58,16,128]{2,1,0:T(8,128)} %get-tuple-element.29), channel_id=1, source_target_pairs={{0,4},{8,12},{16,20},{24,28},{32,36},{40,44},{48,52},{56,60},{4,0}... | collective-permute-start | bytes 1425416 | tf_op jit(solution)/shard_map/ppermute | solution.py:484
  21.5 5.4 %collective-permute-start = (f32[160,128]{1,0:T(8,128)}, f32[160,128]{1,0:T(8,128)S(1)}, u32[]{:S(2)}, u32[]{:S(2)}) collective-permute-start(f32[160,128]{1,0:T(8,128)} %get-tuple-element.21), channel_id=1, source_target_pairs={{0,1},{1,2},{2,3},{3,0},{4,5},{5,6},{6,7},{7,4},{8,9},{9,10},{10,1... | collective-permute-start | bytes 245768 | tf_op jit(solution)/shard_map/ppermute | solution.py:485
  23.4 6.6 %collective-permute-start.1 = (f32[160,128]{1,0:T(8,128)}, f32[160,128]{1,0:T(8,128)S(1)}, u32[]{:S(2)}, u32[]{:S(2)}) collective-permute-start(f32[160,128]{1,0:T(8,128)} %get-tuple-element.21), channel_id=1, source_target_pairs={{0,3},{1,0},{2,1},{3,2},{4,7},{5,4},{6,5},{7,6},{8,11},{9,8},{10,9... | collective-permute-start | bytes 245768 | tf_op jit(solution)/shard_map/ppermute | solution.py:486
  30.1 16.2 %collective-permute-start.2 = (f32[96,128]{1,0:T(8,128)S(1)}, f32[96,128]{1,0:T(8,128)S(1)}, u32[]{:S(2)}, u32[]{:S(2)}) collective-permute-start(f32[96,128]{1,0:T(8,128)S(1)} %get-tuple-element.22), channel_id=1, source_target_pairs={{4,8},{12,16},{20,24},{28,32},{36,40},{44,48},{52,56},{8,4},{16,12... | collective-permute-start | bytes 147464 | tf_op jit(solution)/shard_map/ppermute | solution.py:489
  34.9 11.4 %collective-permute-start.3 = (f32[96,128]{1,0:T(8,128)S(1)}, f32[96,128]{1,0:T(8,128)S(1)}, u32[]{:S(2)}, u32[]{:S(2)}) collective-permute-start(f32[96,128]{1,0:T(8,128)S(1)} %get-tuple-element.23), channel_id=1, source_target_pairs={{0,4},{8,12},{16,20},{24,28},{32,36},{40,44},{48,52},{56,60},{4,0}... | collective-permute-start | bytes 147464 | tf_op jit(solution)/shard_map/ppermute | solution.py:490
  37.6 1.2 %copy-start = (f32[16,8,16,128]{3,2,1,0:T(8,128)S(1)}, f32[16,8,16,128]{3,2,1,0:T(8,128)}, u32[]{:S(2)}) copy-start(f32[16,8,16,128]{3,2,1,0:T(8,128)} %get-tuple-element.24.own) | copy-start | bytes 3145732
  38.9 11.7 %copy-start.1 = (f32[16,8,16,128]{3,2,1,0:T(8,128)S(1)}, f32[16,8,16,128]{3,2,1,0:T(8,128)}, u32[]{:S(2)}) copy-start(f32[16,8,16,128]{3,2,1,0:T(8,128)} %get-tuple-element.24.own) | copy-start | bytes 3145732
  46.5 11.6 %collective-permute-start.6 = (f32[856,128]{1,0:T(8,128)S(1)}, f32[856,128]{1,0:T(8,128)S(1)}, u32[]{:S(2)}, u32[]{:S(2)}) collective-permute-start(f32[856,128]{1,0:T(8,128)S(1)} %get-tuple-element.30), channel_id=1, source_target_pairs={{0,64},{64,128},{128,192},{192,256},{256,320},{320,384},{384,448},... | collective-permute-start | bytes 1314824 | tf_op jit(solution)/shard_map/ppermute | solution.py:500
  49.3 8.8 %copy-start.2 = (f32[8,1,512]{2,1,0:T(1,128)S(1)}, f32[8,1,512]{2,1,0:T(1,128)}, u32[]{:S(2)}) copy-start(f32[8,1,512]{2,1,0:T(1,128)} %packing.1) | copy-start | bytes 49156
  49.3 8.7 %collective-permute-start.7 = (f32[808,128]{1,0:T(8,128)S(1)}, f32[808,128]{1,0:T(8,128)S(1)}, u32[]{:S(2)}, u32[]{:S(2)}) collective-permute-start(f32[808,128]{1,0:T(8,128)S(1)} %get-tuple-element.31), channel_id=1, source_target_pairs={{64,0},{128,64},{192,128},{256,192},{320,256},{384,320},{448,384},... | collective-permute-start | bytes 1241096 | tf_op jit(solution)/shard_map/ppermute | solution.py:501
  69.7 21.9 %collective-permute-start.8 = (f32[8,512]{1,0:T(8,128)S(1)}, f32[8,512]{1,0:T(8,128)S(1)}, u32[]{:S(2)}, u32[]{:S(2)}) collective-permute-start(f32[8,512]{1,0:T(8,128)S(1)} %get-tuple-element.35.warmth), channel_id=1, source_target_pairs={{3,4},{7,8},{11,12},{15,16},{19,20},{23,24},{27,28},{31,32},{35,36... | collective-permute-start | bytes 49160 | tf_op jit(solution)/shard_map/ppermute | solution.py:524
  85.7 3.6 %collective-permute-start.9 = (f32[1,512]{1,0:T(1,128)S(1)}, f32[1,512]{1,0:T(1,128)S(1)}, u32[]{:S(2)}, u32[]{:S(2)}) collective-permute-start(f32[1,512]{1,0:T(1,128)S(1)} %get-tuple-element.38), channel_id=1, source_target_pairs={{0,64},{64,128},{128,192},{192,256},{256,320},{320,384},{384,448},... | collective-permute-start | bytes 6152 | tf_op jit(solution)/shard_map/ppermute | solution.py:525
  87.3 4.3 %collective-permute-start.10 = (f32[1,512]{1,0:T(1,128)S(1)}, f32[1,512]{1,0:T(1,128)S(1)}, u32[]{:S(2)}, u32[]{:S(2)}) collective-permute-start(f32[1,512]{1,0:T(1,128)S(1)} %get-tuple-element.39), channel_id=1, source_target_pairs={{64,0},{128,64},{192,128},{256,192},{320,256},{384,320},{448,384},... | collective-permute-start | bytes 6152 | tf_op jit(solution)/shard_map/ppermute | solution.py:526

commit v5 on v4

--- a/solution.py
+++ b/solution.py
@@ -135,13 +135,12 @@
 
     wide = lane_ids((CX, LANES))
     slot = wide // 8
-    upper = wide % 8 >= W
     for y in range(CY):
         edge = jnp.zeros((CX, LANES), F32)
         for f in range(FIELDS):
             shift = 8 * f + W
-            ends = jnp.where(upper, pltpu.roll(own[2 * f, y], shift, 1), pltpu.roll(own[2 * f + 1, y], shift, 1))
-            edge = jnp.where(slot == f, ends, edge)
+            ends = jnp.where(wide < LANES // 2, own[2 * f, y], own[2 * f + 1, y])
+            edge = jnp.where(slot == f, pltpu.roll(ends, shift, 1), edge)
         shared[pl.ds(CX * y, CX), :] = edge
     copies[8].wait()
     for k in range(heat.shape[2] // LANES):
@@ -284,12 +283,12 @@
                 return turned
             return jnp.where(x == HALF - 1, keep[step, q, pl.ds(j, 1), :], turned)
 
-        def behind_x(value, q, j):
+        def behind_x(value, q, j, cells):
             turned = pltpu.roll(value, 1, 0)
             if middle:
-                keep[step, q, pl.ds(j, 1), :] = value[CX - W - 1 : CX - W]
+                keep[step, q, pl.ds(j, 1), cells] = value[CX - W - 1 : CX - W]
                 return turned
-            return jnp.where(x == HALF, keep[step, q, pl.ds(j, 1), :], turned)
+            return jnp.where(x[:, cells] == HALF, keep[step, q, pl.ds(j, 1), cells], turned)
 
         def magnetic(j):
             ex, ey, ez = s[0, j], s[1, j], s[2, j]
@@ -300,13 +299,19 @@
 
         def electric(j):
             hx, hy, hz = s[3, j], s[4, j], s[5, j]
-            ca, cb, sig = coef[0, j], coef[1, j], coef[2, j]
-            ex = ca * s[0, j] + cb * ((hz - s[5, j - 1]) - (hy - pltpu.roll(hy, 1, 1)))
-            ey = ca * s[1, j] + cb * ((hx - pltpu.roll(hx, 1, 1)) - (hz - behind_x(hz, 3, j)))
-            ez = ca * s[2, j] + cb * (((hy - behind_x(hy, 2, j)) - (hx - s[3, j - 1])) - s[7, j] * wave)
-            s[0, j] = ex
-            s[1, j] = ey
-            s[2, j] = ez
+            cells = slice(0, 2 * LANES if step == ITERS - 1 else span)
+            ca, cb, sig = coef[0, j, :, cells], coef[1, j, :, cells], coef[2, j, :, cells]
+            hy_z, hx_z = pltpu.roll(hy, 1, 1)[:, cells], pltpu.roll(hx, 1, 1)[:, cells]
+            hx, hy, hz = hx[:, cells], hy[:, cells], hz[:, cells]
+            hx_y, hz_y = s[3, j - 1, :, cells], s[5, j - 1, :, cells]
+            ex = ca * s[0, j, :, cells] + cb * ((hz - hz_y) - (hy - hy_z))
+            ey = ca * s[1, j, :, cells] + cb * ((hx - hx_z) - (hz - behind_x(hz, 3, j, cells)))
+            curl = (hy - behind_x(hy, 2, j, cells)) - (hx - hx_y)
+            ez = ca * s[2, j, :, cells] + cb * (curl - s[7, j, :, cells] * wave)
+            if step < ITERS - 1:
+                s[0, j] = ex
+                s[1, j] = ey
+                s[2, j] = ez
             p = j - W
             if 0 <= p < CY:
                 own = slice(0, 2 * LANES)

time: 92.9 us -> 92.7 us (level)
  no operation moved by 1% of the time
where the time goes in v5:
time: 92.7 us; the launch traced here: 92.1 us
  starting transfers between devices  52.9 us (57%)
  waiting for transfers between devices  15.6 us (17%)
  Pallas kernels  14.2 us (15%)
  blocking collectives  6.7 us (7%)
  local copies, waits for them, and re-layouts  1.96 us (2%)
    ppermute x1, starting transfers between devices, local(): in_a = lax.ppermute(to_a, 'gy', across)  15.9 us
    ppermute x1, starting transfers between devices, local(): outer = lax.ppermute(t, ('gy', 'gz'), ends + [(j, i) for i, j in ends])  15.9 us
    ppermute x1, waiting for transfers between devices, local(): z_a = lax.ppermute(z_a, 'gy', across)  7.4 us
    all_to_all x1, blocking collectives, local(): heat = lax.all_to_all(heat, 'gz', split_axis=0, concat_axis=0, tiled=True)  6.7 us
    ppermute x1, starting transfers between devices, local(): z_a = lax.ppermute(z_a, 'gy', across)  4.86 us
    pallas_call x1, Pallas kernels, local(): call(middle_field_kernel, (f32(*power), f32(ITERS, 4, NY, 3 * LANES)), [V...  4.82 us
    pallas_call x1, Pallas kernels, local(): call(field_kernel, f32(TY, 3 + span // LANES, TX, LANES), [VMEM] * 11, sc...  4.81 us
    ppermute x1, starting transfers between devices, local(): lax.ppermute(shared, 'gz', [(i, (i - 1) % n_z) for i in range(n_z)])  3.36 us
  transfers between devices with their start and end apart: 11, of which 5 were waited for; matrix products, arithmetic and copies ran while one was open for 1% of the time, Pallas kernels for 6%

profile of v5, /device:TPU:31, one launch (start us, length us, event | category | flops | bytes accessed | tf_op | source)
XLA Modules:
  0.0 92.1 jit_solution(5326028321273759926)
XLA Ops:
  0.6 2.9 %shard_map.77 = (f32[16,8,16,128]{3,2,1,0:T(8,128)}, f32[58,16,128]{2,1,0:T(8,128)}, f32[58,16,128]{2,1,0:T(8,128)}, f32[160,128]{1,0:T(8,128)}) custom-call(s32[1,16]{1,0:T(1,128)} %spots_hbm.1, f32[3,256,128]{2,1,0:T(8,128)} %bitcast.15, f32[3,256,128]{2,1,0:T(8,128)} %bitcast.16, s32[256,128]{1,0:T(8,128)} %bitcast.17, f32[8,1,512]{2,1,0:T(1,128)} %t_hbm.1), custom_call_target="tpu_custom_call" | custom-call | tf_op jit(solution)/shard_map/pallas_call | solution.py:474
  3.5 15.9 %collective-permute-start.4 = (f32[58,16,128]{2,1,0:T(8,128)}, f32[58,16,128]{2,1,0:T(8,128)S(1)}, u32[]{:S(2)}, u32[]{:S(2)}) collective-permute-start(f32[58,16,128]{2,1,0:T(8,128)} %get-tuple-element.28), channel_id=1, source_target_pairs={{4,8},{12,16},{20,24},{28,32},{36,40},{44,48},{52,56},{8,4},{16,12... | collective-permute-start | bytes 1425416 | tf_op jit(solution)/shard_map/ppermute | solution.py:488
  19.5 1.9 %collective-permute-start.5 = (f32[58,16,128]{2,1,0:T(8,128)}, f32[58,16,128]{2,1,0:T(8,128)S(1)}, u32[]{:S(2)}, u32[]{:S(2)}) collective-permute-start(f32[58,16,128]{2,1,0:T(8,128)} %get-tuple-element.29), channel_id=1, source_target_pairs={{0,4},{8,12},{16,20},{24,28},{32,36},{40,44},{48,52},{56,60},{4,0}... | collective-permute-start | bytes 1425416 | tf_op jit(solution)/shard_map/ppermute | solution.py:489
  21.4 1.9 %collective-permute-start = (f32[160,128]{1,0:T(8,128)}, f32[160,128]{1,0:T(8,128)S(1)}, u32[]{:S(2)}, u32[]{:S(2)}) collective-permute-start(f32[160,128]{1,0:T(8,128)} %get-tuple-element.21), channel_id=1, source_target_pairs={{0,1},{1,2},{2,3},{3,0},{4,5},{5,6},{6,7},{7,4},{8,9},{9,10},{10,1... | collective-permute-start | bytes 245768 | tf_op jit(solution)/shard_map/ppermute | solution.py:490
  23.3 3.4 %collective-permute-start.1 = (f32[160,128]{1,0:T(8,128)}, f32[160,128]{1,0:T(8,128)S(1)}, u32[]{:S(2)}, u32[]{:S(2)}) collective-permute-start(f32[160,128]{1,0:T(8,128)} %get-tuple-element.21), channel_id=1, source_target_pairs={{0,3},{1,0},{2,1},{3,2},{4,7},{5,4},{6,5},{7,6},{8,11},{9,8},{10,9... | collective-permute-start | bytes 245768 | tf_op jit(solution)/shard_map/ppermute | solution.py:491
  26.7 0.1 collective-permute-done.from_below
  26.8 3.1 %collective-permute-done.1.from_above = f32[160,128]{1,0:T(8,128)S(1)} collective-permute-done((f32[160,128]{1,0:T(8,128)}, f32[160,128]{1,0:T(8,128)S(1)}, u32[]{:S(2)}, u32[]{:S(2)}) %collective-permute-start.1) | collective-permute-done | bytes 81952 | tf_op jit(solution)/shard_map/ppermute | solution.py:491
  30.0 4.9 %collective-permute-start.2 = (f32[96,128]{1,0:T(8,128)S(1)}, f32[96,128]{1,0:T(8,128)S(1)}, u32[]{:S(2)}, u32[]{:S(2)}) collective-permute-start(f32[96,128]{1,0:T(8,128)S(1)} %get-tuple-element.22), channel_id=1, source_target_pairs={{4,8},{12,16},{20,24},{28,32},{36,40},{44,48},{52,56},{8,4},{16,12... | collective-permute-start | bytes 147464 | tf_op jit(solution)/shard_map/ppermute | solution.py:494
  34.8 1.9 %collective-permute-start.3 = (f32[96,128]{1,0:T(8,128)S(1)}, f32[96,128]{1,0:T(8,128)S(1)}, u32[]{:S(2)}, u32[]{:S(2)}) collective-permute-start(f32[96,128]{1,0:T(8,128)S(1)} %get-tuple-element.23), channel_id=1, source_target_pairs={{0,4},{8,12},{16,20},{24,28},{32,36},{40,44},{48,52},{56,60},{4,0}... | collective-permute-start | bytes 147464 | tf_op jit(solution)/shard_map/ppermute | solution.py:495
  36.8 0.7 slice.3.warmth
  37.5 1.2 %copy-done = f32[16,8,16,128]{3,2,1,0:T(8,128)S(1)} copy-done((f32[16,8,16,128]{3,2,1,0:T(8,128)S(1)}, f32[16,8,16,128]{3,2,1,0:T(8,128)}, u32[]{:S(2)}) %copy-start) | copy-done | bytes 1048600
  38.7 0.1 shard_map.79
  38.8 7.4 %collective-permute-done.2.z_a = f32[96,128]{1,0:T(8,128)S(1)} collective-permute-done((f32[96,128]{1,0:T(8,128)S(1)}, f32[96,128]{1,0:T(8,128)S(1)}, u32[]{:S(2)}, u32[]{:S(2)}) %collective-permute-start.2) | collective-permute-done | bytes 49184 | tf_op jit(solution)/shard_map/ppermute | solution.py:494
  46.2 0.0 collective-permute-done.4.in_a
  46.2 0.0 collective-permute-done.5.in_b
  46.2 0.1 shard_map.80
  46.3 2.8 %collective-permute-start.6 = (f32[856,128]{1,0:T(8,128)S(1)}, f32[856,128]{1,0:T(8,128)S(1)}, u32[]{:S(2)}, u32[]{:S(2)}) collective-permute-start(f32[856,128]{1,0:T(8,128)S(1)} %get-tuple-element.30), channel_id=1, source_target_pairs={{0,64},{64,128},{128,192},{192,256},{256,320},{320,384},{384,448},... | collective-permute-start | bytes 1314824 | tf_op jit(solution)/shard_map/ppermute | solution.py:505
  49.2 0.0 copy-start.2
  49.2 1.3 %collective-permute-start.7 = (f32[808,128]{1,0:T(8,128)S(1)}, f32[808,128]{1,0:T(8,128)S(1)}, u32[]{:S(2)}, u32[]{:S(2)}) collective-permute-start(f32[808,128]{1,0:T(8,128)S(1)} %get-tuple-element.31), channel_id=1, source_target_pairs={{64,0},{128,64},{192,128},{256,192},{320,256},{384,320},{448,384},... | collective-permute-start | bytes 1241096 | tf_op jit(solution)/shard_map/ppermute | solution.py:506
  50.5 4.8 %shard_map.82 = (f32[8,16,256]{2,1,0:T(8,128)S(1)}, f32[4,4,16,384]{3,2,1,0:T(8,128)S(1)}) custom-call(f32[16,8,16,128]{3,2,1,0:T(8,128)S(1)} %copy-done.1, f32[8,16,128]{2,1,0:T(8,128)S(1)} %get-tuple-element.25.own_z, f32[58,16,128]{2,1,0:T(8,128)S(1)} %collective-permute-done.4.in_a, f32[58,16,128]{2,1,0:T(8,128)S(1)} %collective-permute-done.5.in_b, ...), custom_call_target="tpu_custom_call" | custom-call | tf_op jit(solution)/shard_map/pallas_call | solution.py:519
  55.3 2.6 %collective-permute-done.7.from_high = f32[808,128]{1,0:T(8,128)S(1)} collective-permute-done((f32[808,128]{1,0:T(8,128)S(1)}, f32[808,128]{1,0:T(8,128)S(1)}, u32[]{:S(2)}, u32[]{:S(2)}) %collective-permute-start.7) | collective-permute-done | bytes 413728 | tf_op jit(solution)/shard_map/ppermute | solution.py:506
  58.0 0.1 shard_map.81
  58.0 4.8 %shard_map.83 = f32[4,7,8,128]{3,2,1,0:T(8,128)S(1)} custom-call(f32[16,8,16,128]{3,2,1,0:T(8,128)S(1)} %copy-done.1, f32[8,16,128]{2,1,0:T(8,128)S(1)} %get-tuple-element.25.own_z, f32[58,16,128]{2,1,0:T(8,128)S(1)} %collective-permute-done.4.in_a, f32[58,16,128]{2,1,0:T(8,128)S(1)} %collective-permute-done.5.in_b, ...), custom_call_target="tpu_custom_call" | custom-call | tf_op jit(solution)/shard_map/pallas_call | solution.py:520
  62.9 6.7 %all_to_all.5.heat = f32[4,7,8,128]{3,2,1,0:T(8,128)S(1)} all-to-all(f32[4,7,8,128]{3,2,1,0:T(8,128)S(1)} %shard_map.83), channel_id=1, replica_groups=mesh['gx'=8,'gy'=16,'gz'=4] {'gz'}, dimensions={0} | all-to-all | bytes 229376 | tf_op jit(solution)/shard_map/all_to_all | solution.py:526
  69.6 15.9 %collective-permute-start.8 = (f32[8,512]{1,0:T(8,128)S(1)}, f32[8,512]{1,0:T(8,128)S(1)}, u32[]{:S(2)}, u32[]{:S(2)}) collective-permute-start(f32[8,512]{1,0:T(8,128)S(1)} %get-tuple-element.35.warmth), channel_id=1, source_target_pairs={{3,4},{7,8},{11,12},{15,16},{19,20},{23,24},{27,28},{31,32},{35,36... | collective-permute-start | bytes 49160 | tf_op jit(solution)/shard_map/ppermute | solution.py:529
  85.5 1.6 %collective-permute-start.9 = (f32[1,512]{1,0:T(1,128)S(1)}, f32[1,512]{1,0:T(1,128)S(1)}, u32[]{:S(2)}, u32[]{:S(2)}) collective-permute-start(f32[1,512]{1,0:T(1,128)S(1)} %get-tuple-element.38), channel_id=1, source_target_pairs={{0,64},{64,128},{128,192},{192,256},{256,320},{320,384},{384,448},... | collective-permute-start | bytes 6152 | tf_op jit(solution)/shard_map/ppermute | solution.py:530
  87.1 1.3 %collective-permute-start.10 = (f32[1,512]{1,0:T(1,128)S(1)}, f32[1,512]{1,0:T(1,128)S(1)}, u32[]{:S(2)}, u32[]{:S(2)}) collective-permute-start(f32[1,512]{1,0:T(1,128)S(1)} %get-tuple-element.39), channel_id=1, source_target_pairs={{64,0},{128,64},{192,128},{256,192},{320,256},{384,320},{448,384},... | collective-permute-start | bytes 6152 | tf_op jit(solution)/shard_map/ppermute | solution.py:531
  88.4 0.6 shard_map.86
  89.1 0.0 collective-permute-done.9.before
  89.1 2.4 %collective-permute-done.10.after = f32[1,512]{1,0:T(1,128)S(1)} collective-permute-done((f32[1,512]{1,0:T(1,128)S(1)}, f32[1,512]{1,0:T(1,128)S(1)}, u32[]{:S(2)}, u32[]{:S(2)}) %collective-permute-start.10) | collective-permute-done | bytes 2080 | tf_op jit(solution)/shard_map/ppermute | solution.py:531
  91.4 0.0 collective-permute-done.8.across
  91.4 0.7 shard_map.85
  (8 shorter events, 0.1 us)
Async XLA Ops:
  3.5 42.7 %collective-permute-start.4 = (f32[58,16,128]{2,1,0:T(8,128)}, f32[58,16,128]{2,1,0:T(8,128)S(1)}, u32[]{:S(2)}, u32[]{:S(2)}) collective-permute-start(f32[58,16,128]{2,1,0:T(8,128)} %get-tuple-element.28), channel_id=1, source_target_pairs={{4,8},{12,16},{20,24},{28,32},{36,40},{44,48},{52,56},{8,4},{16,12... | collective-permute-start | bytes 1425416 | tf_op jit(solution)/shard_map/ppermute | solution.py:488
  19.5 26.7 %collective-permute-start.5 = (f32[58,16,128]{2,1,0:T(8,128)}, f32[58,16,128]{2,1,0:T(8,128)S(1)}, u32[]{:S(2)}, u32[]{:S(2)}) collective-permute-start(f32[58,16,128]{2,1,0:T(8,128)} %get-tuple-element.29), channel_id=1, source_target_pairs={{0,4},{8,12},{16,20},{24,28},{32,36},{40,44},{48,52},{56,60},{4,0}... | collective-permute-start | bytes 1425416 | tf_op jit(solution)/shard_map/ppermute | solution.py:489
  21.4 5.4 %collective-permute-start = (f32[160,128]{1,0:T(8,128)}, f32[160,128]{1,0:T(8,128)S(1)}, u32[]{:S(2)}, u32[]{:S(2)}) collective-permute-start(f32[160,128]{1,0:T(8,128)} %get-tuple-element.21), channel_id=1, source_target_pairs={{0,1},{1,2},{2,3},{3,0},{4,5},{5,6},{6,7},{7,4},{8,9},{9,10},{10,1... | collective-permute-start | bytes 245768 | tf_op jit(solution)/shard_map/ppermute | solution.py:490
  23.3 6.6 %collective-permute-start.1 = (f32[160,128]{1,0:T(8,128)}, f32[160,128]{1,0:T(8,128)S(1)}, u32[]{:S(2)}, u32[]{:S(2)}) collective-permute-start(f32[160,128]{1,0:T(8,128)} %get-tuple-element.21), channel_id=1, source_target_pairs={{0,3},{1,0},{2,1},{3,2},{4,7},{5,4},{6,5},{7,6},{8,11},{9,8},{10,9... | collective-permute-start | bytes 245768 | tf_op jit(solution)/shard_map/ppermute | solution.py:491
  30.0 16.2 %collective-permute-start.2 = (f32[96,128]{1,0:T(8,128)S(1)}, f32[96,128]{1,0:T(8,128)S(1)}, u32[]{:S(2)}, u32[]{:S(2)}) collective-permute-start(f32[96,128]{1,0:T(8,128)S(1)} %get-tuple-element.22), channel_id=1, source_target_pairs={{4,8},{12,16},{20,24},{28,32},{36,40},{44,48},{52,56},{8,4},{16,12... | collective-permute-start | bytes 147464 | tf_op jit(solution)/shard_map/ppermute | solution.py:494
  34.8 11.4 %collective-permute-start.3 = (f32[96,128]{1,0:T(8,128)S(1)}, f32[96,128]{1,0:T(8,128)S(1)}, u32[]{:S(2)}, u32[]{:S(2)}) collective-permute-start(f32[96,128]{1,0:T(8,128)S(1)} %get-tuple-element.23), channel_id=1, source_target_pairs={{0,4},{8,12},{16,20},{24,28},{32,36},{40,44},{48,52},{56,60},{4,0}... | collective-permute-start | bytes 147464 | tf_op jit(solution)/shard_map/ppermute | solution.py:495
  37.5 1.2 %copy-start = (f32[16,8,16,128]{3,2,1,0:T(8,128)S(1)}, f32[16,8,16,128]{3,2,1,0:T(8,128)}, u32[]{:S(2)}) copy-start(f32[16,8,16,128]{3,2,1,0:T(8,128)} %get-tuple-element.24.own) | copy-start | bytes 3145732
  38.8 11.7 %copy-start.1 = (f32[16,8,16,128]{3,2,1,0:T(8,128)S(1)}, f32[16,8,16,128]{3,2,1,0:T(8,128)}, u32[]{:S(2)}) copy-start(f32[16,8,16,128]{3,2,1,0:T(8,128)} %get-tuple-element.24.own) | copy-start | bytes 3145732
  46.3 11.6 %collective-permute-start.6 = (f32[856,128]{1,0:T(8,128)S(1)}, f32[856,128]{1,0:T(8,128)S(1)}, u32[]{:S(2)}, u32[]{:S(2)}) collective-permute-start(f32[856,128]{1,0:T(8,128)S(1)} %get-tuple-element.30), channel_id=1, source_target_pairs={{0,64},{64,128},{128,192},{192,256},{256,320},{320,384},{384,448},... | collective-permute-start | bytes 1314824 | tf_op jit(solution)/shard_map/ppermute | solution.py:505
  49.2 8.8 %copy-start.2 = (f32[8,1,512]{2,1,0:T(1,128)S(1)}, f32[8,1,512]{2,1,0:T(1,128)}, u32[]{:S(2)}) copy-start(f32[8,1,512]{2,1,0:T(1,128)} %packing.1) | copy-start | bytes 49156
  49.2 8.7 %collective-permute-start.7 = (f32[808,128]{1,0:T(8,128)S(1)}, f32[808,128]{1,0:T(8,128)S(1)}, u32[]{:S(2)}, u32[]{:S(2)}) collective-permute-start(f32[808,128]{1,0:T(8,128)S(1)} %get-tuple-element.31), channel_id=1, source_target_pairs={{64,0},{128,64},{192,128},{256,192},{320,256},{384,320},{448,384},... | collective-permute-start | bytes 1241096 | tf_op jit(solution)/shard_map/ppermute | solution.py:506
  69.6 21.9 %collective-permute-start.8 = (f32[8,512]{1,0:T(8,128)S(1)}, f32[8,512]{1,0:T(8,128)S(1)}, u32[]{:S(2)}, u32[]{:S(2)}) collective-permute-start(f32[8,512]{1,0:T(8,128)S(1)} %get-tuple-element.35.warmth), channel_id=1, source_target_pairs={{3,4},{7,8},{11,12},{15,16},{19,20},{23,24},{27,28},{31,32},{35,36... | collective-permute-start | bytes 49160 | tf_op jit(solution)/shard_map/ppermute | solution.py:529
  85.5 3.6 %collective-permute-start.9 = (f32[1,512]{1,0:T(1,128)S(1)}, f32[1,512]{1,0:T(1,128)S(1)}, u32[]{:S(2)}, u32[]{:S(2)}) collective-permute-start(f32[1,512]{1,0:T(1,128)S(1)} %get-tuple-element.38), channel_id=1, source_target_pairs={{0,64},{64,128},{128,192},{192,256},{256,320},{320,384},{384,448},... | collective-permute-start | bytes 6152 | tf_op jit(solution)/shard_map/ppermute | solution.py:530
  87.1 4.3 %collective-permute-start.10 = (f32[1,512]{1,0:T(1,128)S(1)}, f32[1,512]{1,0:T(1,128)S(1)}, u32[]{:S(2)}, u32[]{:S(2)}) collective-permute-start(f32[1,512]{1,0:T(1,128)S(1)} %get-tuple-element.39), channel_id=1, source_target_pairs={{64,0},{128,64},{192,128},{256,192},{320,256},{384,320},{448,384},... | collective-permute-start | bytes 6152 | tf_op jit(solution)/shard_map/ppermute | solution.py:531

commit v6 on v5

--- a/solution.py
+++ b/solution.py
@@ -257,21 +257,16 @@
     reach[0] = inside
     reach[1] = inside * (lax.axis_index("gy") > 0).astype(F32)
 
-    def coefs(j, carry):
+    for j in range(NY):
         phase = s[6, j]
-
-        def chosen(table):
+        for i, table in enumerate((ca_table, cb_table, sig_table)):
+            if i == 2 and not W <= j < W + CY:
+                continue
             value = jnp.zeros_like(phase)
             for index in range(4):
-                value = jnp.where(phase == index + 1.0, table[index], value)
-            return value
-
-        coef[0, j] = chosen(ca_table)
-        coef[1, j] = chosen(cb_table)
-        coef[2, j] = chosen(sig_table)
-        return carry
-
-    lax.fori_loop(0, NY, coefs, 0)
+                if table[index]:
+                    value = jnp.where(phase == index + 1.0, table[index], value)
+            coef[i, j] = value
 
     for step in range(ITERS):
         wave = 60.0 * math.sin(0.6 * (step + 0.5) * courant_dt)
@@ -300,7 +295,7 @@
         def electric(j):
             hx, hy, hz = s[3, j], s[4, j], s[5, j]
             cells = slice(0, 2 * LANES if step == ITERS - 1 else span)
-            ca, cb, sig = coef[0, j, :, cells], coef[1, j, :, cells], coef[2, j, :, cells]
+            ca, cb = coef[0, j, :, cells], coef[1, j, :, cells]
             hy_z, hx_z = pltpu.roll(hy, 1, 1)[:, cells], pltpu.roll(hx, 1, 1)[:, cells]
             hx, hy, hz = hx[:, cells], hy[:, cells], hz[:, cells]
             hx_y, hz_y = s[3, j - 1, :, cells], s[5, j - 1, :, cells]
@@ -316,7 +311,7 @@
             if 0 <= p < CY:
                 own = slice(0, 2 * LANES)
                 ex, ey, ez = ex[:, own], ey[:, own], ez[:, own]
-                now = sig[:, own] * (ex * ex + ey * ey + ez * ez)
+                now = coef[2, j, :, own] * (ex * ex + ey * ey + ez * ez)
                 power[p] = now if step == 0 else power[p] + now
 
         magnetic(step)

time: 92.7 us -> 92.5 us (level)
  no operation moved by 1% of the time
where the time goes in v6:
time: 92.5 us; the launch traced here: 91.9 us
  starting transfers between devices  52.9 us (57%)
  waiting for transfers between devices  15.7 us (17%)
  Pallas kernels  13.9 us (15%)
  blocking collectives  6.7 us (7%)
  local copies, waits for them, and re-layouts  1.96 us (2%)
    ppermute x1, starting transfers between devices, local(): in_a = lax.ppermute(to_a, 'gy', across)  15.9 us
    ppermute x1, starting transfers between devices, local(): outer = lax.ppermute(t, ('gy', 'gz'), ends + [(j, i) for i, j in ends])  15.9 us
    ppermute x1, waiting for transfers between devices, local(): z_a = lax.ppermute(z_a, 'gy', across)  7.4 us
    all_to_all x1, blocking collectives, local(): heat = lax.all_to_all(heat, 'gz', split_axis=0, concat_axis=0, tiled=True)  6.7 us
    ppermute x1, starting transfers between devices, local(): z_a = lax.ppermute(z_a, 'gy', across)  4.86 us
    pallas_call x1, Pallas kernels, local(): call(middle_field_kernel, (f32(*power), f32(ITERS, 4, NY, 3 * LANES)), [V...  4.77 us
    pallas_call x1, Pallas kernels, local(): call(field_kernel, f32(TY, 3 + span // LANES, TX, LANES), [VMEM] * 11, sc...  4.6 us
    ppermute x1, starting transfers between devices, local(): lax.ppermute(shared, 'gz', [(i, (i - 1) % n_z) for i in range(n_z)])  3.36 us
  transfers between devices with their start and end apart: 11, of which 5 were waited for; matrix products, arithmetic and copies ran while one was open for 1% of the time, Pallas kernels for 6%

profile of v6, /device:TPU:31, one launch (start us, length us, event | category | flops | bytes accessed | tf_op | source)
XLA Modules:
  0.0 91.9 jit_solution(16392490251941201689)
XLA Ops:
  0.6 2.9 %shard_map.77 = (f32[16,8,16,128]{3,2,1,0:T(8,128)}, f32[58,16,128]{2,1,0:T(8,128)}, f32[58,16,128]{2,1,0:T(8,128)}, f32[160,128]{1,0:T(8,128)}) custom-call(s32[1,16]{1,0:T(1,128)} %spots_hbm.1, f32[3,256,128]{2,1,0:T(8,128)} %bitcast.15, f32[3,256,128]{2,1,0:T(8,128)} %bitcast.16, s32[256,128]{1,0:T(8,128)} %bitcast.17, f32[8,1,512]{2,1,0:T(1,128)} %t_hbm.1), custom_call_target="tpu_custom_call" | custom-call | tf_op jit(solution)/shard_map/pallas_call | solution.py:469
  3.5 15.9 %collective-permute-start.4 = (f32[58,16,128]{2,1,0:T(8,128)}, f32[58,16,128]{2,1,0:T(8,128)S(1)}, u32[]{:S(2)}, u32[]{:S(2)}) collective-permute-start(f32[58,16,128]{2,1,0:T(8,128)} %get-tuple-element.28), channel_id=1, source_target_pairs={{4,8},{12,16},{20,24},{28,32},{36,40},{44,48},{52,56},{8,4},{16,12... | collective-permute-start | bytes 1425416 | tf_op jit(solution)/shard_map/ppermute | solution.py:483
  19.5 1.9 %collective-permute-start.5 = (f32[58,16,128]{2,1,0:T(8,128)}, f32[58,16,128]{2,1,0:T(8,128)S(1)}, u32[]{:S(2)}, u32[]{:S(2)}) collective-permute-start(f32[58,16,128]{2,1,0:T(8,128)} %get-tuple-element.29), channel_id=1, source_target_pairs={{0,4},{8,12},{16,20},{24,28},{32,36},{40,44},{48,52},{56,60},{4,0}... | collective-permute-start | bytes 1425416 | tf_op jit(solution)/shard_map/ppermute | solution.py:484
  21.4 1.9 %collective-permute-start = (f32[160,128]{1,0:T(8,128)}, f32[160,128]{1,0:T(8,128)S(1)}, u32[]{:S(2)}, u32[]{:S(2)}) collective-permute-start(f32[160,128]{1,0:T(8,128)} %get-tuple-element.21), channel_id=1, source_target_pairs={{0,1},{1,2},{2,3},{3,0},{4,5},{5,6},{6,7},{7,4},{8,9},{9,10},{10,1... | collective-permute-start | bytes 245768 | tf_op jit(solution)/shard_map/ppermute | solution.py:485
  23.3 3.4 %collective-permute-start.1 = (f32[160,128]{1,0:T(8,128)}, f32[160,128]{1,0:T(8,128)S(1)}, u32[]{:S(2)}, u32[]{:S(2)}) collective-permute-start(f32[160,128]{1,0:T(8,128)} %get-tuple-element.21), channel_id=1, source_target_pairs={{0,3},{1,0},{2,1},{3,2},{4,7},{5,4},{6,5},{7,6},{8,11},{9,8},{10,9... | collective-permute-start | bytes 245768 | tf_op jit(solution)/shard_map/ppermute | solution.py:486
  26.7 0.1 collective-permute-done.from_below
  26.8 3.1 %collective-permute-done.1.from_above = f32[160,128]{1,0:T(8,128)S(1)} collective-permute-done((f32[160,128]{1,0:T(8,128)}, f32[160,128]{1,0:T(8,128)S(1)}, u32[]{:S(2)}, u32[]{:S(2)}) %collective-permute-start.1) | collective-permute-done | bytes 81952 | tf_op jit(solution)/shard_map/ppermute | solution.py:486
  30.0 4.9 %collective-permute-start.2 = (f32[96,128]{1,0:T(8,128)S(1)}, f32[96,128]{1,0:T(8,128)S(1)}, u32[]{:S(2)}, u32[]{:S(2)}) collective-permute-start(f32[96,128]{1,0:T(8,128)S(1)} %get-tuple-element.22), channel_id=1, source_target_pairs={{4,8},{12,16},{20,24},{28,32},{36,40},{44,48},{52,56},{8,4},{16,12... | collective-permute-start | bytes 147464 | tf_op jit(solution)/shard_map/ppermute | solution.py:489
  34.8 1.9 %collective-permute-start.3 = (f32[96,128]{1,0:T(8,128)S(1)}, f32[96,128]{1,0:T(8,128)S(1)}, u32[]{:S(2)}, u32[]{:S(2)}) collective-permute-start(f32[96,128]{1,0:T(8,128)S(1)} %get-tuple-element.23), channel_id=1, source_target_pairs={{0,4},{8,12},{16,20},{24,28},{32,36},{40,44},{48,52},{56,60},{4,0}... | collective-permute-start | bytes 147464 | tf_op jit(solution)/shard_map/ppermute | solution.py:490
  36.8 0.7 slice.3.warmth
  37.5 1.2 %copy-done = f32[16,8,16,128]{3,2,1,0:T(8,128)S(1)} copy-done((f32[16,8,16,128]{3,2,1,0:T(8,128)S(1)}, f32[16,8,16,128]{3,2,1,0:T(8,128)}, u32[]{:S(2)}) %copy-start) | copy-done | bytes 1048600
  38.7 0.1 shard_map.79
  38.8 7.4 %collective-permute-done.2.z_a = f32[96,128]{1,0:T(8,128)S(1)} collective-permute-done((f32[96,128]{1,0:T(8,128)S(1)}, f32[96,128]{1,0:T(8,128)S(1)}, u32[]{:S(2)}, u32[]{:S(2)}) %collective-permute-start.2) | collective-permute-done | bytes 49184 | tf_op jit(solution)/shard_map/ppermute | solution.py:489
  46.2 0.0 collective-permute-done.3.z_b
  46.2 0.0 collective-permute-done.4.in_a
  46.2 0.1 shard_map.80
  46.3 2.8 %collective-permute-start.6 = (f32[856,128]{1,0:T(8,128)S(1)}, f32[856,128]{1,0:T(8,128)S(1)}, u32[]{:S(2)}, u32[]{:S(2)}) collective-permute-start(f32[856,128]{1,0:T(8,128)S(1)} %get-tuple-element.30), channel_id=1, source_target_pairs={{0,64},{64,128},{128,192},{192,256},{256,320},{320,384},{384,448},... | collective-permute-start | bytes 1314824 | tf_op jit(solution)/shard_map/ppermute | solution.py:500
  49.2 0.0 copy-start.2
  49.2 1.3 %collective-permute-start.7 = (f32[808,128]{1,0:T(8,128)S(1)}, f32[808,128]{1,0:T(8,128)S(1)}, u32[]{:S(2)}, u32[]{:S(2)}) collective-permute-start(f32[808,128]{1,0:T(8,128)S(1)} %get-tuple-element.31), channel_id=1, source_target_pairs={{64,0},{128,64},{192,128},{256,192},{320,256},{384,320},{448,384},... | collective-permute-start | bytes 1241096 | tf_op jit(solution)/shard_map/ppermute | solution.py:501
  50.5 4.8 %shard_map.82 = (f32[8,16,256]{2,1,0:T(8,128)S(1)}, f32[4,4,16,384]{3,2,1,0:T(8,128)S(1)}) custom-call(f32[16,8,16,128]{3,2,1,0:T(8,128)S(1)} %copy-done.1, f32[8,16,128]{2,1,0:T(8,128)S(1)} %get-tuple-element.25.own_z, f32[58,16,128]{2,1,0:T(8,128)S(1)} %collective-permute-done.4.in_a, f32[58,16,128]{2,1,0:T(8,128)S(1)} %collective-permute-done.5.in_b, ...), custom_call_target="tpu_custom_call" | custom-call | tf_op jit(solution)/shard_map/pallas_call | solution.py:514
  55.3 2.7 %collective-permute-done.7.from_high = f32[808,128]{1,0:T(8,128)S(1)} collective-permute-done((f32[808,128]{1,0:T(8,128)S(1)}, f32[808,128]{1,0:T(8,128)S(1)}, u32[]{:S(2)}, u32[]{:S(2)}) %collective-permute-start.7) | collective-permute-done | bytes 413728 | tf_op jit(solution)/shard_map/ppermute | solution.py:501
  57.9 0.0 collective-permute-done.6.from_low
  58.0 0.1 shard_map.81
  58.0 4.6 %shard_map.83 = f32[4,7,8,128]{3,2,1,0:T(8,128)S(1)} custom-call(f32[16,8,16,128]{3,2,1,0:T(8,128)S(1)} %copy-done.1, f32[8,16,128]{2,1,0:T(8,128)S(1)} %get-tuple-element.25.own_z, f32[58,16,128]{2,1,0:T(8,128)S(1)} %collective-permute-done.4.in_a, f32[58,16,128]{2,1,0:T(8,128)S(1)} %collective-permute-done.5.in_b, ...), custom_call_target="tpu_custom_call" | custom-call | tf_op jit(solution)/shard_map/pallas_call | solution.py:515
  62.6 6.7 %all_to_all.5.heat = f32[4,7,8,128]{3,2,1,0:T(8,128)S(1)} all-to-all(f32[4,7,8,128]{3,2,1,0:T(8,128)S(1)} %shard_map.83), channel_id=1, replica_groups=mesh['gx'=8,'gy'=16,'gz'=4] {'gz'}, dimensions={0} | all-to-all | bytes 229376 | tf_op jit(solution)/shard_map/all_to_all | solution.py:521
  69.4 15.9 %collective-permute-start.8 = (f32[8,512]{1,0:T(8,128)S(1)}, f32[8,512]{1,0:T(8,128)S(1)}, u32[]{:S(2)}, u32[]{:S(2)}) collective-permute-start(f32[8,512]{1,0:T(8,128)S(1)} %get-tuple-element.35.warmth), channel_id=1, source_target_pairs={{3,4},{7,8},{11,12},{15,16},{19,20},{23,24},{27,28},{31,32},{35,36... | collective-permute-start | bytes 49160 | tf_op jit(solution)/shard_map/ppermute | solution.py:524
  85.3 1.6 %collective-permute-start.9 = (f32[1,512]{1,0:T(1,128)S(1)}, f32[1,512]{1,0:T(1,128)S(1)}, u32[]{:S(2)}, u32[]{:S(2)}) collective-permute-start(f32[1,512]{1,0:T(1,128)S(1)} %get-tuple-element.38), channel_id=1, source_target_pairs={{0,64},{64,128},{128,192},{192,256},{256,320},{320,384},{384,448},... | collective-permute-start | bytes 6152 | tf_op jit(solution)/shard_map/ppermute | solution.py:525
  86.9 1.3 %collective-permute-start.10 = (f32[1,512]{1,0:T(1,128)S(1)}, f32[1,512]{1,0:T(1,128)S(1)}, u32[]{:S(2)}, u32[]{:S(2)}) collective-permute-start(f32[1,512]{1,0:T(1,128)S(1)} %get-tuple-element.39), channel_id=1, source_target_pairs={{64,0},{128,64},{192,128},{256,192},{320,256},{384,320},{448,384},... | collective-permute-start | bytes 6152 | tf_op jit(solution)/shard_map/ppermute | solution.py:526
  88.2 0.6 shard_map.86
  88.8 0.0 collective-permute-done.9.before
  88.8 2.4 %collective-permute-done.10.after = f32[1,512]{1,0:T(1,128)S(1)} collective-permute-done((f32[1,512]{1,0:T(1,128)S(1)}, f32[1,512]{1,0:T(1,128)S(1)}, u32[]{:S(2)}, u32[]{:S(2)}) %collective-permute-start.10) | collective-permute-done | bytes 2080 | tf_op jit(solution)/shard_map/ppermute | solution.py:526
  91.2 0.7 shard_map.85
  (8 shorter events, 0.1 us)
Async XLA Ops:
  3.5 42.7 %collective-permute-start.4 = (f32[58,16,128]{2,1,0:T(8,128)}, f32[58,16,128]{2,1,0:T(8,128)S(1)}, u32[]{:S(2)}, u32[]{:S(2)}) collective-permute-start(f32[58,16,128]{2,1,0:T(8,128)} %get-tuple-element.28), channel_id=1, source_target_pairs={{4,8},{12,16},{20,24},{28,32},{36,40},{44,48},{52,56},{8,4},{16,12... | collective-permute-start | bytes 1425416 | tf_op jit(solution)/shard_map/ppermute | solution.py:483
  19.5 26.7 %collective-permute-start.5 = (f32[58,16,128]{2,1,0:T(8,128)}, f32[58,16,128]{2,1,0:T(8,128)S(1)}, u32[]{:S(2)}, u32[]{:S(2)}) collective-permute-start(f32[58,16,128]{2,1,0:T(8,128)} %get-tuple-element.29), channel_id=1, source_target_pairs={{0,4},{8,12},{16,20},{24,28},{32,36},{40,44},{48,52},{56,60},{4,0}... | collective-permute-start | bytes 1425416 | tf_op jit(solution)/shard_map/ppermute | solution.py:484
  21.4 5.4 %collective-permute-start = (f32[160,128]{1,0:T(8,128)}, f32[160,128]{1,0:T(8,128)S(1)}, u32[]{:S(2)}, u32[]{:S(2)}) collective-permute-start(f32[160,128]{1,0:T(8,128)} %get-tuple-element.21), channel_id=1, source_target_pairs={{0,1},{1,2},{2,3},{3,0},{4,5},{5,6},{6,7},{7,4},{8,9},{9,10},{10,1... | collective-permute-start | bytes 245768 | tf_op jit(solution)/shard_map/ppermute | solution.py:485
  23.3 6.6 %collective-permute-start.1 = (f32[160,128]{1,0:T(8,128)}, f32[160,128]{1,0:T(8,128)S(1)}, u32[]{:S(2)}, u32[]{:S(2)}) collective-permute-start(f32[160,128]{1,0:T(8,128)} %get-tuple-element.21), channel_id=1, source_target_pairs={{0,3},{1,0},{2,1},{3,2},{4,7},{5,4},{6,5},{7,6},{8,11},{9,8},{10,9... | collective-permute-start | bytes 245768 | tf_op jit(solution)/shard_map/ppermute | solution.py:486
  30.0 16.2 %collective-permute-start.2 = (f32[96,128]{1,0:T(8,128)S(1)}, f32[96,128]{1,0:T(8,128)S(1)}, u32[]{:S(2)}, u32[]{:S(2)}) collective-permute-start(f32[96,128]{1,0:T(8,128)S(1)} %get-tuple-element.22), channel_id=1, source_target_pairs={{4,8},{12,16},{20,24},{28,32},{36,40},{44,48},{52,56},{8,4},{16,12... | collective-permute-start | bytes 147464 | tf_op jit(solution)/shard_map/ppermute | solution.py:489
  34.8 11.4 %collective-permute-start.3 = (f32[96,128]{1,0:T(8,128)S(1)}, f32[96,128]{1,0:T(8,128)S(1)}, u32[]{:S(2)}, u32[]{:S(2)}) collective-permute-start(f32[96,128]{1,0:T(8,128)S(1)} %get-tuple-element.23), channel_id=1, source_target_pairs={{0,4},{8,12},{16,20},{24,28},{32,36},{40,44},{48,52},{56,60},{4,0}... | collective-permute-start | bytes 147464 | tf_op jit(solution)/shard_map/ppermute | solution.py:490
  37.5 1.2 %copy-start = (f32[16,8,16,128]{3,2,1,0:T(8,128)S(1)}, f32[16,8,16,128]{3,2,1,0:T(8,128)}, u32[]{:S(2)}) copy-start(f32[16,8,16,128]{3,2,1,0:T(8,128)} %get-tuple-element.24.own) | copy-start | bytes 3145732
  38.8 11.7 %copy-start.1 = (f32[16,8,16,128]{3,2,1,0:T(8,128)S(1)}, f32[16,8,16,128]{3,2,1,0:T(8,128)}, u32[]{:S(2)}) copy-start(f32[16,8,16,128]{3,2,1,0:T(8,128)} %get-tuple-element.24.own) | copy-start | bytes 3145732
  46.3 11.6 %collective-permute-start.6 = (f32[856,128]{1,0:T(8,128)S(1)}, f32[856,128]{1,0:T(8,128)S(1)}, u32[]{:S(2)}, u32[]{:S(2)}) collective-permute-start(f32[856,128]{1,0:T(8,128)S(1)} %get-tuple-element.30), channel_id=1, source_target_pairs={{0,64},{64,128},{128,192},{192,256},{256,320},{320,384},{384,448},... | collective-permute-start | bytes 1314824 | tf_op jit(solution)/shard_map/ppermute | solution.py:500
  49.2 8.8 %copy-start.2 = (f32[8,1,512]{2,1,0:T(1,128)S(1)}, f32[8,1,512]{2,1,0:T(1,128)}, u32[]{:S(2)}) copy-start(f32[8,1,512]{2,1,0:T(1,128)} %packing.1) | copy-start | bytes 49156
  49.2 8.7 %collective-permute-start.7 = (f32[808,128]{1,0:T(8,128)S(1)}, f32[808,128]{1,0:T(8,128)S(1)}, u32[]{:S(2)}, u32[]{:S(2)}) collective-permute-start(f32[808,128]{1,0:T(8,128)S(1)} %get-tuple-element.31), channel_id=1, source_target_pairs={{64,0},{128,64},{192,128},{256,192},{320,256},{384,320},{448,384},... | collective-permute-start | bytes 1241096 | tf_op jit(solution)/shard_map/ppermute | solution.py:501
  69.4 21.9 %collective-permute-start.8 = (f32[8,512]{1,0:T(8,128)S(1)}, f32[8,512]{1,0:T(8,128)S(1)}, u32[]{:S(2)}, u32[]{:S(2)}) collective-permute-start(f32[8,512]{1,0:T(8,128)S(1)} %get-tuple-element.35.warmth), channel_id=1, source_target_pairs={{3,4},{7,8},{11,12},{15,16},{19,20},{23,24},{27,28},{31,32},{35,36... | collective-permute-start | bytes 49160 | tf_op jit(solution)/shard_map/ppermute | solution.py:524
  85.3 3.6 %collective-permute-start.9 = (f32[1,512]{1,0:T(1,128)S(1)}, f32[1,512]{1,0:T(1,128)S(1)}, u32[]{:S(2)}, u32[]{:S(2)}) collective-permute-start(f32[1,512]{1,0:T(1,128)S(1)} %get-tuple-element.38), channel_id=1, source_target_pairs={{0,64},{64,128},{128,192},{192,256},{256,320},{320,384},{384,448},... | collective-permute-start | bytes 6152 | tf_op jit(solution)/shard_map/ppermute | solution.py:525
  86.9 4.3 %collective-permute-start.10 = (f32[1,512]{1,0:T(1,128)S(1)}, f32[1,512]{1,0:T(1,128)S(1)}, u32[]{:S(2)}, u32[]{:S(2)}) collective-permute-start(f32[1,512]{1,0:T(1,128)S(1)} %get-tuple-element.39), channel_id=1, source_target_pairs={{64,0},{128,64},{192,128},{256,192},{320,256},{384,320},{448,384},... | collective-permute-start | bytes 6152 | tf_op jit(solution)/shard_map/ppermute | solution.py:526
